TPU v7x, 256 devices: a whole 4x4x8 slice. The times are simulated.
256 devices in a mesh: kgrp: 8 (over x, y_hi), atom: 32 (over y_lo, z, core).
Axes of the slice: x: 4, y: 4 (y_hi: 2, y_lo: 2; y = y_hi * 2 + y_lo), z: 8, core: 2. Of those that a mesh axis runs over, the one named last changes fastest.
Arguments:
- atomic_descriptors: bfloat16 [65536, 128], P('atom'), may hold values from -6 to 6
- unit_cell_coordinates: float32 [3, 65536], P(None, 'atom'), may hold values from 0 to 1
- element_labels: int32 [65536], P('atom'), may hold values from 0 to 5
- lattice_momenta: int32 [3, 4096], P(None, 'kgrp'), may hold values from -8 to 8
- feature_to_latent_matrix: bfloat16 [2, 128, 128], replicated, may hold values from -0.5 to 0.5
- latent_to_feature_matrix: bfloat16 [2, 128, 128], replicated, may hold values from -0.5 to 0.5
- element_latent_multiplier: float32 [2, 6, 128], replicated, may hold values from 0.5 to 2
- upstream_gradient: bfloat16 [65536, 128], P('atom'), may hold values from -6 to 6
Outputs:
- grad_features: bfloat16 [65536, 128], P(('atom', 'kgrp'))
- grad_positions: float32 [3, 65536], P(None, ('atom', 'kgrp'))
All inputs are finite; a program needn't handle non-finite values.
Results may differ from a plain program's by a relative error of at most 0.014.
Values may be sent and summed in bfloat16 or wider, within the bound.
No kernel may reach another device: no remote copies, remote signals or barrier semaphores. Data moves between devices by JAX's collectives and lax.ppermute only.
A program may use at most 128 MiB of HBM per device.

v0:
```python
import math

import jax
import jax.numpy as jnp
from jax import lax
from jax.sharding import PartitionSpec as P

TWO_PI = 2.0 * math.pi
BOX_LENGTH = 100.0
GAUSSIAN_SIGMAS = (200.0, 100.0)


def trigonometric_lookup(unit_cell_coordinates, kblock):
    kfloat = kblock.astype(jnp.float32)
    theta = TWO_PI * (
        unit_cell_coordinates[0][:, None] * kfloat[0][None, :]
        + unit_cell_coordinates[1][:, None] * kfloat[1][None, :]
        + unit_cell_coordinates[2][:, None] * kfloat[2][None, :]
    )
    return (jnp.cos(theta), jnp.sin(theta))


def green_function_coefficients(kblock, spread, green_function_prefactor):
    kfloat = kblock.astype(jnp.float32)
    return green_function_prefactor * jnp.exp(-jnp.sum(kfloat * kfloat, axis=0) / spread)


def contract_rows(table, values):
    return lax.dot_general(
        table, values, (((0,), (0,)), ((), ())), preferred_element_type=jnp.float32
    )


def contract_cols(left, right):
    return lax.dot_general(
        left, right, (((1,), (1,)), ((), ())), preferred_element_type=jnp.float32
    )


def make_charges(feats, weight_in, gain_rows):
    return (jnp.dot(feats, weight_in, preferred_element_type=jnp.float32) * gain_rows).astype(
        jnp.bfloat16
    )


def theta_grad(
    structure_factor_real,
    structure_factor_imaginary,
    grad_pot,
    charges,
    field_re,
    field_im,
    grad_re,
    grad_im,
    kblock,
):
    along_re = contract_cols(grad_pot, field_re) + contract_cols(charges, grad_re)
    along_im = contract_cols(grad_pot, field_im) + contract_cols(charges, grad_im)
    gtheta = structure_factor_real * along_im - structure_factor_imaginary * along_re
    kfloat = kblock.astype(jnp.float32)
    summed = jnp.sum(kfloat[:, None, :] * gtheta[None, :, :], axis=2)
    return TWO_PI / BOX_LENGTH * summed


def rows_product(cosine_bf, sine_bf, part_re, part_im):

    def product_rows(start, count):
        result = jnp.dot(cosine_bf, part_re, preferred_element_type=jnp.float32)
        return result + jnp.dot(sine_bf, part_im, preferred_element_type=jnp.float32)

    return product_rows


def scaled_pair(weights, real_part, imag_part):
    return (
        (weights[:, None] * real_part).astype(jnp.bfloat16),
        (weights[:, None] * imag_part).astype(jnp.bfloat16),
    )


def per_device(
    atomic_descriptors,
    unit_cell_coordinates,
    element_labels,
    lattice_momenta,
    feature_to_latent_matrix,
    latent_to_feature_matrix,
    element_latent_multiplier,
    upstream_gradient,
):
    atoms_here = atomic_descriptors.shape[0]
    number_of_momenta = lattice_momenta.shape[1]
    groups = lax.axis_size("kgrp")
    share = atoms_here // groups
    green_function_prefactor = 1.0 / math.sqrt(
        atoms_here * lax.axis_size("atom") * number_of_momenta * groups
    )
    offset = lax.axis_index("kgrp") * share
    onehot = (
        element_labels[:, None]
        == jnp.arange(element_latent_multiplier.shape[1], dtype=jnp.int32)[None, :]
    ).astype(jnp.float32)
    gains_one = jnp.dot(onehot, element_latent_multiplier[0], precision=lax.Precision.HIGHEST)
    gains_two = jnp.dot(onehot, element_latent_multiplier[1], precision=lax.Precision.HIGHEST)
    structure_factor_real, structure_factor_imaginary = trigonometric_lookup(
        unit_cell_coordinates, lattice_momenta
    )
    cosine_bf = structure_factor_real.astype(jnp.bfloat16)
    sine_bf = structure_factor_imaginary.astype(jnp.bfloat16)
    leading_layer_mixing = green_function_coefficients(
        lattice_momenta, GAUSSIAN_SIGMAS[0], green_function_prefactor
    )
    trailing_layer_mixing = green_function_coefficients(
        lattice_momenta, GAUSSIAN_SIGMAS[1], green_function_prefactor
    )
    charges_one = make_charges(atomic_descriptors, feature_to_latent_matrix[0], gains_one)
    real_one, imag_one = lax.psum(
        (contract_rows(cosine_bf, charges_one), contract_rows(sine_bf, charges_one)), "atom"
    )
    field_one_re, field_one_im = scaled_pair(leading_layer_mixing, real_one, imag_one)
    potential_rows = rows_product(cosine_bf, sine_bf, field_one_re, field_one_im)
    potential_one = lax.psum(potential_rows(0, atoms_here), "kgrp").astype(jnp.bfloat16)
    hidden = (
        atomic_descriptors.astype(jnp.float32)
        + jnp.dot(potential_one, latent_to_feature_matrix[0], preferred_element_type=jnp.float32)
    ).astype(jnp.bfloat16)
    charges_two = make_charges(hidden, feature_to_latent_matrix[1], gains_two)
    grad_pot_two = jnp.dot(
        upstream_gradient, latent_to_feature_matrix[1].T, preferred_element_type=jnp.float32
    ).astype(jnp.bfloat16)
    summed_two = lax.psum(
        (
            contract_rows(cosine_bf, charges_two),
            contract_rows(sine_bf, charges_two),
            contract_rows(cosine_bf, grad_pot_two),
            contract_rows(sine_bf, grad_pot_two),
        ),
        "atom",
    )
    field_two_re, field_two_im = scaled_pair(trailing_layer_mixing, summed_two[0], summed_two[1])
    grad_two_re, grad_two_im = scaled_pair(trailing_layer_mixing, summed_two[2], summed_two[3])
    pos_two = theta_grad(
        structure_factor_real,
        structure_factor_imaginary,
        grad_pot_two,
        charges_two,
        field_two_re,
        field_two_im,
        grad_two_re,
        grad_two_im,
        lattice_momenta,
    )
    charge_grad_rows = rows_product(cosine_bf, sine_bf, grad_two_re, grad_two_im)
    grad_charge_two = lax.psum(charge_grad_rows(0, atoms_here), "kgrp")
    scaled_two = (grad_charge_two * gains_two).astype(jnp.bfloat16)
    grad_hidden = (
        upstream_gradient.astype(jnp.float32)
        + jnp.dot(scaled_two, feature_to_latent_matrix[1].T, preferred_element_type=jnp.float32)
    ).astype(jnp.bfloat16)
    grad_hidden_share = lax.dynamic_slice_in_dim(grad_hidden, offset, share, 0)
    grad_pot_one = jnp.dot(
        grad_hidden, latent_to_feature_matrix[0].T, preferred_element_type=jnp.float32
    ).astype(jnp.bfloat16)
    greal_one, gimag_one = lax.psum(
        (contract_rows(cosine_bf, grad_pot_one), contract_rows(sine_bf, grad_pot_one)), "atom"
    )
    grad_one_re, grad_one_im = scaled_pair(leading_layer_mixing, greal_one, gimag_one)
    grad_charge_part = rows_product(cosine_bf, sine_bf, grad_one_re, grad_one_im)(0, atoms_here)
    pos_one = theta_grad(
        structure_factor_real,
        structure_factor_imaginary,
        grad_pot_one,
        charges_one,
        field_one_re,
        field_one_im,
        grad_one_re,
        grad_one_im,
        lattice_momenta,
    )
    grad_charge_one, grad_positions = (
        lax.psum_scatter(grad_charge_part, "kgrp", scatter_dimension=0, tiled=True),
        lax.psum_scatter(pos_one + pos_two, "kgrp", scatter_dimension=1, tiled=True),
    )
    scaled_one = (grad_charge_one * lax.dynamic_slice_in_dim(gains_one, offset, share, 0)).astype(
        jnp.bfloat16
    )
    grad_features = (
        grad_hidden_share.astype(jnp.float32)
        + jnp.dot(scaled_one, feature_to_latent_matrix[0].T, preferred_element_type=jnp.float32)
    ).astype(jnp.bfloat16)
    return (grad_features, grad_positions)


def solution(mesh):
    in_specs = (
        P("atom", None),
        P(None, "atom"),
        P("atom"),
        P(None, "kgrp"),
        P(),
        P(),
        P(),
        P("atom", None),
    )
    out_specs = (P(("atom", "kgrp"), None), P(None, ("atom", "kgrp")))
    return jax.shard_map(
        per_device, mesh=mesh, in_specs=in_specs, out_specs=out_specs, check_vma=False
    )
```

profile of v0, /device:TPU:6, one launch (start us, length us, event | category | flops | bytes accessed | tf_op | source)
XLA Modules:
  0.0 979.3 jit_solution(6453147378366742730)
XLA Ops:
  10.2 16.0 %fusion.64 = f32[512,128]{1,0:T(8,128)} fusion(bf16[2048,128]{1,0:T(8,128)(2,1)S(1)} %convolution_convert_fusion.1, f32[512]{0:T(512)S(1)} %bitcast.119, f32[2048]{0:T(1024)S(1)} %bitcast.71, f32[512]{0:T(512)S(1)} %bitcast.135, f32[2048]{0:T(1024)S(1)} %bitcast.87, f32[512]{0:T(512)S(1)} %bitcast.103, f32[2048]{0:T(1024)S(1)} %bitcast.55), kind=kOutput, calls=%fused_computation.80 | convolution fusion | flops 275775488 | bytes 817152 | tf_op jit(solution)/shard_map/dot_general | solution.py:29
  26.2 16.3 %fusion.53 = f32[512,128]{1,0:T(8,128)} fusion(bf16[2048,128]{1,0:T(8,128)(2,1)S(1)} %convolution_convert_fusion.1, f32[512]{0:T(512)S(1)} %bitcast.120, f32[2048]{0:T(1024)S(1)} %bitcast.72, f32[512]{0:T(512)S(1)} %bitcast.136, f32[2048]{0:T(1024)S(1)} %bitcast.88, f32[512]{0:T(512)S(1)} %bitcast.104, f32[2048]{0:T(1024)S(1)} %bitcast.56), kind=kOutput, calls=%fused_computation.76 | convolution fusion | flops 275775488 | bytes 817152 | tf_op jit(solution)/shard_map/dot_general | solution.py:29
  44.0 16.0 %fusion.58 = f32[512,128]{1,0:T(8,128)} fusion(bf16[2048,128]{1,0:T(8,128)(2,1)S(1)} %fusion.5, f32[512]{0:T(512)S(1)} %bitcast.121, f32[2048]{0:T(1024)S(1)} %bitcast.73, f32[512]{0:T(512)S(1)} %bitcast.137, f32[2048]{0:T(1024)S(1)} %bitcast.89, f32[512]{0:T(512)S(1)} %bitcast.105, f32[2048]{0:T(1024)S(1)} %bitcast.57), kind=kOutput, calls=%fused_computation.78 | convolution fusion | flops 275775488 | bytes 817152 | tf_op jit(solution)/shard_map/dot_general | solution.py:29
  60.0 16.3 %fusion.47 = f32[512,128]{1,0:T(8,128)} fusion(bf16[2048,128]{1,0:T(8,128)(2,1)S(1)} %fusion.5, f32[512]{0:T(512)S(1)} %bitcast.122, f32[2048]{0:T(1024)S(1)} %bitcast.74, f32[512]{0:T(512)S(1)} %bitcast.138, f32[2048]{0:T(1024)S(1)} %bitcast.90, f32[512]{0:T(512)S(1)} %bitcast.106, f32[2048]{0:T(1024)S(1)} %bitcast.58), kind=kOutput, calls=%fused_computation.74 | convolution fusion | flops 275775488 | bytes 817152 | tf_op jit(solution)/shard_map/dot_general | solution.py:29
  77.5 226.6 %all-reduce.11.cloned.1.call-done = (f32[512,128]{1,0:T(8,128)}, f32[512,128]{1,0:T(8,128)}, f32[512,128]{1,0:T(8,128)}, f32[512,128]{1,0:T(8,128)}) async-done(((f32[512,128]{1,0:T(8,128)}, f32[512,128]{1,0:T(8,128)}, f32[512,128]{1,0:T(8,128)}, f32[512,128]{1,0:T(8,128)}), (f32[512,128]{1,0:T(8,128)}, f32[512,128]{1,0:T(8,128)}, f32[512,128]{1,0:T(8,128)}, ...) | async-done | bytes 1048592 | tf_op jit(solution)/shard_map/psum | solution.py:131
  304.1 16.2 %fusion.37 = f32[2048,128]{1,0:T(8,128)S(1)} fusion(f32[512,128]{1,0:T(8,128)} %get-tuple-element.8, f32[512]{0:T(512)S(1)} %get-tuple-element.21, f32[512]{0:T(512)S(1)} %bitcast.123, f32[2048]{0:T(1024)S(1)} %bitcast.75, f32[512]{0:T(512)S(1)} %bitcast.139, f32[2048]{0:T(1024)S(1)} %bitcast.91, f32[512]{0:T(512)S(1)} %bitcast.107, f32[2048]{0:T(1024)S(1)} %bitcast.59), kind=kOutput, calls=%fused_computation.66 | convolution fusion | flops 275906560 | bytes 1343488 | tf_op jit(solution)/shard_map/dot_general | solution.py:68
  320.3 16.6 %convolution_add_fusion.4 = f32[2048,128]{1,0:T(8,128)} fusion(f32[2048,128]{1,0:T(8,128)S(1)} %fusion.37, f32[512,128]{1,0:T(8,128)S(1)} %copy-done.12, f32[512]{0:T(512)S(1)} %get-tuple-element.21, f32[512]{0:T(512)S(1)} %bitcast.124, f32[2048]{0:T(1024)S(1)} %bitcast.76, f32[512]{0:T(512)S(1)} %bitcast.140, f32[2048]{0:T(1024)S(1)} %bitcast.92, ...), kind=kOutput, calls=%fused_computation.15 | convolution fusion | flops 276168704 | bytes 2392064 | tf_op jit(solution)/shard_map/dot_general | solution.py:69
  337.4 16.1 %fusion.42 = f32[2048,128]{1,0:T(8,128)S(1)} fusion(f32[512,128]{1,0:T(8,128)} %get-tuple-element.10, f32[512]{0:T(512)S(1)} %get-tuple-element.20, f32[512]{0:T(512)S(1)} %bitcast.125, f32[2048]{0:T(1024)S(1)} %bitcast.77, f32[512]{0:T(512)S(1)} %bitcast.141, f32[2048]{0:T(1024)S(1)} %bitcast.93, f32[512]{0:T(512)S(1)} %bitcast.109, f32[2048]{0:T(1024)S(1)} %bitcast.61), kind=kOutput, calls=%fused_computation.71 | convolution fusion | flops 275906560 | bytes 1343488 | tf_op jit(solution)/shard_map/dot_general | solution.py:68
  353.5 17.3 %convolution_add_fusion.1 = f32[2048,128]{1,0:T(8,128)} fusion(f32[2048,128]{1,0:T(8,128)S(1)} %fusion.42, f32[512,128]{1,0:T(8,128)S(1)} %copy-done.10, f32[512]{0:T(512)} %copy-done.23, f32[512]{0:T(512)} %bitcast.126, f32[2048]{0:T(1024)S(1)} %bitcast.78, f32[512]{0:T(512)} %bitcast.142, f32[2048]{0:T(1024)} %bitcast.94, f32[512]{0:T(512)} %bitcast.110, ...), kind=kOutput, calls=%fused_computation.11 | convolution fusion | flops 276168704 | bytes 2392064 | tf_op jit(solution)/shard_map/dot_general | solution.py:69
  370.8 91.6 %all-reduce.12 = bf16[2048,128]{1,0:T(8,128)(2,1)} all-reduce(f32[2048,128]{1,0:T(8,128)} %convolution_add_fusion.1), channel_id=1, replica_groups=mesh['kgrp'=8,'atom'=32] {'kgrp'}, use_global_device_ids=true, to_apply=%region_10.0 | all-reduce | flops 262144 | bytes 1572864 | tf_op jit(solution)/shard_map/psum | solution.py:122
  464.9 17.1 %fusion.55 = f32[512,128]{1,0:T(8,128)} fusion(bf16[2048,128]{1,0:T(8,128)(2,1)} %fusion.7, f32[512]{0:T(512)} %bitcast.127, f32[2048]{0:T(1024)S(1)} %bitcast.79, f32[512]{0:T(512)} %bitcast.143, f32[2048]{0:T(1024)} %bitcast.95, f32[512]{0:T(512)} %bitcast.111, f32[2048]{0:T(1024)S(1)} %bitcast.63), kind=kOutput, calls=%fused_computation.77 | convolution fusion | flops 275775488 | bytes 817152 | tf_op jit(solution)/shard_map/dot_general | solution.py:29
  482.1 16.3 %fusion.44 = f32[512,128]{1,0:T(8,128)} fusion(bf16[2048,128]{1,0:T(8,128)(2,1)S(1)} %copy-done.3, f32[512]{0:T(512)S(1)} %bitcast.128, f32[2048]{0:T(1024)S(1)} %bitcast.80, f32[512]{0:T(512)S(1)} %bitcast.144, f32[2048]{0:T(1024)S(1)} %bitcast.96, f32[512]{0:T(512)S(1)} %bitcast.112, f32[2048]{0:T(1024)S(1)} %bitcast.64), kind=kOutput, calls=%fused_computation.73 | convolution fusion | flops 275775488 | bytes 817152 | tf_op jit(solution)/shard_map/dot_general | solution.py:29
  500.4 16.4 %fusion.61 = f32[512,128]{1,0:T(8,128)} fusion(bf16[2048,128]{1,0:T(8,128)(2,1)S(1)} %convolution_convert_fusion, f32[512]{0:T(512)S(1)} %bitcast.129, f32[2048]{0:T(1024)S(1)} %bitcast.81, f32[512]{0:T(512)S(1)} %bitcast.145, f32[2048]{0:T(1024)S(1)} %bitcast.97, f32[512]{0:T(512)S(1)} %bitcast.113, f32[2048]{0:T(1024)S(1)} %bitcast.65), kind=kOutput, calls=%fused_computation.79 | convolution fusion | flops 275775488 | bytes 817152 | tf_op jit(solution)/shard_map/dot_general | solution.py:29
  516.8 16.1 %fusion.50 = f32[512,128]{1,0:T(8,128)} fusion(bf16[2048,128]{1,0:T(8,128)(2,1)S(1)} %convolution_convert_fusion, f32[512]{0:T(512)S(1)} %bitcast.130, f32[2048]{0:T(1024)S(1)} %bitcast.82, f32[512]{0:T(512)S(1)} %bitcast.146, f32[2048]{0:T(1024)S(1)} %bitcast.98, f32[512]{0:T(512)S(1)} %bitcast.114, f32[2048]{0:T(1024)S(1)} %bitcast.66), kind=kOutput, calls=%fused_computation.75 | convolution fusion | flops 275775488 | bytes 817152 | tf_op jit(solution)/shard_map/dot_general | solution.py:29
  533.0 3.8 fusion.38
  536.8 2.8 fusion.43
  539.6 2.8 fusion.41
  542.5 213.9 %all-reduce.9.cloned.1.call-done = (f32[512,128]{1,0:T(8,128)}, f32[512,128]{1,0:T(8,128)}, f32[512,128]{1,0:T(8,128)}, f32[512,128]{1,0:T(8,128)}) async-done(((f32[512,128]{1,0:T(8,128)}, f32[512,128]{1,0:T(8,128)}, f32[512,128]{1,0:T(8,128)}, f32[512,128]{1,0:T(8,128)}), (f32[512,128]{1,0:T(8,128)}, f32[512,128]{1,0:T(8,128)}, f32[512,128]{1,0:T(8,128)}, ...) | async-done | bytes 1048592 | tf_op jit(solution)/shard_map/psum | solution.py:164
  756.4 17.4 %fusion.39 = f32[2048,128]{1,0:T(8,128)} fusion(f32[512,128]{1,0:T(8,128)} %get-tuple-element.4, f32[512]{0:T(512)S(1)} %copy-done.24, f32[512]{0:T(512)S(1)} %bitcast.131, f32[2048]{0:T(1024)S(1)} %bitcast.83, f32[512]{0:T(512)S(1)} %bitcast.147, f32[2048]{0:T(1024)S(1)} %bitcast.99, f32[512]{0:T(512)S(1)} %bitcast.115, f32[2048]{0:T(1024)S(1)} %bitcast.67), kind=kOutput, calls=%fused_computation.68 | convolution fusion | flops 275906560 | bytes 1343488 | tf_op jit(solution)/shard_map/dot_general | solution.py:68
  777.0 17.2 %multiply_subtract_fusion = f32[2048,512]{1,0:T(8,128)S(1)} fusion(f32[2048,512]{1,0:T(8,128)S(1)} %fusion.17, f32[2048,512]{1,0:T(8,128)S(1)} %fusion.16, f32[2048,512]{1,0:T(8,128)S(1)} %copy-done.2, bf16[2048,128]{1,0:T(8,128)(2,1)S(1)} %copy-done.4, f32[512]{0:T(512)S(1)} %bitcast.132, f32[2048]{0:T(1024)S(1)} %bitcast.84, f32[512]{0:T(512)S(1)} %bitcast.148, ...), kind=kOutput, calls=%fused_computation.2 | convolution fusion | flops 280100864 | bytes 17596416 | tf_op jit(solution)/shard_map/dot_general | solution.py:35
  794.2 17.2 %multiply_subtract_fusion.1 = f32[2048,512]{1,0:T(8,128)S(1)} fusion(f32[2048,512]{1,0:T(8,128)S(1)} %copy-done, f32[2048,512]{1,0:T(8,128)S(1)} %copy-done.1, f32[2048,512]{1,0:T(8,128)S(1)} %fusion.40, bf16[2048,128]{1,0:T(8,128)(2,1)S(1)} %fusion.5, f32[512]{0:T(512)S(1)} %bitcast.133, f32[2048]{0:T(1024)S(1)} %bitcast.85, f32[512]{0:T(512)S(1)} %bitcast.149, ...), kind=kOutput, calls=%fused_computation.3 | convolution fusion | flops 280100864 | bytes 17596416 | tf_op jit(solution)/shard_map/dot_general | solution.py:35
  814.8 16.3 %convolution_add_fusion.2 = f32[2048,128]{1,0:T(8,128)} fusion(f32[2048,128]{1,0:T(8,128)S(1)} %copy-done.42, f32[512,128]{1,0:T(8,128)S(1)} %copy-done.13, f32[512]{0:T(512)S(1)} %copy-done.24, f32[512]{0:T(512)S(1)} %bitcast.134, f32[2048]{0:T(1024)S(1)} %bitcast.86, f32[512]{0:T(512)S(1)} %bitcast.150, f32[2048]{0:T(1024)S(1)} %bitcast.102, ...), kind=kOutput, calls=%fused_computation.13 | convolution fusion | flops 276168704 | bytes 2392064 | tf_op jit(solution)/shard_map/dot_general | solution.py:69
  831.2 59.1 %reduce-scatter.7.cloned.1.call-done = f32[256,3]{1,0:T(8,128)} async-done(((f32[2048,3]{1,0:T(8,128)}), f32[256,3]{1,0:T(8,128)}) %reduce-scatter.7.cloned.1.call-update) | async-done | bytes 3088
  891.9 78.9 %reduce-scatter.5.cloned.1.call-done = f32[256,128]{1,0:T(8,128)} async-done(((f32[2048,128]{1,0:T(8,128)}), f32[256,128]{1,0:T(8,128)}) %reduce-scatter.5.cloned.1.call-update) | async-done | bytes 131088 | tf_op jit(solution)/shard_map/reduce_scatter | solution.py:181
  (118 shorter events, 20.6 us)
Async XLA Ops:
  7.2 297.0 %all-reduce.11.cloned.1.call-start = ((), (), s32[]{:S(2)}) async-start(), calls=%async_computation.6 | async-start | bytes 2097152 | tf_op jit(solution)/shard_map/psum | solution.py:131
  7.9 18.3 %copy-start.21 = (f32[3,512]{1,0:T(4,128)}, f32[3,512]{1,0:T(4,128)S(1)}, u32[]{:S(2)}) copy-start(f32[3,512]{1,0:T(4,128)S(1)} %convert_element_type.78) | copy-start | bytes 18436
  7.9 329.4 %copy-start.29 = (f32[1,512]{1,0:T(1,128)}, f32[1,512]{1,0:T(1,128)S(1)}, u32[]{:S(2)}) copy-start(f32[1,512]{1,0:T(1,128)S(1)} %get-tuple-element.15) | copy-start | bytes 6148
  7.9 329.4 %copy-start.33 = (f32[1,512]{1,0:T(1,128)}, f32[1,512]{1,0:T(1,128)S(1)}, u32[]{:S(2)}) copy-start(f32[1,512]{1,0:T(1,128)S(1)} %get-tuple-element.16) | copy-start | bytes 6148
  7.9 329.4 %copy-start.37 = (f32[1,512]{1,0:T(1,128)}, f32[1,512]{1,0:T(1,128)S(1)}, u32[]{:S(2)}) copy-start(f32[1,512]{1,0:T(1,128)S(1)} %get-tuple-element.17) | copy-start | bytes 6148
  8.9 328.5 %copy-start.17 = (f32[1,2048]{1,0:T(1,128)}, f32[1,2048]{1,0:T(1,128)S(1)}, u32[]{:S(2)}) copy-start(f32[1,2048]{1,0:T(1,128)S(1)} %get-tuple-element.14) | copy-start | bytes 24580
  26.2 17.5 %copy-start.6 = (bf16[2048,128]{1,0:T(8,128)(2,1)S(1)}, bf16[2048,128]{1,0:T(8,128)(2,1)}, u32[]{:S(2)}) copy-start(bf16[2048,128]{1,0:T(8,128)(2,1)} %param.8) | copy-start | bytes 1572868
  26.2 17.5 %copy-start.9 = (bf16[2,128,128]{2,1,0:T(8,128)(2,1)S(1)}, bf16[2,128,128]{2,1,0:T(8,128)(2,1)}, u32[]{:S(2)}) copy-start(bf16[2,128,128]{2,1,0:T(8,128)(2,1)} %param.12) | copy-start | bytes 196612
  76.3 422.1 %all-reduce.7.cloned.1.call-start = ((), (), s32[]{:S(2)}) async-start(), calls=%async_computation.2 | async-start | bytes 2097152 | tf_op jit(solution)/shard_map/psum | solution.py:154
  76.4 243.9 %copy-start.25 = (f32[512]{0:T(512)}, f32[512]{0:T(512)S(1)}, u32[]{:S(2)}) copy-start(f32[512]{0:T(512)S(1)} %get-tuple-element.21) | copy-start | bytes 6148
  76.4 261.0 %copy-start.23 = (f32[512]{0:T(512)}, f32[512]{0:T(512)S(1)}, u32[]{:S(2)}) copy-start(f32[512]{0:T(512)S(1)} %get-tuple-element.20) | copy-start | bytes 6148
  336.9 419.5 %all-reduce.9.cloned.1.call-start = ((), (), s32[]{:S(2)}) async-start(), calls=%async_computation.5 | async-start | bytes 2097152 | tf_op jit(solution)/shard_map/psum | solution.py:164
  353.5 108.9 %copy-start.16 = (bf16[2,128,128]{2,1,0:T(8,128)(2,1)S(1)}, bf16[2,128,128]{2,1,0:T(8,128)(2,1)}, u32[]{:S(2)}) copy-start(bf16[2,128,128]{2,1,0:T(8,128)(2,1)} %param.13) | copy-start | bytes 196612
  532.9 357.4 %reduce-scatter.7.cloned.1.call-start = ((), (), s32[]{:S(2)}) async-start(), calls=%async_computation.4 | async-start | bytes 1179648
  536.8 219.6 %copy-start.20 = (f32[1,2048]{1,0:T(1,128)S(1)}, f32[1,2048]{1,0:T(1,128)}, u32[]{:S(2)}) copy-start(f32[1,2048]{1,0:T(1,128)} %copy-done.17) | copy-start | bytes 24580
  536.8 219.6 %copy-start.32 = (f32[1,512]{1,0:T(1,128)S(1)}, f32[1,512]{1,0:T(1,128)}, u32[]{:S(2)}) copy-start(f32[1,512]{1,0:T(1,128)} %copy-done.29) | copy-start | bytes 6148
  536.8 219.6 %copy-start.36 = (f32[1,512]{1,0:T(1,128)S(1)}, f32[1,512]{1,0:T(1,128)}, u32[]{:S(2)}) copy-start(f32[1,512]{1,0:T(1,128)} %copy-done.33) | copy-start | bytes 6148
  536.8 219.6 %copy-start.40 = (f32[1,512]{1,0:T(1,128)S(1)}, f32[1,512]{1,0:T(1,128)}, u32[]{:S(2)}) copy-start(f32[1,512]{1,0:T(1,128)} %copy-done.37) | copy-start | bytes 6148
  756.4 17.4 %copy-start.15 = (f32[512,128]{1,0:T(8,128)S(1)}, f32[512,128]{1,0:T(8,128)}, u32[]{:S(2)}) copy-start(f32[512,128]{1,0:T(8,128)} %get-tuple-element.6) | copy-start | bytes 786436
  777.0 17.2 %copy-start = (f32[2048,512]{1,0:T(8,128)S(1)}, f32[2048,512]{1,0:T(8,128)}, u32[]{:S(2)}) copy-start(f32[2048,512]{1,0:T(8,128)} %fusion.43) | copy-start | bytes 12582916
  777.0 17.2 %copy-start.1 = (f32[2048,512]{1,0:T(8,128)S(1)}, f32[2048,512]{1,0:T(8,128)}, u32[]{:S(2)}) copy-start(f32[2048,512]{1,0:T(8,128)} %fusion.41) | copy-start | bytes 12582916
  777.0 17.2 %copy-start.8 = (f32[512,128]{1,0:T(8,128)S(1)}, f32[512,128]{1,0:T(8,128)}, u32[]{:S(2)}) copy-start(f32[512,128]{1,0:T(8,128)} %get-tuple-element.4) | copy-start | bytes 786436
  794.2 17.2 %copy-start.22 = (f32[3,512]{1,0:T(4,128)S(1)}, f32[3,512]{1,0:T(4,128)}, u32[]{:S(2)}) copy-start(f32[3,512]{1,0:T(4,128)} %copy-done.21) | copy-start | bytes 18436
  814.6 156.2 %reduce-scatter.5.cloned.1.call-start = ((), (), s32[]{:S(2)}) async-start(), calls=%async_computation.3 | async-start | bytes 1179648 | tf_op jit(solution)/shard_map/reduce_scatter | solution.py:181
  (24 other events, 242.9 us)
Sparse Core Ops, SparseCore 0:
  76.4 227.6 all-reduce.10
  337.0 101.4 all-reduce.6
  533.0 223.3 all-reduce.8
  814.7 75.5 reduce-scatter.6
  894.6 76.1 reduce-scatter.4
where the time goes:
time: 989 us; the launch traced here: 979 us
  waiting for transfers between devices  579 us (59%)
  matrix products  287 us (29%)
  blocking collectives  91.6 us (9%)
  between operations  14.5 us (1%)
    psum x1, waiting for transfers between devices, per_device(): lax.psum((contract_rows(cosine_bf, charges_two), contract_rows(sine_bf, c...  227 us
    psum x1, waiting for transfers between devices, per_device(): lax.psum((contract_rows(cosine_bf, grad_pot_one), contract_rows(sine_bf,...  214 us
    dot_general x8, matrix products, contract_rows(): lax.dot_general(table, values, (((0,), (0,)), ((), ())), preferred_elemen...  130 us
    psum x1, blocking collectives, per_device(): lax.psum(potential_rows(0, atoms_here), 'kgrp').astype(jnp.bfloat16)  91.6 us
    reduce_scatter x1, waiting for transfers between devices, per_device(): lax.psum_scatter(grad_charge_part, 'kgrp', scatter_dimension=0, tiled=True)  78.9 us
    unnamed x6, waiting for transfers between devices  59.2 us
    dot_general x3, matrix products, product_rows(): jnp.dot(sine_bf, part_im, preferred_element_type=jnp.float32)  50.2 us
    dot_general x3, matrix products, product_rows(): result = jnp.dot(cosine_bf, part_re, preferred_element_type=jnp.float32)  49.6 us
  transfers between devices with their start and end apart: 5, of which 4 were waited for; matrix products, arithmetic and copies ran while one was open for 10% of the time, Pallas kernels for 0%

commit v1 on v0

v1 whole, which is shorter than its diff:
```python
import functools
import math

import jax
import jax.numpy as jnp
import numpy as np
from jax import lax
from jax.experimental import pallas as pl
from jax.experimental.pallas import tpu as pltpu
from jax.sharding import Mesh
from jax.sharding import PartitionSpec as P

BOX_LENGTH = 100.0
GAUSSIAN_SIGMAS = (200.0, 100.0)
REACH = 8
SPAN = 2 * REACH + 1
CLASSES = (SPAN**3 + 1) // 2
SLABS = 4
SLAB = 640
TABLE = 2 * SLAB
BLOCK = 256
CHANNELS = 128
ROWS = 40
PIECES = 32
VMEM_LIMIT = 48 * 1024 * 1024
BF16 = jnp.bfloat16
F32 = jnp.float32

COS_SERIES = (
    0.999999995487496,
    -19.739205575083908,
    64.93915835436466,
    -85.45075924609554,
    60.172044623035546,
    -25.982406908145567,
    6.5475440523380986,
)
SIN_SERIES = (
    6.283185281044049,
    -41.34169782356279,
    81.60504596930859,
    -76.70182055142223,
    42.01785583003898,
    -14.873772878742722,
    3.2058159421849517,
)


def class_vectors():
    label = np.arange(SLABS * SLAB)
    label = np.where(label < CLASSES, label, 0)
    first = (label + (SPAN * SPAN) // 2) // (SPAN * SPAN)
    rest = label - SPAN * SPAN * first + (SPAN * SPAN) // 2
    second = rest // SPAN - REACH
    third = rest % SPAN - REACH
    table = np.zeros((SLABS * SLAB, CHANNELS), np.float32)
    table[:, 0], table[:, 1], table[:, 2] = first, second, third
    return table


def matmul(left, right, left_dim, right_dim):
    return lax.dot_general(
        left, right, (((left_dim,), (right_dim,)), ((), ())), preferred_element_type=F32
    )


def flip(matrix):
    return jnp.transpose(matrix.astype(F32)).astype(BF16)


def gain_columns(multiplier, labels):
    result = jnp.zeros((multiplier.shape[0], labels.shape[1]), F32)
    for species in range(multiplier.shape[1]):
        result = jnp.where(labels == species, multiplier[:, species : species + 1], result)
    return result


def series(coefficients, square):
    result = coefficients[-1] * square + coefficients[-2]
    for coefficient in coefficients[-3::-1]:
        result = result * square + coefficient
    return result


def write_pieces(place, total_ref, keep_ref, send_ref):
    core = place[2]
    for target, half in ((keep_ref, core), (send_ref, 1 - core)):
        for index in range(PIECES):
            row, side = index // 2, index % 2
            start = pl.multiple_of(half * SLAB + row * ROWS, 8)
            target[index] = total_ref[
                pl.ds(start, ROWS), side * CHANNELS : (side + 1) * CHANNELS
            ].astype(BF16)


def read_pieces(place, mine_ref, other_ref, total_ref):
    core = place[2]
    for source, half in ((mine_ref, core), (other_ref, 1 - core)):
        for index in range(PIECES):
            row, side = index // 2, index % 2
            start = pl.multiple_of(half * SLAB + row * ROWS, 8)
            total_ref[pl.ds(start, ROWS), side * CHANNELS : (side + 1) * CHANNELS] = source[
                index
            ].astype(F32)


def tables_kernel(
    place,
    vectors_ref,
    coordinates_ref,
    labels_ref,
    features_ref,
    upstream_ref,
    inward_ref,
    outward_ref,
    multiplier_ref,
    table_ref,
    values_ref,
    keep_ref,
    send_ref,
    total_ref,
):
    step = pl.program_id(0)
    along = [coordinates_ref[axis : axis + 1, :] for axis in range(3)]
    chunk = 64
    for start in range(0, SLAB, chunk):
        rows = pl.ds(start, chunk)
        turns = vectors_ref[rows, 0:1] * along[0]
        turns += vectors_ref[rows, 1:2] * along[1]
        turns += vectors_ref[rows, 2:3] * along[2]
        turns -= jnp.floor(turns + 0.5)
        square = turns * turns
        table_ref[0, rows, :] = series(COS_SERIES, square).astype(BF16)
        table_ref[0, pl.ds(SLAB + start, chunk), :] = (
            turns * series(SIN_SERIES, square)
        ).astype(BF16)
    gains = gain_columns(multiplier_ref[0], labels_ref[...])
    charges = matmul(flip(inward_ref[0]), features_ref[...], 1, 1) * gains
    grad_pot = matmul(outward_ref[1], upstream_ref[...], 1, 1)
    values = jnp.concatenate([charges, grad_pot], axis=0).astype(BF16)
    values_ref[0] = values
    part = matmul(table_ref[0], values, 1, 1)

    @pl.when(step == 0)
    def _():
        total_ref[...] = part

    @pl.when(step != 0)
    def _():
        total_ref[...] += part

    @pl.when(step == pl.num_programs(0) - 1)
    def _():
        write_pieces(place, total_ref, keep_ref, send_ref)


def weights_kernel(prefactor, place, vectors_ref, classes_ref, weights_ref):
    chunk = 128
    for start in range(0, SLAB, chunk):
        rows = pl.ds(start, chunk)
        own = lax.broadcasted_iota(jnp.int32, (chunk, CHANNELS), 0) + (place[0] * SLAB + start)
        count = jnp.zeros((chunk, CHANNELS), F32)
        for group in range(classes_ref.shape[0]):
            for offset in range(0, classes_ref.shape[1], CHANNELS):
                classes = classes_ref[group : group + 1, offset : offset + CHANNELS]
                count += jnp.where(classes == own, 1.0, 0.0)
        count = jnp.sum(count, axis=1, keepdims=True)
        vectors = vectors_ref[rows, :]
        norm = jnp.sum(vectors * vectors, axis=1, keepdims=True)
        for block, spread in enumerate(GAUSSIAN_SIGMAS):
            weight = count * (prefactor * jnp.exp(norm * (-1.0 / spread)))
            weights_ref[block, rows, :] = jnp.broadcast_to(weight, (chunk, CHANNELS))


def potential_kernel(
    place, weights_ref, mine_ref, other_ref, table_ref, fields_ref, p0, p1, p2, p3, total_ref, flipped_ref
):
    step = pl.program_id(0)

    @pl.when(step == 0)
    def _():
        read_pieces(place, mine_ref, other_ref, total_ref)
        for half in range(2):
            rows = pl.ds(half * SLAB, SLAB)
            for side in range(2):
                columns = pl.ds(side * CHANNELS, CHANNELS)
                total_ref[rows, columns] = total_ref[rows, columns] * weights_ref[side]
        fields_ref[...] = total_ref[...].astype(BF16)
        flipped_ref[...] = jnp.transpose(total_ref[...]).astype(BF16)

    product = matmul(flipped_ref[...], table_ref[0], 1, 0).astype(BF16)
    for index, target in enumerate((p0, p1, p2, p3)):

        @pl.when(step == index)
        def _():
            target[...] = product


def middle_kernel(
    place,
    q0,
    q1,
    q2,
    q3,
    labels_ref,
    features_ref,
    upstream_ref,
    inward_ref,
    outward_ref,
    multiplier_ref,
    values_ref,
    hidden_grad_ref,
):
    total = (q0[...].astype(F32) + q1[...].astype(F32)) + (q2[...].astype(F32) + q3[...].astype(F32))
    potential = total[:CHANNELS].astype(BF16)
    grad_charge = total[CHANNELS:]
    gains = gain_columns(multiplier_ref[1], labels_ref[...])
    hidden = (
        features_ref[...].astype(F32)
        + matmul(jnp.transpose(potential.astype(F32)).astype(BF16), outward_ref[0], 1, 0)
    ).astype(BF16)
    inward_flipped = flip(inward_ref[1])
    charges = matmul(inward_flipped, hidden, 1, 1) * gains
    scaled = jnp.transpose(grad_charge * gains).astype(BF16)
    hidden_grad = (
        upstream_ref[...].astype(F32) + matmul(scaled, inward_flipped, 1, 0)
    ).astype(BF16)
    hidden_grad_ref[...] = hidden_grad
    grad_pot = matmul(outward_ref[0], hidden_grad, 1, 1)
    values_ref[...] = jnp.concatenate([charges, grad_pot], axis=0).astype(BF16)


def second_kernel(place, table_ref, v0, v1, v2, v3, keep_ref, send_ref, total_ref):
    step = pl.program_id(0)
    for index, source in enumerate((v0, v1, v2, v3)):

        @pl.when(step == index)
        def _():
            part = matmul(table_ref[0], source[...], 1, 1)
            if index == 0:
                total_ref[...] = part
            else:
                total_ref[...] += part

    @pl.when(step == pl.num_programs(0) - 1)
    def _():
        write_pieces(place, total_ref, keep_ref, send_ref)


def gradient_kernel(
    place,
    weights_ref,
    mine_ref,
    other_ref,
    fields_ref,
    vectors_ref,
    table_ref,
    first_ref,
    v0,
    v1,
    v2,
    v3,
    o0,
    o1,
    o2,
    o3,
    total_ref,
    pairs_ref,
    flipped_ref,
    directions_ref,
    theta_ref,
    second_ref,
):
    step = pl.program_id(0)

    @pl.when(step == 0)
    def _():
        read_pieces(place, mine_ref, other_ref, total_ref)
        for half in range(2):
            rows = pl.ds(half * SLAB, SLAB)
            for side in range(2):
                columns = pl.ds(side * CHANNELS, CHANNELS)
                total_ref[rows, columns] = total_ref[rows, columns] * weights_ref[1 - side]
        field_two = total_ref[:, :CHANNELS].astype(BF16)
        grad_one = total_ref[:, CHANNELS:]
        pairs_ref[:, 0:CHANNELS] = grad_one.astype(BF16)
        pairs_ref[:, CHANNELS : 2 * CHANNELS] = field_two
        pairs_ref[:, 2 * CHANNELS : 3 * CHANNELS] = fields_ref[:, CHANNELS:]
        pairs_ref[:, 3 * CHANNELS :] = fields_ref[:, :CHANNELS]
        flipped_ref[...] = jnp.transpose(grad_one).astype(BF16)
        directions_ref[...] = jnp.transpose(vectors_ref[...])[:16].astype(BF16)

    for index, source in enumerate((v0, v1, v2, v3)):

        @pl.when(step == index)
        def _():
            second_ref[...] = source[...]

    values = jnp.concatenate([first_ref[0], second_ref[...]], axis=0)
    chunk = 128
    for start in range(0, SLAB, chunk):
        real = pl.ds(start, chunk)
        imag = pl.ds(SLAB + start, chunk)
        along_real = matmul(pairs_ref[real, :], values, 1, 0)
        along_imag = matmul(pairs_ref[imag, :], values, 1, 0)
        theta_ref[real, :] = (
            table_ref[0, real, :].astype(F32) * along_imag
            - table_ref[0, imag, :].astype(F32) * along_real
        ).astype(BF16)
    charge = matmul(flipped_ref[...], table_ref[0], 1, 0)
    position = matmul(directions_ref[...], theta_ref[...], 1, 0)
    result = jnp.concatenate([charge, position * (2.0 * math.pi / BOX_LENGTH)], axis=0).astype(BF16)
    for index, target in enumerate((o0, o1, o2, o3)):

        @pl.when(step == index)
        def _():
            target[...] = result


def final_kernel(
    place, q0, q1, q2, q3, labels_ref, hidden_grad_ref, inward_ref, multiplier_ref, features_ref, positions_ref
):
    total = (q0[...].astype(F32) + q1[...].astype(F32)) + (q2[...].astype(F32) + q3[...].astype(F32))
    gains = gain_columns(multiplier_ref[0], labels_ref[...])
    scaled = jnp.transpose(total[:CHANNELS] * gains).astype(BF16)
    features_ref[...] = (
        hidden_grad_ref[...].astype(F32) + matmul(scaled, flip(inward_ref[0]), 1, 0)
    ).astype(BF16)
    positions_ref[...] = total[CHANNELS : CHANNELS + 3]


def shape_of(shape, dtype):
    return jax.ShapeDtypeStruct(shape, dtype)


def whole(shape):
    return pl.BlockSpec(shape, lambda step, place: (0,) * len(shape))


def call(kernel, steps, in_specs, outs, out_specs, scratch, operands):
    return pl.pallas_call(
        kernel,
        grid_spec=pltpu.PrefetchScalarGridSpec(
            num_scalar_prefetch=1,
            grid=(steps,),
            in_specs=in_specs,
            out_specs=out_specs,
            scratch_shapes=scratch,
        ),
        out_shape=outs,
        compiler_params=pltpu.CompilerParams(
            dimension_semantics=("arbitrary",), vmem_limit_bytes=VMEM_LIMIT
        ),
    )(*operands)


ATOM_REST = ("yh", "yl", "z")


def shifted(value, shift):
    return lax.ppermute(value, "x", [(i, (i + shift) % SLABS) for i in range(SLABS)])


def swapped(value):
    return lax.ppermute(value, "core", [(0, 1), (1, 0)])


def sum_fields(keep, send):
    part = (keep.astype(F32) + swapped(send).astype(F32)).astype(BF16)
    parts = lax.all_to_all(part, ATOM_REST, 0, 0, tiled=True)
    total = jnp.sum(parts.astype(F32), axis=0).astype(BF16)
    spread = jnp.broadcast_to(total[None], (PIECES,) + total.shape)
    mine = lax.all_to_all(spread, ATOM_REST, 0, 0, tiled=True)
    return mine, swapped(mine)


def per_device(
    atomic_descriptors,
    unit_cell_coordinates,
    element_labels,
    lattice_momenta,
    feature_to_latent_matrix,
    latent_to_feature_matrix,
    element_latent_multiplier,
    upstream_gradient,
):
    place = jnp.stack(
        [lax.axis_index("x"), lax.axis_index("yh"), lax.axis_index("core")]
    ).astype(jnp.int32)
    prefactor = 1.0 / math.sqrt(
        atomic_descriptors.shape[0]
        * lattice_momenta.shape[1]
        * lax.axis_size(("x", "yh", "yl", "z", "core"))
    )
    labels = element_labels[None, :]
    multiplier = jnp.swapaxes(element_latent_multiplier, 1, 2)
    species = multiplier.shape[2]
    vectors = jnp.asarray(class_vectors())
    signed = (
        lattice_momenta[0] * (SPAN * SPAN) + lattice_momenta[1] * SPAN + lattice_momenta[2]
    )
    classes = lax.all_gather(jnp.abs(signed)[None], ("x", "yh"), axis=0, tiled=True)

    slab = pl.BlockSpec((SLAB, CHANNELS), lambda step, place: (place[0], 0))
    own_slab = slab
    matrices = whole((2, CHANNELS, CHANNELS))
    gains_spec = whole((2, CHANNELS, species))
    pieces_spec = whole((PIECES, ROWS, CHANNELS))
    pieces_shape = shape_of((PIECES, ROWS, CHANNELS), BF16)
    values_block = whole((BLOCK, BLOCK))
    values_shape = shape_of((BLOCK, BLOCK), BF16)
    table_shape = shape_of((SLABS, TABLE, BLOCK), BF16)

    def rotated(shape, sign):
        return pl.BlockSpec(
            (1,) + shape, lambda step, place: ((place[0] + sign * step + SLABS) % SLABS, 0, 0)
        )

    table, values_one, keep, send = call(
        tables_kernel,
        SLABS,
        [
            slab,
            pl.BlockSpec((3, BLOCK), lambda step, place: (0, 2 * step + place[1])),
            pl.BlockSpec((1, BLOCK), lambda step, place: (0, 2 * step + place[1])),
            pl.BlockSpec((BLOCK, CHANNELS), lambda step, place: (2 * step + place[1], 0)),
            pl.BlockSpec((BLOCK, CHANNELS), lambda step, place: (2 * step + place[1], 0)),
            matrices,
            matrices,
            gains_spec,
        ],
        (table_shape, shape_of((SLABS, BLOCK, BLOCK), BF16), pieces_shape, pieces_shape),
        (
            pl.BlockSpec((1, TABLE, BLOCK), lambda step, place: (step, 0, 0)),
            pl.BlockSpec((1, BLOCK, BLOCK), lambda step, place: (step, 0, 0)),
            pieces_spec,
            pieces_spec,
        ),
        [pltpu.VMEM((TABLE, BLOCK), F32)],
        (
            place,
            vectors,
            unit_cell_coordinates,
            labels,
            atomic_descriptors,
            upstream_gradient,
            feature_to_latent_matrix,
            latent_to_feature_matrix,
            multiplier,
        ),
    )
    weights = call(
        functools.partial(weights_kernel, prefactor),
        1,
        [own_slab, whole(classes.shape)],
        shape_of((2, SLAB, CHANNELS), F32),
        whole((2, SLAB, CHANNELS)),
        [],
        (place, vectors, classes),
    )
    mine, other = sum_fields(keep, send)
    fields, *products = call(
        potential_kernel,
        SLABS,
        [whole((2, SLAB, CHANNELS)), pieces_spec, pieces_spec, rotated((TABLE, BLOCK), 1)],
        (shape_of((TABLE, BLOCK), BF16),) + (values_shape,) * SLABS,
        (whole((TABLE, BLOCK)),) + (values_block,) * SLABS,
        [pltpu.VMEM((TABLE, BLOCK), F32), pltpu.VMEM((BLOCK, TABLE), BF16)],
        (place, weights, mine, other, table),
    )
    arrived = [products[0]] + [shifted(products[shift], shift) for shift in range(1, SLABS)]
    own_atoms = pl.BlockSpec((BLOCK, CHANNELS), lambda step, place: (2 * place[0] + place[1], 0))
    own_labels = pl.BlockSpec((1, BLOCK), lambda step, place: (0, 2 * place[0] + place[1]))
    values_two, hidden_grad = call(
        middle_kernel,
        1,
        [values_block] * SLABS
        + [own_labels, own_atoms, own_atoms, matrices, matrices, gains_spec],
        (values_shape, shape_of((BLOCK, CHANNELS), BF16)),
        (values_block, whole((BLOCK, CHANNELS))),
        [],
        (
            place,
            *arrived,
            labels,
            atomic_descriptors,
            upstream_gradient,
            feature_to_latent_matrix,
            latent_to_feature_matrix,
            multiplier,
        ),
    )
    seconds = [values_two] + [shifted(values_two, SLABS - slot) for slot in range(1, SLABS)]
    keep, send = call(
        second_kernel,
        SLABS,
        [rotated((TABLE, BLOCK), 1)] + [values_block] * SLABS,
        (pieces_shape, pieces_shape),
        (pieces_spec, pieces_spec),
        [pltpu.VMEM((TABLE, BLOCK), F32)],
        (place, table, *seconds),
    )
    mine, other = sum_fields(keep, send)
    result_shape = shape_of((CHANNELS + 16, BLOCK), BF16)
    result_spec = whole((CHANNELS + 16, BLOCK))
    results = call(
        gradient_kernel,
        SLABS,
        [
            whole((2, SLAB, CHANNELS)),
            pieces_spec,
            pieces_spec,
            whole((TABLE, BLOCK)),
            own_slab,
            rotated((TABLE, BLOCK), 1),
            rotated((BLOCK, BLOCK), 1),
        ]
        + [values_block] * SLABS,
        (result_shape,) * SLABS,
        (result_spec,) * SLABS,
        [
            pltpu.VMEM((TABLE, BLOCK), F32),
            pltpu.VMEM((TABLE, 2 * BLOCK), BF16),
            pltpu.VMEM((CHANNELS, TABLE), BF16),
            pltpu.VMEM((16, SLAB), BF16),
            pltpu.VMEM((SLAB, BLOCK), BF16),
            pltpu.VMEM((BLOCK, BLOCK), BF16),
        ],
        (place, weights, mine, other, fields, vectors, table, values_one, *seconds),
    )
    arrived = [results[0]] + [shifted(results[shift], shift) for shift in range(1, SLABS)]
    return call(
        final_kernel,
        1,
        [result_spec] * SLABS
        + [own_labels, whole((BLOCK, CHANNELS)), matrices, gains_spec],
        (shape_of((BLOCK, CHANNELS), BF16), shape_of((3, BLOCK), F32)),
        (whole((BLOCK, CHANNELS)), whole((3, BLOCK))),
        [],
        (place, *arrived, labels, hidden_grad, feature_to_latent_matrix, multiplier),
    )


def solution(mesh):
    fine = Mesh(mesh.devices.reshape(SLABS, 2, 2, -1, 2), ("x", "yh", "yl", "z", "core"))
    atom, group = ("yl", "z", "core"), ("x", "yh")
    in_specs = (
        P(atom, None),
        P(None, atom),
        P(atom),
        P(None, group),
        P(),
        P(),
        P(),
        P(atom, None),
    )
    out_specs = (P(atom + group, None), P(None, atom + group))
    return jax.shard_map(
        per_device, mesh=fine, in_specs=in_specs, out_specs=out_specs, check_vma=False
    )
```

time: 989 us -> 176 us (0.18)
  waiting for transfers between devices: 579 us -> 21.8 us
  matrix products: 287 us -> 0 us
  Pallas kernels: 0 us -> 21 us
  blocking collectives: 91.6 us -> 107 us
  between operations: 14.5 us -> 0.86 us
  starting transfers between devices: 0.72 us -> 10.8 us
    psum x3 -> x0, waiting for transfers between devices: 441 us -> none  [the longest x1 227 us: per_device(): lax.psum((contract_rows(cosine_bf, charges_two), contract_rows(sine_bf, c...]
    dot_general x30 -> x0, matrix products: 287 us -> none  [the longest x8 130 us: contract_rows(): lax.dot_general(table, values, (((0,), (0,)), ((), ())), preferred_elemen...]
    psum x1 -> x0, blocking collectives: 91.6 us -> none  [per_device(): lax.psum(potential_rows(0, atoms_here), 'kgrp').astype(jnp.bfloat16)]
    reduce_scatter x1 -> x0, waiting for transfers between devices: 78.9 us -> none  [per_device(): lax.psum_scatter(grad_charge_part, 'kgrp', scatter_dimension=0, tiled=True)]
    all_to_all x0 -> x4, blocking collectives: none -> 78.5 us  [the longest x2 42.7 us: sum_fields(): parts = lax.all_to_all(part, ATOM_REST, 0, 0, tiled=True)]
    unnamed x6 -> x0, waiting for transfers between devices: 59.2 us -> none
    all_gather x0 -> x1, blocking collectives: none -> 28 us  [per_device(): lax.all_gather(jnp.abs(signed)[None], ('x', 'yh'), axis=0, tiled=True)]
    ppermute x0 -> x13, waiting for transfers between devices: none -> 21.8 us  [the longest x9 17 us: shifted(): lax.ppermute(value, 'x', [(i, (i + shift) % SLABS) for i in range(SLABS)])]
  transfers between devices with their start and end apart: 5 -> 13, of which waited for: 4 -> 12; matrix products, arithmetic and copies ran while one was open for 10% -> 0% of each run, Pallas kernels for 0% -> 1%
where the time goes in v1:
time: 176 us; the launch traced here: 175 us
  blocking collectives  107 us (61%)
  waiting for transfers between devices  21.8 us (12%)
  Pallas kernels  21 us (12%)
  local copies, waits for them, and re-layouts  13.1 us (7%)
  starting transfers between devices  10.8 us (6%)
    all_to_all x2, blocking collectives, sum_fields(): parts = lax.all_to_all(part, ATOM_REST, 0, 0, tiled=True)  42.7 us
    all_to_all x2, blocking collectives, sum_fields(): mine = lax.all_to_all(spread, ATOM_REST, 0, 0, tiled=True)  35.8 us
    all_gather x1, blocking collectives, per_device(): lax.all_gather(jnp.abs(signed)[None], ('x', 'yh'), axis=0, tiled=True)  28 us
    pallas_call x7, Pallas kernels, call(): pl.pallas_call(kernel, grid_spec=pltpu.PrefetchScalarGridSpec(num_scalar_...  21 us
    ppermute x9, waiting for transfers between devices, shifted(): lax.ppermute(value, 'x', [(i, (i + shift) % SLABS) for i in range(SLABS)])  17 us
    unnamed x58, local copies, waits for them, and re-layouts  13 us
    ppermute x9, starting transfers between devices, shifted(): lax.ppermute(value, 'x', [(i, (i + shift) % SLABS) for i in range(SLABS)])  10.5 us
    ppermute x4, waiting for transfers between devices, swapped(): return lax.ppermute(value, 'core', [(0, 1), (1, 0)])  4.85 us
  transfers between devices with their start and end apart: 13, of which 12 were waited for; matrix products, arithmetic and copies ran while one was open for 0% of the time, Pallas kernels for 1%

profile of v1, /device:TPU:6, one launch (start us, length us, event | category | flops | bytes accessed | tf_op | source)
XLA Modules:
  0.0 174.5 jit_solution(13204846033488340174)
XLA Ops:
  8.1 6.4 %shard_map.105 = (bf16[4,1280,256]{2,1,0:T(8,128)(2,1)}, bf16[4,256,256]{2,1,0:T(8,128)(2,1)S(1)}, bf16[32,40,128]{2,1,0:T(8,128)(2,1)S(1)}, bf16[32,40,128]{2,1,0:T(8,128)(2,1)S(1)}) custom-call(s32[3]{0:T(128)S(1)} %pad_add_fusion.place, f32[2560,128]{1,0:T(8,128)S(1)} %copy-done.1, f32[3,2048]{1,0:T(4,128)S(1)} %copy-done.26, s32[1,2048]{1,0:T(1,128)S(1)} %bitcast.13, ...), custom_call_target="tpu_custom_call" | custom-call | tf_op jit(solution)/shard_map/pallas_call | solution.py:341
  15.3 1.6 collective-permute-done
  17.0 24.9 %all_to_all.20 = bf16[32,40,128]{2,1,0:T(8,128)(2,1)S(1)} all-to-all(bf16[32,40,128]{2,1,0:T(8,128)(2,1)S(1)} %add_convert_fusion.1), channel_id=1, replica_groups=mesh['x'=4,'yh'=2,'yl'=2,'z'=8,'core'=2] {'yh','yl','z'}, dimensions={0} | all-to-all | bytes 655360 | tf_op jit(solution)/shard_map/all_to_all | solution.py:370
  42.0 17.9 %all_to_all.21.mine_ref = bf16[32,40,128]{2,1,0:T(8,128)(2,1)S(1)} all-to-all(bf16[32,40,128]{2,1,0:T(8,128)(2,1)S(1)} %broadcast_in_dim.7), channel_id=1, replica_groups=mesh['x'=4,'yh'=2,'yl'=2,'z'=8,'core'=2] {'yh','yl','z'}, dimensions={0} | all-to-all | bytes 655360 | tf_op jit(solution)/shard_map/all_to_all | solution.py:373
  60.0 28.0 %all-gather = s32[8,1,512]{2,1,0:T(1,128)S(1)} all-gather(s32[1,1,512]{2,1,0:T(1,128)S(1)} %abs_bitcast_fusion), channel_id=1, replica_groups=mesh['x'=4,'yh'=2,'yl'=2,'z'=8,'core'=2] {'x','yh'}, dimensions={0}, use_global_device_ids=true | all-gather | bytes 18432 | tf_op jit(solution)/shard_map/all_gather | solution.py:402
  89.3 1.7 %shard_map.104.weights_ref = f32[2,640,128]{2,1,0:T(8,128)S(1)} custom-call(s32[3]{0:T(128)S(1)} %pad_add_fusion.place, f32[2560,128]{1,0:T(8,128)S(1)} %copy-done.2, s32[8,512]{1,0:T(8,128)S(1)} %bitcast.16), custom_call_target="tpu_custom_call" | custom-call | tf_op jit(solution)/shard_map/pallas_call | solution.py:341
  91.1 2.5 %shard_map.106 = (bf16[1280,256]{1,0:T(8,128)(2,1)S(1)}, bf16[256,256]{1,0:T(8,128)(2,1)S(1)}, bf16[256,256]{1,0:T(8,128)(2,1)S(1)}, bf16[256,256]{1,0:T(8,128)(2,1)S(1)}, bf16[256,256]{1,0:T(8,128)(2,1)S(1)}) custom-call(s32[3]{0:T(128)S(1)} %pad_add_fusion.place, f32[2,640,128]{2,1,0:T(8,128)S(1)} %shard_map.104.weights_ref, ...), custom_call_target="tpu_custom_call" | custom-call | tf_op jit(solution)/shard_map/pallas_call | solution.py:341
  93.6 2.5 %collective-permute-start.2 = (bf16[256,256]{1,0:T(8,128)(2,1)S(1)}, bf16[256,256]{1,0:T(8,128)(2,1)S(1)}, u32[]{:S(2)}, u32[]{:S(2)}) collective-permute-start(bf16[256,256]{1,0:T(8,128)(2,1)S(1)} %get-tuple-element.23), channel_id=1, source_target_pairs={{0,64},{64,128},{128,192},{192,0},{1,65},{65,129},{129,193},{193,1... | collective-permute-start | bytes 393224 | tf_op jit(solution)/shard_map/ppermute | solution.py:361
  97.8 2.2 %collective-permute-done.2.q1 = bf16[256,256]{1,0:T(8,128)(2,1)S(1)} collective-permute-done((bf16[256,256]{1,0:T(8,128)(2,1)S(1)}, bf16[256,256]{1,0:T(8,128)(2,1)S(1)}, u32[]{:S(2)}, u32[]{:S(2)}) %collective-permute-start.2) | collective-permute-done | bytes 131104 | tf_op jit(solution)/shard_map/ppermute | solution.py:361
  100.0 2.6 %collective-permute-done.3.q2 = bf16[256,256]{1,0:T(8,128)(2,1)S(1)} collective-permute-done((bf16[256,256]{1,0:T(8,128)(2,1)S(1)}, bf16[256,256]{1,0:T(8,128)(2,1)S(1)}, u32[]{:S(2)}, u32[]{:S(2)}) %collective-permute-start.3) | collective-permute-done | bytes 131104 | tf_op jit(solution)/shard_map/ppermute | solution.py:361
  102.7 1.3 collective-permute-done.4.q3
  105.8 1.9 %collective-permute-start.6 = (bf16[256,256]{1,0:T(8,128)(2,1)S(1)}, bf16[256,256]{1,0:T(8,128)(2,1)S(1)}, u32[]{:S(2)}, u32[]{:S(2)}) collective-permute-start(bf16[256,256]{1,0:T(8,128)(2,1)S(1)} %get-tuple-element.26.v0), channel_id=1, source_target_pairs={{0,128},{64,192},{128,0},{192,64},{1,129},{65,193},{129,1},{193,65... | collective-permute-start | bytes 393224 | tf_op jit(solution)/shard_map/ppermute | solution.py:361
  108.6 1.6 collective-permute-done.7.v3
  110.3 2.1 %collective-permute-done.6.v2 = bf16[256,256]{1,0:T(8,128)(2,1)S(1)} collective-permute-done((bf16[256,256]{1,0:T(8,128)(2,1)S(1)}, bf16[256,256]{1,0:T(8,128)(2,1)S(1)}, u32[]{:S(2)}, u32[]{:S(2)}) %collective-permute-start.6) | collective-permute-done | bytes 131104 | tf_op jit(solution)/shard_map/ppermute | solution.py:361
  112.3 1.6 collective-permute-done.5.v1
  113.9 2.2 %shard_map.108 = (bf16[32,40,128]{2,1,0:T(8,128)(2,1)S(1)}, bf16[32,40,128]{2,1,0:T(8,128)(2,1)S(1)}) custom-call(s32[3]{0:T(128)S(1)} %pad_add_fusion.place, bf16[4,1280,256]{2,1,0:T(8,128)(2,1)S(1)} %copy-done, bf16[256,256]{1,0:T(8,128)(2,1)S(1)} %get-tuple-element.26.v0, bf16[256,256]{1,0:T(8,128)(2,1)S(1)} %collective-permute-done.5.v1, ...), custom_call_target="tpu_custom_call" | custom-call | tf_op jit(solution)/shard_map/pallas_call | solution.py:341
  116.4 1.6 collective-permute-done.8
  118.2 17.8 %all_to_all.22 = bf16[32,40,128]{2,1,0:T(8,128)(2,1)S(1)} all-to-all(bf16[32,40,128]{2,1,0:T(8,128)(2,1)S(1)} %add_convert_fusion), channel_id=1, replica_groups=mesh['x'=4,'yh'=2,'yl'=2,'z'=8,'core'=2] {'yh','yl','z'}, dimensions={0} | all-to-all | bytes 655360 | tf_op jit(solution)/shard_map/all_to_all | solution.py:370
  136.1 17.9 %all_to_all.23.mine_ref = bf16[32,40,128]{2,1,0:T(8,128)(2,1)S(1)} all-to-all(bf16[32,40,128]{2,1,0:T(8,128)(2,1)S(1)} %broadcast_in_dim.8), channel_id=1, replica_groups=mesh['x'=4,'yh'=2,'yl'=2,'z'=8,'core'=2] {'yh','yl','z'}, dimensions={0} | all-to-all | bytes 655360 | tf_op jit(solution)/shard_map/all_to_all | solution.py:373
  154.0 1.6 collective-permute-done.9.other_ref
  159.1 5.5 %shard_map.109 = (bf16[144,256]{1,0:T(8,128)(2,1)S(1)}, bf16[144,256]{1,0:T(8,128)(2,1)S(1)}, bf16[144,256]{1,0:T(8,128)(2,1)S(1)}, bf16[144,256]{1,0:T(8,128)(2,1)S(1)}) custom-call(s32[3]{0:T(128)S(1)} %pad_add_fusion.place, f32[2,640,128]{2,1,0:T(8,128)S(1)} %shard_map.104.weights_ref, bf16[32,40,128]{2,1,0:T(8,128)(2,1)S(1)} %all_to_all.23.mine_ref, ...), custom_call_target="tpu_custom_call" | custom-call | tf_op jit(solution)/shard_map/pallas_call | solution.py:341
  167.4 2.3 %collective-permute-done.10.q1 = bf16[144,256]{1,0:T(8,128)(2,1)S(1)} collective-permute-done((bf16[144,256]{1,0:T(8,128)(2,1)S(1)}, bf16[144,256]{1,0:T(8,128)(2,1)S(1)}, u32[]{:S(2)}, u32[]{:S(2)}) %collective-permute-start.10) | collective-permute-done | bytes 73760 | tf_op jit(solution)/shard_map/ppermute | solution.py:361
  169.7 2.8 %collective-permute-done.11.q2 = bf16[144,256]{1,0:T(8,128)(2,1)S(1)} collective-permute-done((bf16[144,256]{1,0:T(8,128)(2,1)S(1)}, bf16[144,256]{1,0:T(8,128)(2,1)S(1)}, u32[]{:S(2)}, u32[]{:S(2)}) %collective-permute-start.11) | collective-permute-done | bytes 73760 | tf_op jit(solution)/shard_map/ppermute | solution.py:361
  173.0 1.6 shard_map.110
  (80 shorter events, 21.5 us)
Async XLA Ops:
  8.1 51.9 %copy-start.27 = (s32[3,512]{1,0:T(4,128)S(1)}, s32[3,512]{1,0:T(4,128)}, u32[]{:S(2)}) copy-start(s32[3,512]{1,0:T(4,128)} %param.12) | copy-start | bytes 18436
  15.3 75.8 %copy-start = (bf16[4,1280,256]{2,1,0:T(8,128)(2,1)S(1)}, bf16[4,1280,256]{2,1,0:T(8,128)(2,1)}, u32[]{:S(2)}) copy-start(bf16[4,1280,256]{2,1,0:T(8,128)(2,1)} %get-tuple-element.19.table_ref) | copy-start | bytes 7864324
  15.3 1.6 collective-permute-start
  59.9 31.2 %collective-permute-start.1 = (bf16[32,40,128]{2,1,0:T(8,128)(2,1)S(1)}, bf16[32,40,128]{2,1,0:T(8,128)(2,1)S(1)}, u32[]{:S(2)}, u32[]{:S(2)}) collective-permute-start(bf16[32,40,128]{2,1,0:T(8,128)(2,1)S(1)} %all_to_all.21.mine_ref), channel_id=1, source_target_pairs={{0,1},{1,0},{2,3},{3,2},{4,5},{5,4},{6,7},{7,6},{8,9},{9,8},{10,11... | collective-permute-start | bytes 983048 | tf_op jit(solution)/shard_map/ppermute | solution.py:365
  89.3 14.7 %copy-start.7 = (bf16[2048,128]{1,0:T(8,128)(2,1)S(1)}, bf16[2048,128]{1,0:T(8,128)(2,1)}, u32[]{:S(2)}) copy-start(bf16[2048,128]{1,0:T(8,128)(2,1)} %upstream_ref.3) | copy-start | bytes 1572868
  89.3 14.7 %copy-start.11 = (bf16[2,128,128]{2,1,0:T(8,128)(2,1)S(1)}, bf16[2,128,128]{2,1,0:T(8,128)(2,1)}, u32[]{:S(2)}) copy-start(bf16[2,128,128]{2,1,0:T(8,128)(2,1)} %inward_ref.5) | copy-start | bytes 196612
  89.3 14.7 %copy-start.23 = (bf16[2,128,128]{2,1,0:T(8,128)(2,1)S(1)}, bf16[2,128,128]{2,1,0:T(8,128)(2,1)}, u32[]{:S(2)}) copy-start(bf16[2,128,128]{2,1,0:T(8,128)(2,1)} %outward_ref.3) | copy-start | bytes 196612
  89.3 14.7 %copy-start.25 = (s32[2048]{0:T(1024)S(1)}, s32[2048]{0:T(1024)}, u32[]{:S(2)}) copy-start(s32[2048]{0:T(1024)} %param.11) | copy-start | bytes 24580
  93.6 24.6 %copy-start.8 = (bf16[1280,256]{1,0:T(8,128)(2,1)}, bf16[1280,256]{1,0:T(8,128)(2,1)S(1)}, u32[]{:S(2)}) copy-start(bf16[1280,256]{1,0:T(8,128)(2,1)S(1)} %get-tuple-element.29.fields_ref) | copy-start | bytes 1966084
  93.6 6.4 %collective-permute-start.2 = (bf16[256,256]{1,0:T(8,128)(2,1)S(1)}, bf16[256,256]{1,0:T(8,128)(2,1)S(1)}, u32[]{:S(2)}, u32[]{:S(2)}) collective-permute-start(bf16[256,256]{1,0:T(8,128)(2,1)S(1)} %get-tuple-element.23), channel_id=1, source_target_pairs={{0,64},{64,128},{128,192},{192,0},{1,65},{65,129},{129,193},{193,1... | collective-permute-start | bytes 393224 | tf_op jit(solution)/shard_map/ppermute | solution.py:361
  96.1 6.5 %collective-permute-start.3 = (bf16[256,256]{1,0:T(8,128)(2,1)S(1)}, bf16[256,256]{1,0:T(8,128)(2,1)S(1)}, u32[]{:S(2)}, u32[]{:S(2)}) collective-permute-start(bf16[256,256]{1,0:T(8,128)(2,1)S(1)} %get-tuple-element.24), channel_id=1, source_target_pairs={{0,128},{64,192},{128,0},{192,64},{1,129},{65,193},{129,1},{193,65... | collective-permute-start | bytes 393224 | tf_op jit(solution)/shard_map/ppermute | solution.py:361
  97.2 6.8 %collective-permute-start.4 = (bf16[256,256]{1,0:T(8,128)(2,1)S(1)}, bf16[256,256]{1,0:T(8,128)(2,1)S(1)}, u32[]{:S(2)}, u32[]{:S(2)}) collective-permute-start(bf16[256,256]{1,0:T(8,128)(2,1)S(1)} %get-tuple-element.25), channel_id=1, source_target_pairs={{0,192},{64,0},{128,64},{192,128},{1,193},{65,1},{129,65},{193,129... | collective-permute-start | bytes 393224 | tf_op jit(solution)/shard_map/ppermute | solution.py:361
  105.2 5.0 %collective-permute-start.7 = (bf16[256,256]{1,0:T(8,128)(2,1)S(1)}, bf16[256,256]{1,0:T(8,128)(2,1)S(1)}, u32[]{:S(2)}, u32[]{:S(2)}) collective-permute-start(bf16[256,256]{1,0:T(8,128)(2,1)S(1)} %get-tuple-element.26.v0), channel_id=1, source_target_pairs={{0,64},{64,128},{128,192},{192,0},{1,65},{65,129},{129,193},{193,1... | collective-permute-start | bytes 393224 | tf_op jit(solution)/shard_map/ppermute | solution.py:361
  105.8 6.5 %collective-permute-start.6 = (bf16[256,256]{1,0:T(8,128)(2,1)S(1)}, bf16[256,256]{1,0:T(8,128)(2,1)S(1)}, u32[]{:S(2)}, u32[]{:S(2)}) collective-permute-start(bf16[256,256]{1,0:T(8,128)(2,1)S(1)} %get-tuple-element.26.v0), channel_id=1, source_target_pairs={{0,128},{64,192},{128,0},{192,64},{1,129},{65,193},{129,1},{193,65... | collective-permute-start | bytes 393224 | tf_op jit(solution)/shard_map/ppermute | solution.py:361
  107.7 6.2 %collective-permute-start.5 = (bf16[256,256]{1,0:T(8,128)(2,1)S(1)}, bf16[256,256]{1,0:T(8,128)(2,1)S(1)}, u32[]{:S(2)}, u32[]{:S(2)}) collective-permute-start(bf16[256,256]{1,0:T(8,128)(2,1)S(1)} %get-tuple-element.26.v0), channel_id=1, source_target_pairs={{0,192},{64,0},{128,64},{192,128},{1,193},{65,1},{129,65},{193,129... | collective-permute-start | bytes 393224 | tf_op jit(solution)/shard_map/ppermute | solution.py:361
  116.1 39.5 %copy-start.15 = (bf16[256,256]{1,0:T(8,128)(2,1)S(1)}, bf16[256,256]{1,0:T(8,128)(2,1)}, u32[]{:S(2)}) copy-start(bf16[256,256]{1,0:T(8,128)(2,1)} %copy-done.14) | copy-start | bytes 393220
  116.1 1.9 %collective-permute-start.8 = (bf16[32,40,128]{2,1,0:T(8,128)(2,1)S(1)}, bf16[32,40,128]{2,1,0:T(8,128)(2,1)S(1)}, u32[]{:S(2)}, u32[]{:S(2)}) collective-permute-start(bf16[32,40,128]{2,1,0:T(8,128)(2,1)S(1)} %get-tuple-element.28), channel_id=1, source_target_pairs={{0,1},{1,0},{2,3},{3,2},{4,5},{5,4},{6,7},{7,6},{8,9},{9,8},{10,11... | collective-permute-start | bytes 983048 | tf_op jit(solution)/shard_map/ppermute | solution.py:365
  116.4 39.2 %copy-start.17 = (bf16[256,256]{1,0:T(8,128)(2,1)S(1)}, bf16[256,256]{1,0:T(8,128)(2,1)}, u32[]{:S(2)}) copy-start(bf16[256,256]{1,0:T(8,128)(2,1)} %copy-done.16) | copy-start | bytes 393220
  118.0 37.6 %copy-start.19 = (bf16[256,256]{1,0:T(8,128)(2,1)S(1)}, bf16[256,256]{1,0:T(8,128)(2,1)}, u32[]{:S(2)}) copy-start(bf16[256,256]{1,0:T(8,128)(2,1)} %copy-done.18) | copy-start | bytes 393220
  118.0 37.6 %copy-start.21 = (bf16[256,256]{1,0:T(8,128)(2,1)S(1)}, bf16[256,256]{1,0:T(8,128)(2,1)}, u32[]{:S(2)}) copy-start(bf16[256,256]{1,0:T(8,128)(2,1)} %copy-done.20) | copy-start | bytes 393220
  154.0 1.6 collective-permute-start.9
  164.5 5.2 %collective-permute-start.10 = (bf16[144,256]{1,0:T(8,128)(2,1)S(1)}, bf16[144,256]{1,0:T(8,128)(2,1)S(1)}, u32[]{:S(2)}, u32[]{:S(2)}) collective-permute-start(bf16[144,256]{1,0:T(8,128)(2,1)S(1)} %get-tuple-element.32), channel_id=1, source_target_pairs={{0,64},{64,128},{128,192},{192,0},{1,65},{65,129},{129,193},{193,1... | collective-permute-start | bytes 221192 | tf_op jit(solution)/shard_map/ppermute | solution.py:361
  165.8 6.6 %collective-permute-start.11 = (bf16[144,256]{1,0:T(8,128)(2,1)S(1)}, bf16[144,256]{1,0:T(8,128)(2,1)S(1)}, u32[]{:S(2)}, u32[]{:S(2)}) collective-permute-start(bf16[144,256]{1,0:T(8,128)(2,1)S(1)} %get-tuple-element.33), channel_id=1, source_target_pairs={{0,128},{64,192},{128,0},{192,64},{1,129},{65,193},{129,1},{193,65... | collective-permute-start | bytes 221192 | tf_op jit(solution)/shard_map/ppermute | solution.py:361
  166.7 6.2 %collective-permute-start.12 = (bf16[144,256]{1,0:T(8,128)(2,1)S(1)}, bf16[144,256]{1,0:T(8,128)(2,1)S(1)}, u32[]{:S(2)}, u32[]{:S(2)}) collective-permute-start(bf16[144,256]{1,0:T(8,128)(2,1)S(1)} %get-tuple-element.34), channel_id=1, source_target_pairs={{0,192},{64,0},{128,64},{192,128},{1,193},{65,1},{129,65},{193,129... | collective-permute-start | bytes 221192 | tf_op jit(solution)/shard_map/ppermute | solution.py:361
  (17 other events, 51.8 us)

commit v2 on v1

--- a/solution.py
+++ b/solution.py
@@ -3,7 +3,6 @@
 
 import jax
 import jax.numpy as jnp
-import numpy as np
 from jax import lax
 from jax.experimental import pallas as pl
 from jax.experimental.pallas import tpu as pltpu
@@ -22,40 +21,36 @@
 CHANNELS = 128
 ROWS = 40
 PIECES = 32
-VMEM_LIMIT = 48 * 1024 * 1024
+VMEM_SHARED = 24 * 1024 * 1024
+VMEM_ALL = 62 * 1024 * 1024
 BF16 = jnp.bfloat16
 F32 = jnp.float32
 
 COS_SERIES = (
-    0.999999995487496,
-    -19.739205575083908,
-    64.93915835436466,
-    -85.45075924609554,
-    60.172044623035546,
-    -25.982406908145567,
-    6.5475440523380986,
+    0.999999660315462,
+    -19.739032161520388,
+    64.93001235415629,
+    -85.28515888817482,
+    58.84788533073816,
+    -21.15810679384873,
 )
 SIN_SERIES = (
-    6.283185281044049,
-    -41.34169782356279,
-    81.60504596930859,
-    -76.70182055142223,
-    42.01785583003898,
-    -14.873772878742722,
-    3.2058159421849517,
+    6.283183359037432,
+    -41.341456424111435,
+    81.59687947501621,
+    -76.58597187733577,
+    41.22756686823296,
+    -12.302134397179453,
 )
 
 
-def class_vectors():
-    label = np.arange(SLABS * SLAB)
-    label = np.where(label < CLASSES, label, 0)
-    first = (label + (SPAN * SPAN) // 2) // (SPAN * SPAN)
-    rest = label - SPAN * SPAN * first + (SPAN * SPAN) // 2
-    second = rest // SPAN - REACH
-    third = rest % SPAN - REACH
-    table = np.zeros((SLABS * SLAB, CHANNELS), np.float32)
-    table[:, 0], table[:, 1], table[:, 2] = first, second, third
-    return table
+def class_vectors(first_class, shape, axis):
+    label = (lax.broadcasted_iota(jnp.int32, shape, axis) + first_class).astype(F32)
+    square = SPAN * SPAN
+    first = jnp.floor((label + (square // 2 + 0.5)) * (1.0 / square))
+    rest = label - square * first
+    second = jnp.floor((rest + (REACH + 0.5)) * (1.0 / SPAN))
+    return first, second, rest - SPAN * second
 
 
 def matmul(left, right, left_dim, right_dim):
@@ -69,9 +64,12 @@
 
 
 def gain_columns(multiplier, labels):
-    result = jnp.zeros((multiplier.shape[0], labels.shape[1]), F32)
-    for species in range(multiplier.shape[1]):
-        result = jnp.where(labels == species, multiplier[:, species : species + 1], result)
+    species_count, channels = multiplier.shape
+    padding = jnp.zeros((8 - species_count, channels), F32)
+    columns = jnp.transpose(jnp.concatenate([multiplier, padding], axis=0))
+    result = jnp.zeros((channels, labels.shape[1]), F32)
+    for species in range(species_count):
+        result = jnp.where(labels == species, columns[:, species : species + 1], result)
     return result
 
 
@@ -106,7 +104,6 @@
 
 def tables_kernel(
     place,
-    vectors_ref,
     coordinates_ref,
     labels_ref,
     features_ref,
@@ -121,20 +118,22 @@
     total_ref,
 ):
     step = pl.program_id(0)
-    along = [coordinates_ref[axis : axis + 1, :] for axis in range(3)]
     chunk = 64
     for start in range(0, SLAB, chunk):
         rows = pl.ds(start, chunk)
-        turns = vectors_ref[rows, 0:1] * along[0]
-        turns += vectors_ref[rows, 1:2] * along[1]
-        turns += vectors_ref[rows, 2:3] * along[2]
-        turns -= jnp.floor(turns + 0.5)
-        square = turns * turns
-        table_ref[0, rows, :] = series(COS_SERIES, square).astype(BF16)
-        table_ref[0, pl.ds(SLAB + start, chunk), :] = (
-            turns * series(SIN_SERIES, square)
-        ).astype(BF16)
-    gains = gain_columns(multiplier_ref[0], labels_ref[...])
+        vectors = class_vectors(place[0] * SLAB + start, (chunk, CHANNELS), 0)
+        for side in range(BLOCK // CHANNELS):
+            columns = pl.ds(side * CHANNELS, CHANNELS)
+            turns = vectors[0] * coordinates_ref[0:1, columns]
+            turns += vectors[1] * coordinates_ref[1:2, columns]
+            turns += vectors[2] * coordinates_ref[2:3, columns]
+            turns -= jnp.floor(turns + 0.5)
+            square = turns * turns
+            table_ref[0, rows, columns] = series(COS_SERIES, square).astype(BF16)
+            table_ref[0, pl.ds(SLAB + start, chunk), columns] = (
+                turns * series(SIN_SERIES, square)
+            ).astype(BF16)
+    gains = gain_columns(multiplier_ref[:, 0, :], labels_ref[...])
     charges = matmul(flip(inward_ref[0]), features_ref[...], 1, 1) * gains
     grad_pot = matmul(outward_ref[1], upstream_ref[...], 1, 1)
     values = jnp.concatenate([charges, grad_pot], axis=0).astype(BF16)
@@ -154,7 +153,7 @@
         write_pieces(place, total_ref, keep_ref, send_ref)
 
 
-def weights_kernel(prefactor, place, vectors_ref, classes_ref, weights_ref):
+def weights_kernel(prefactor, place, classes_ref, weights_ref):
     chunk = 128
     for start in range(0, SLAB, chunk):
         rows = pl.ds(start, chunk)
@@ -165,11 +164,10 @@
                 classes = classes_ref[group : group + 1, offset : offset + CHANNELS]
                 count += jnp.where(classes == own, 1.0, 0.0)
         count = jnp.sum(count, axis=1, keepdims=True)
-        vectors = vectors_ref[rows, :]
-        norm = jnp.sum(vectors * vectors, axis=1, keepdims=True)
+        vectors = class_vectors(place[0] * SLAB + start, (chunk, CHANNELS), 0)
+        norm = vectors[0] * vectors[0] + vectors[1] * vectors[1] + vectors[2] * vectors[2]
         for block, spread in enumerate(GAUSSIAN_SIGMAS):
-            weight = count * (prefactor * jnp.exp(norm * (-1.0 / spread)))
-            weights_ref[block, rows, :] = jnp.broadcast_to(weight, (chunk, CHANNELS))
+            weights_ref[block, rows, :] = count * (prefactor * jnp.exp(norm * (-1.0 / spread)))
 
 
 def potential_kernel(
@@ -214,7 +212,7 @@
     total = (q0[...].astype(F32) + q1[...].astype(F32)) + (q2[...].astype(F32) + q3[...].astype(F32))
     potential = total[:CHANNELS].astype(BF16)
     grad_charge = total[CHANNELS:]
-    gains = gain_columns(multiplier_ref[1], labels_ref[...])
+    gains = gain_columns(multiplier_ref[:, 1, :], labels_ref[...])
     hidden = (
         features_ref[...].astype(F32)
         + matmul(jnp.transpose(potential.astype(F32)).astype(BF16), outward_ref[0], 1, 0)
@@ -253,7 +251,6 @@
     mine_ref,
     other_ref,
     fields_ref,
-    vectors_ref,
     table_ref,
     first_ref,
     v0,
@@ -288,7 +285,10 @@
         pairs_ref[:, 2 * CHANNELS : 3 * CHANNELS] = fields_ref[:, CHANNELS:]
         pairs_ref[:, 3 * CHANNELS :] = fields_ref[:, :CHANNELS]
         flipped_ref[...] = jnp.transpose(grad_one).astype(BF16)
-        directions_ref[...] = jnp.transpose(vectors_ref[...])[:16].astype(BF16)
+        vectors = class_vectors(place[0] * SLAB, (16, SLAB), 1)
+        row = lax.broadcasted_iota(jnp.int32, (16, SLAB), 0)
+        directions = jnp.where(row == 0, vectors[0], jnp.where(row == 1, vectors[1], vectors[2]))
+        directions_ref[...] = jnp.where(row < 3, directions, 0.0).astype(BF16)
 
     for index, source in enumerate((v0, v1, v2, v3)):
 
@@ -321,7 +321,7 @@
     place, q0, q1, q2, q3, labels_ref, hidden_grad_ref, inward_ref, multiplier_ref, features_ref, positions_ref
 ):
     total = (q0[...].astype(F32) + q1[...].astype(F32)) + (q2[...].astype(F32) + q3[...].astype(F32))
-    gains = gain_columns(multiplier_ref[0], labels_ref[...])
+    gains = gain_columns(multiplier_ref[:, 0, :], labels_ref[...])
     scaled = jnp.transpose(total[:CHANNELS] * gains).astype(BF16)
     features_ref[...] = (
         hidden_grad_ref[...].astype(F32) + matmul(scaled, flip(inward_ref[0]), 1, 0)
@@ -337,7 +337,9 @@
     return pl.BlockSpec(shape, lambda step, place: (0,) * len(shape))
 
 
-def call(kernel, steps, in_specs, outs, out_specs, scratch, operands):
+def call(
+    kernel, steps, in_specs, outs, out_specs, scratch, operands, limit=VMEM_SHARED, micros=2
+):
     return pl.pallas_call(
         kernel,
         grid_spec=pltpu.PrefetchScalarGridSpec(
@@ -349,7 +351,10 @@
         ),
         out_shape=outs,
         compiler_params=pltpu.CompilerParams(
-            dimension_semantics=("arbitrary",), vmem_limit_bytes=VMEM_LIMIT
+            dimension_semantics=("arbitrary",), vmem_limit_bytes=limit
+        ),
+        cost_estimate=pl.CostEstimate(
+            flops=micros * 10**9, bytes_accessed=micros * 10**6, transcendentals=0
         ),
     )(*operands)
 
@@ -365,8 +370,11 @@
     return lax.ppermute(value, "core", [(0, 1), (1, 0)])
 
 
-def sum_fields(keep, send):
-    part = (keep.astype(F32) + swapped(send).astype(F32)).astype(BF16)
+def add_halves(keep, send):
+    return (keep.astype(F32) + swapped(send).astype(F32)).astype(BF16)
+
+
+def sum_fields(part):
     parts = lax.all_to_all(part, ATOM_REST, 0, 0, tiled=True)
     total = jnp.sum(parts.astype(F32), axis=0).astype(BF16)
     spread = jnp.broadcast_to(total[None], (PIECES,) + total.shape)
@@ -393,18 +401,15 @@
         * lax.axis_size(("x", "yh", "yl", "z", "core"))
     )
     labels = element_labels[None, :]
-    multiplier = jnp.swapaxes(element_latent_multiplier, 1, 2)
-    species = multiplier.shape[2]
-    vectors = jnp.asarray(class_vectors())
+    multiplier = jnp.swapaxes(element_latent_multiplier, 0, 1)
     signed = (
         lattice_momenta[0] * (SPAN * SPAN) + lattice_momenta[1] * SPAN + lattice_momenta[2]
     )
-    classes = lax.all_gather(jnp.abs(signed)[None], ("x", "yh"), axis=0, tiled=True)
-
-    slab = pl.BlockSpec((SLAB, CHANNELS), lambda step, place: (place[0], 0))
-    own_slab = slab
+    own = jnp.abs(signed)[None]
+    row = jnp.concatenate([own] + [shifted(own, shift) for shift in range(1, SLABS)], axis=0)
+
     matrices = whole((2, CHANNELS, CHANNELS))
-    gains_spec = whole((2, CHANNELS, species))
+    gains_spec = whole(multiplier.shape)
     pieces_spec = whole((PIECES, ROWS, CHANNELS))
     pieces_shape = shape_of((PIECES, ROWS, CHANNELS), BF16)
     values_block = whole((BLOCK, BLOCK))
@@ -420,7 +425,6 @@
         tables_kernel,
         SLABS,
         [
-            slab,
             pl.BlockSpec((3, BLOCK), lambda step, place: (0, 2 * step + place[1])),
             pl.BlockSpec((1, BLOCK), lambda step, place: (0, 2 * step + place[1])),
             pl.BlockSpec((BLOCK, CHANNELS), lambda step, place: (2 * step + place[1], 0)),
@@ -439,7 +443,6 @@
         [pltpu.VMEM((TABLE, BLOCK), F32)],
         (
             place,
-            vectors,
             unit_cell_coordinates,
             labels,
             atomic_descriptors,
@@ -448,17 +451,24 @@
             latent_to_feature_matrix,
             multiplier,
         ),
-    )
+        limit=VMEM_ALL,
+        micros=9,
+    )
+    keep, send, row = lax.optimization_barrier((keep, send, row))
+    part = add_halves(keep, send)
+    other_row = lax.ppermute(row, "yh", [(0, 1), (1, 0)])
+    part, other_row = lax.optimization_barrier((part, other_row))
+    classes = jnp.concatenate([row, other_row], axis=0)
     weights = call(
         functools.partial(weights_kernel, prefactor),
         1,
-        [own_slab, whole(classes.shape)],
+        [whole(classes.shape)],
         shape_of((2, SLAB, CHANNELS), F32),
         whole((2, SLAB, CHANNELS)),
         [],
-        (place, vectors, classes),
-    )
-    mine, other = sum_fields(keep, send)
+        (place, classes),
+    )
+    mine, other = sum_fields(part)
     fields, *products = call(
         potential_kernel,
         SLABS,
@@ -500,7 +510,7 @@
         [pltpu.VMEM((TABLE, BLOCK), F32)],
         (place, table, *seconds),
     )
-    mine, other = sum_fields(keep, send)
+    mine, other = sum_fields(add_halves(keep, send))
     result_shape = shape_of((CHANNELS + 16, BLOCK), BF16)
     result_spec = whole((CHANNELS + 16, BLOCK))
     results = call(
@@ -511,7 +521,6 @@
             pieces_spec,
             pieces_spec,
             whole((TABLE, BLOCK)),
-            own_slab,
             rotated((TABLE, BLOCK), 1),
             rotated((BLOCK, BLOCK), 1),
         ]
@@ -526,7 +535,9 @@
             pltpu.VMEM((SLAB, BLOCK), BF16),
             pltpu.VMEM((BLOCK, BLOCK), BF16),
         ],
-        (place, weights, mine, other, fields, vectors, table, values_one, *seconds),
+        (place, weights, mine, other, fields, table, values_one, *seconds),
+        limit=VMEM_ALL,
+        micros=6,
     )
     arrived = [results[0]] + [shifted(results[shift], shift) for shift in range(1, SLABS)]
     return call(

time: 176 us -> 150 us (0.85)
  blocking collectives: 107 us -> 76.9 us
  local copies, waits for them, and re-layouts: 13.1 us -> 1.79 us
  starting transfers between devices: 10.8 us -> 17.4 us
  Pallas kernels: 21 us -> 25.7 us
  other arithmetic: 0.4 us -> 2.71 us
  waiting for transfers between devices: 21.8 us -> 23.6 us
    all_gather x1 -> x0, blocking collectives: 28 us -> none  [per_device(): lax.all_gather(jnp.abs(signed)[None], ('x', 'yh'), axis=0, tiled=True)]
    unnamed x58 -> x36, local copies, waits for them, and re-layouts: 13 us -> 1.7 us
    pallas_call x7, Pallas kernels: 21 us -> 25.7 us  [call(): pl.pallas_call(kernel, grid_spec=pltpu.PrefetchScalarGridSpec(num_scalar_...]
    ppermute x9 -> x12, starting transfers between devices: 10.5 us -> 13.9 us  [shifted(): lax.ppermute(value, 'x', [(i, (i + shift) % SLABS) for i in range(SLABS)])]
    ppermute x0 -> x1, starting transfers between devices: none -> 3.28 us  [per_device(): other_row = lax.ppermute(row, 'yh', [(0, 1), (1, 0)])]
    ppermute x9 -> x12, waiting for transfers between devices: 17 us -> 19.5 us  [shifted(): lax.ppermute(value, 'x', [(i, (i + shift) % SLABS) for i in range(SLABS)])]
  transfers between devices with their start and end apart: 13 -> 17, of which waited for: 12 -> 12; matrix products, arithmetic and copies ran while one was open for 0% -> 1% of each run, Pallas kernels for 1% -> 7%
where the time goes in v2:
time: 150 us; the launch traced here: 149 us
  blocking collectives  76.9 us (51%)
  Pallas kernels  25.7 us (17%)
  waiting for transfers between devices  23.6 us (16%)
  starting transfers between devices  17.4 us (12%)
  other arithmetic  2.71 us (2%)
  local copies, waits for them, and re-layouts  1.79 us (1%)
    all_to_all x2, blocking collectives, sum_fields(): parts = lax.all_to_all(part, ATOM_REST, 0, 0, tiled=True)  42.4 us
    all_to_all x2, blocking collectives, sum_fields(): mine = lax.all_to_all(spread, ATOM_REST, 0, 0, tiled=True)  34.5 us
    pallas_call x7, Pallas kernels, call(): pl.pallas_call(kernel, grid_spec=pltpu.PrefetchScalarGridSpec(num_scalar_...  25.7 us
    ppermute x12, waiting for transfers between devices, shifted(): lax.ppermute(value, 'x', [(i, (i + shift) % SLABS) for i in range(SLABS)])  19.5 us
    ppermute x12, starting transfers between devices, shifted(): lax.ppermute(value, 'x', [(i, (i + shift) % SLABS) for i in range(SLABS)])  13.9 us
    ppermute x1, starting transfers between devices, per_device(): other_row = lax.ppermute(row, 'yh', [(0, 1), (1, 0)])  3.28 us
    ppermute x4, waiting for transfers between devices, swapped(): return lax.ppermute(value, 'core', [(0, 1), (1, 0)])  3.25 us
  transfers between devices with their start and end apart: 17, of which 12 were waited for; matrix products, arithmetic and copies ran while one was open for 1% of the time, Pallas kernels for 7%

profile of v2, /device:TPU:6, one launch (start us, length us, event | category | flops | bytes accessed | tf_op | source)
XLA Modules:
  0.0 149.0 jit_solution(16055779804792546132)
XLA Ops:
  2.4 2.8 %collective-permute-start.1 = (s32[1,512]{1,0:T(1,128)S(1)}, s32[1,512]{1,0:T(1,128)S(1)}, u32[]{:S(2)}, u32[]{:S(2)}) collective-permute-start(s32[1,512]{1,0:T(1,128)S(1)} %add_abs_fusion), channel_id=1, source_target_pairs={{0,128},{64,192},{128,0},{192,64},{1,129},{65,193},{129,1},{193,65... | collective-permute-start | bytes 6152 | tf_op jit(solution)/shard_map/ppermute | solution.py:366
  6.1 9.0 %shard_map.95 = (bf16[4,1280,256]{2,1,0:T(8,128)(2,1)}, bf16[4,256,256]{2,1,0:T(8,128)(2,1)}, bf16[32,40,128]{2,1,0:T(8,128)(2,1)}, bf16[32,40,128]{2,1,0:T(8,128)(2,1)}) custom-call(s32[3]{0:T(128)} %pad_add_fusion.2.place, f32[3,2048]{1,0:T(4,128)} %coordinates_ref.1, s32[1,2048]{1,0:T(1,128)} %bitcast.5, bf16[2048,128]{1,0:T(8,128)(2,1)} %features_ref.3, ...), custom_call_target="tpu_custom_call" | custom-call | flops 8999999488 | bytes 9000000 | tf_op jit(solution)/shard_map/pallas_call | solution.py:343
  15.3 3.3 %collective-permute-start.4 = (s32[4,512]{1,0:T(4,128)S(1)}, s32[4,512]{1,0:T(4,128)S(1)}, u32[]{:S(2)}, u32[]{:S(2)}) collective-permute-start(s32[4,512]{1,0:T(4,128)S(1)} %pad_add_fusion.1), channel_id=1, source_target_pairs={{0,32},{32,0},{1,33},{33,1},{2,34},{34,2},{3,35},{35,3},{4,36},{36... | collective-permute-start | bytes 24584 | tf_op jit(solution)/shard_map/ppermute | solution.py:459
  20.6 24.1 %all_to_all.20 = bf16[32,40,128]{2,1,0:T(8,128)(2,1)S(1)} all-to-all(bf16[32,40,128]{2,1,0:T(8,128)(2,1)S(1)} %add_convert_fusion.1), channel_id=1, replica_groups=mesh['x'=4,'yh'=2,'yl'=2,'z'=8,'core'=2] {'yh','yl','z'}, dimensions={0} | all-to-all | bytes 655360 | tf_op jit(solution)/shard_map/all_to_all | solution.py:378
  44.8 16.6 %all_to_all.21.mine_ref = bf16[32,40,128]{2,1,0:T(8,128)(2,1)S(1)} all-to-all(bf16[32,40,128]{2,1,0:T(8,128)(2,1)S(1)} %broadcast_in_dim.7), channel_id=1, replica_groups=mesh['x'=4,'yh'=2,'yl'=2,'z'=8,'core'=2] {'yh','yl','z'}, dimensions={0} | all-to-all | bytes 655360 | tf_op jit(solution)/shard_map/all_to_all | solution.py:381
  61.4 1.9 %shard_map.96.weights_ref = f32[2,640,128]{2,1,0:T(8,128)S(1)} custom-call(s32[3]{0:T(128)S(1)} %copy-done, s32[8,512]{1,0:T(8,128)S(1)} %pad_add_fusion.classes_ref), custom_call_target="tpu_custom_call" | custom-call | flops 2000000000 | bytes 2000000 | tf_op jit(solution)/shard_map/pallas_call | solution.py:343
  63.4 2.5 %shard_map.97 = (bf16[1280,256]{1,0:T(8,128)(2,1)S(1)}, bf16[256,256]{1,0:T(8,128)(2,1)S(1)}, bf16[256,256]{1,0:T(8,128)(2,1)S(1)}, bf16[256,256]{1,0:T(8,128)(2,1)S(1)}, bf16[256,256]{1,0:T(8,128)(2,1)S(1)}) custom-call(s32[3]{0:T(128)S(1)} %copy-done, f32[2,640,128]{2,1,0:T(8,128)S(1)} %shard_map.96.weights_ref, ...), custom_call_target="tpu_custom_call" | custom-call | flops 2000000000 | bytes 2000000 | tf_op jit(solution)/shard_map/pallas_call | solution.py:343
  66.8 1.4 collective-permute-start.7
  69.5 2.7 %collective-permute-done.6.q1 = bf16[256,256]{1,0:T(8,128)(2,1)S(1)} collective-permute-done((bf16[256,256]{1,0:T(8,128)(2,1)S(1)}, bf16[256,256]{1,0:T(8,128)(2,1)S(1)}, u32[]{:S(2)}, u32[]{:S(2)}) %collective-permute-start.6) | collective-permute-done | bytes 131104 | tf_op jit(solution)/shard_map/ppermute | solution.py:366
  72.3 2.4 %collective-permute-done.7.q2 = bf16[256,256]{1,0:T(8,128)(2,1)S(1)} collective-permute-done((bf16[256,256]{1,0:T(8,128)(2,1)S(1)}, bf16[256,256]{1,0:T(8,128)(2,1)S(1)}, u32[]{:S(2)}, u32[]{:S(2)}) %collective-permute-start.7) | collective-permute-done | bytes 131104 | tf_op jit(solution)/shard_map/ppermute | solution.py:366
  74.7 2.1 %collective-permute-done.8.q3 = bf16[256,256]{1,0:T(8,128)(2,1)S(1)} collective-permute-done((bf16[256,256]{1,0:T(8,128)(2,1)S(1)}, bf16[256,256]{1,0:T(8,128)(2,1)S(1)}, u32[]{:S(2)}, u32[]{:S(2)}) %collective-permute-start.8) | collective-permute-done | bytes 131104 | tf_op jit(solution)/shard_map/ppermute | solution.py:366
  78.7 1.6 %collective-permute-start.10 = (bf16[256,256]{1,0:T(8,128)(2,1)S(1)}, bf16[256,256]{1,0:T(8,128)(2,1)S(1)}, u32[]{:S(2)}, u32[]{:S(2)}) collective-permute-start(bf16[256,256]{1,0:T(8,128)(2,1)S(1)} %get-tuple-element.36.v0), channel_id=1, source_target_pairs={{0,128},{64,192},{128,0},{192,64},{1,129},{65,193},{129,1},{193,65... | collective-permute-start | bytes 393224 | tf_op jit(solution)/shard_map/ppermute | solution.py:366
  81.2 3.3 %collective-permute-done.11.v3 = bf16[256,256]{1,0:T(8,128)(2,1)S(1)} collective-permute-done((bf16[256,256]{1,0:T(8,128)(2,1)S(1)}, bf16[256,256]{1,0:T(8,128)(2,1)S(1)}, u32[]{:S(2)}, u32[]{:S(2)}) %collective-permute-start.11) | collective-permute-done | bytes 131104 | tf_op jit(solution)/shard_map/ppermute | solution.py:366
  84.5 1.9 %collective-permute-done.10.v2 = bf16[256,256]{1,0:T(8,128)(2,1)S(1)} collective-permute-done((bf16[256,256]{1,0:T(8,128)(2,1)S(1)}, bf16[256,256]{1,0:T(8,128)(2,1)S(1)}, u32[]{:S(2)}, u32[]{:S(2)}) %collective-permute-start.10) | collective-permute-done | bytes 131104 | tf_op jit(solution)/shard_map/ppermute | solution.py:366
  86.5 1.7 %collective-permute-done.9.v1 = bf16[256,256]{1,0:T(8,128)(2,1)S(1)} collective-permute-done((bf16[256,256]{1,0:T(8,128)(2,1)S(1)}, bf16[256,256]{1,0:T(8,128)(2,1)S(1)}, u32[]{:S(2)}, u32[]{:S(2)}) %collective-permute-start.9) | collective-permute-done | bytes 131104 | tf_op jit(solution)/shard_map/ppermute | solution.py:366
  88.2 2.2 %shard_map.99 = (bf16[32,40,128]{2,1,0:T(8,128)(2,1)S(1)}, bf16[32,40,128]{2,1,0:T(8,128)(2,1)S(1)}) custom-call(s32[3]{0:T(128)S(1)} %copy-done, bf16[4,1280,256]{2,1,0:T(8,128)(2,1)S(1)} %copy-done.12, bf16[256,256]{1,0:T(8,128)(2,1)S(1)} %get-tuple-element.36.v0, bf16[256,256]{1,0:T(8,128)(2,1)S(1)} %collective-permute-done.9.v1, ...), custom_call_target="tpu_custom_call" | custom-call | flops 2000000000 | bytes 2000000 | tf_op jit(solution)/shard_map/pallas_call | solution.py:343
  90.5 1.6 %collective-permute-done.12 = bf16[32,40,128]{2,1,0:T(8,128)(2,1)S(1)} collective-permute-done((bf16[32,40,128]{2,1,0:T(8,128)(2,1)S(1)}, bf16[32,40,128]{2,1,0:T(8,128)(2,1)S(1)}, u32[]{:S(2)}, u32[]{:S(2)}) %collective-permute-start.12) | collective-permute-done | bytes 327712 | tf_op jit(solution)/shard_map/ppermute | solution.py:370
  92.3 18.4 %all_to_all.22 = bf16[32,40,128]{2,1,0:T(8,128)(2,1)S(1)} all-to-all(bf16[32,40,128]{2,1,0:T(8,128)(2,1)S(1)} %add_convert_fusion), channel_id=1, replica_groups=mesh['x'=4,'yh'=2,'yl'=2,'z'=8,'core'=2] {'yh','yl','z'}, dimensions={0} | all-to-all | bytes 655360 | tf_op jit(solution)/shard_map/all_to_all | solution.py:378
  110.7 17.9 %all_to_all.23.mine_ref = bf16[32,40,128]{2,1,0:T(8,128)(2,1)S(1)} all-to-all(bf16[32,40,128]{2,1,0:T(8,128)(2,1)S(1)} %broadcast_in_dim.8), channel_id=1, replica_groups=mesh['x'=4,'yh'=2,'yl'=2,'z'=8,'core'=2] {'yh','yl','z'}, dimensions={0} | all-to-all | bytes 655360 | tf_op jit(solution)/shard_map/all_to_all | solution.py:381
  128.6 1.6 %collective-permute-done.13.other_ref = bf16[32,40,128]{2,1,0:T(8,128)(2,1)S(1)} collective-permute-done((bf16[32,40,128]{2,1,0:T(8,128)(2,1)S(1)}, bf16[32,40,128]{2,1,0:T(8,128)(2,1)S(1)}, u32[]{:S(2)}, u32[]{:S(2)}) %collective-permute-start.13) | collective-permute-done | bytes 327712 | tf_op jit(solution)/shard_map/ppermute | solution.py:370
  131.0 7.2 %shard_map.100 = (bf16[144,256]{1,0:T(8,128)(2,1)}, bf16[144,256]{1,0:T(8,128)(2,1)}, bf16[144,256]{1,0:T(8,128)(2,1)}, bf16[144,256]{1,0:T(8,128)(2,1)}) custom-call(s32[3]{0:T(128)} %pad_add_fusion.2.place, f32[2,640,128]{2,1,0:T(8,128)} %copy-done.13, bf16[32,40,128]{2,1,0:T(8,128)(2,1)} %copy-done.16, bf16[32,40,128]{2,1,0:T(8,128)(2,1)} %copy-done.17, ...), custom_call_target="tpu_custom_call" | custom-call | flops 6000000000 | bytes 6000000 | tf_op jit(solution)/shard_map/pallas_call | solution.py:343
  141.3 2.3 %collective-permute-done.14.q1 = bf16[144,256]{1,0:T(8,128)(2,1)S(1)} collective-permute-done((bf16[144,256]{1,0:T(8,128)(2,1)}, bf16[144,256]{1,0:T(8,128)(2,1)S(1)}, u32[]{:S(2)}, u32[]{:S(2)}) %collective-permute-start.14) | collective-permute-done | bytes 73760 | tf_op jit(solution)/shard_map/ppermute | solution.py:366
  143.5 2.2 %collective-permute-done.15.q2 = bf16[144,256]{1,0:T(8,128)(2,1)S(1)} collective-permute-done((bf16[144,256]{1,0:T(8,128)(2,1)}, bf16[144,256]{1,0:T(8,128)(2,1)S(1)}, u32[]{:S(2)}, u32[]{:S(2)}) %collective-permute-start.15) | collective-permute-done | bytes 73760 | tf_op jit(solution)/shard_map/ppermute | solution.py:366
  147.3 1.7 %shard_map.101 = (bf16[256,128]{1,0:T(8,128)(2,1)}, f32[3,256]{1,0:T(4,128)}) custom-call(s32[3]{0:T(128)S(1)} %copy-done.1, bf16[144,256]{1,0:T(8,128)(2,1)S(1)} %copy-done.15, bf16[144,256]{1,0:T(8,128)(2,1)S(1)} %collective-permute-done.14.q1, bf16[144,256]{1,0:T(8,128)(2,1)S(1)} %collective-permute-done.15.q2, ...), custom_call_target="tpu_custom_call" | custom-call | flops 2000000000 | bytes 2000000 | tf_op jit(solution)/shard_map/pallas_call | solution.py:343
  (67 shorter events, 15.6 us)
Async XLA Ops:
  1.5 13.7 %collective-permute-start.2 = (s32[1,512]{1,0:T(1,128)S(1)}, s32[1,512]{1,0:T(1,128)S(1)}, u32[]{:S(2)}, u32[]{:S(2)}) collective-permute-start(s32[1,512]{1,0:T(1,128)S(1)} %add_abs_fusion), channel_id=1, source_target_pairs={{0,192},{64,0},{128,64},{192,128},{1,193},{65,1},{129,65},{193,129... | collective-permute-start | bytes 6152 | tf_op jit(solution)/shard_map/ppermute | solution.py:366
  2.4 12.8 %collective-permute-start.1 = (s32[1,512]{1,0:T(1,128)S(1)}, s32[1,512]{1,0:T(1,128)S(1)}, u32[]{:S(2)}, u32[]{:S(2)}) collective-permute-start(s32[1,512]{1,0:T(1,128)S(1)} %add_abs_fusion), channel_id=1, source_target_pairs={{0,128},{64,192},{128,0},{192,64},{1,129},{65,193},{129,1},{193,65... | collective-permute-start | bytes 6152 | tf_op jit(solution)/shard_map/ppermute | solution.py:366
  5.2 10.0 %collective-permute-start = (s32[1,512]{1,0:T(1,128)S(1)}, s32[1,512]{1,0:T(1,128)S(1)}, u32[]{:S(2)}, u32[]{:S(2)}) collective-permute-start(s32[1,512]{1,0:T(1,128)S(1)} %add_abs_fusion), channel_id=1, source_target_pairs={{0,64},{64,128},{128,192},{192,0},{1,65},{65,129},{129,193},{193,1... | collective-permute-start | bytes 6152 | tf_op jit(solution)/shard_map/ppermute | solution.py:366
  15.1 46.2 %copy-start = (s32[3]{0:T(128)S(1)}, s32[3]{0:T(128)}, u32[]{:S(2)}) copy-start(s32[3]{0:T(128)} %pad_add_fusion.2.place) | copy-start | bytes 40
  15.2 3.4 %collective-permute-start.3 = (bf16[32,40,128]{2,1,0:T(8,128)(2,1)}, bf16[32,40,128]{2,1,0:T(8,128)(2,1)S(1)}, u32[]{:S(2)}, u32[]{:S(2)}) collective-permute-start(bf16[32,40,128]{2,1,0:T(8,128)(2,1)} %get-tuple-element.28), channel_id=1, source_target_pairs={{0,1},{1,0},{2,3},{3,2},{4,5},{5,4},{6,7},{7,6},{8,9},{9,8},{10,11... | collective-permute-start | bytes 983048 | tf_op jit(solution)/shard_map/ppermute | solution.py:370
  15.3 5.2 %collective-permute-start.4 = (s32[4,512]{1,0:T(4,128)S(1)}, s32[4,512]{1,0:T(4,128)S(1)}, u32[]{:S(2)}, u32[]{:S(2)}) collective-permute-start(s32[4,512]{1,0:T(4,128)S(1)} %pad_add_fusion.1), channel_id=1, source_target_pairs={{0,32},{32,0},{1,33},{33,1},{2,34},{34,2},{3,35},{35,3},{4,36},{36... | collective-permute-start | bytes 24584 | tf_op jit(solution)/shard_map/ppermute | solution.py:459
  61.3 1.9 %collective-permute-start.5 = (bf16[32,40,128]{2,1,0:T(8,128)(2,1)S(1)}, bf16[32,40,128]{2,1,0:T(8,128)(2,1)S(1)}, u32[]{:S(2)}, u32[]{:S(2)}) collective-permute-start(bf16[32,40,128]{2,1,0:T(8,128)(2,1)S(1)} %all_to_all.21.mine_ref), channel_id=1, source_target_pairs={{0,1},{1,0},{2,3},{3,2},{4,5},{5,4},{6,7},{7,6},{8,9},{9,8},{10,11... | collective-permute-start | bytes 983048 | tf_op jit(solution)/shard_map/ppermute | solution.py:370
  63.3 13.5 %copy-start.2 = (bf16[2048,128]{1,0:T(8,128)(2,1)S(1)}, bf16[2048,128]{1,0:T(8,128)(2,1)}, u32[]{:S(2)}) copy-start(bf16[2048,128]{1,0:T(8,128)(2,1)} %features_ref.3) | copy-start | bytes 1572868
  63.3 13.5 %copy-start.3 = (bf16[2048,128]{1,0:T(8,128)(2,1)S(1)}, bf16[2048,128]{1,0:T(8,128)(2,1)}, u32[]{:S(2)}) copy-start(bf16[2048,128]{1,0:T(8,128)(2,1)} %upstream_ref.3) | copy-start | bytes 1572868
  63.3 13.5 %copy-start.8 = (bf16[2,128,128]{2,1,0:T(8,128)(2,1)S(1)}, bf16[2,128,128]{2,1,0:T(8,128)(2,1)}, u32[]{:S(2)}) copy-start(bf16[2,128,128]{2,1,0:T(8,128)(2,1)} %outward_ref.3) | copy-start | bytes 196612
  63.3 13.5 %copy-start.9 = (bf16[2,128,128]{2,1,0:T(8,128)(2,1)S(1)}, bf16[2,128,128]{2,1,0:T(8,128)(2,1)}, u32[]{:S(2)}) copy-start(bf16[2,128,128]{2,1,0:T(8,128)(2,1)} %inward_ref.5) | copy-start | bytes 196612
  63.3 13.5 %copy-start.10 = (s32[2048]{0:T(1024)S(1)}, s32[2048]{0:T(1024)}, u32[]{:S(2)}) copy-start(s32[2048]{0:T(1024)} %param.10) | copy-start | bytes 24580
  65.9 6.4 %collective-permute-start.6 = (bf16[256,256]{1,0:T(8,128)(2,1)S(1)}, bf16[256,256]{1,0:T(8,128)(2,1)S(1)}, u32[]{:S(2)}, u32[]{:S(2)}) collective-permute-start(bf16[256,256]{1,0:T(8,128)(2,1)S(1)} %get-tuple-element.33), channel_id=1, source_target_pairs={{0,64},{64,128},{128,192},{192,0},{1,65},{65,129},{129,193},{193,1... | collective-permute-start | bytes 393224 | tf_op jit(solution)/shard_map/ppermute | solution.py:366
  66.8 7.8 %collective-permute-start.7 = (bf16[256,256]{1,0:T(8,128)(2,1)S(1)}, bf16[256,256]{1,0:T(8,128)(2,1)S(1)}, u32[]{:S(2)}, u32[]{:S(2)}) collective-permute-start(bf16[256,256]{1,0:T(8,128)(2,1)S(1)} %get-tuple-element.34), channel_id=1, source_target_pairs={{0,128},{64,192},{128,0},{192,64},{1,129},{65,193},{129,1},{193,65... | collective-permute-start | bytes 393224 | tf_op jit(solution)/shard_map/ppermute | solution.py:366
  68.2 8.6 %collective-permute-start.8 = (bf16[256,256]{1,0:T(8,128)(2,1)S(1)}, bf16[256,256]{1,0:T(8,128)(2,1)S(1)}, u32[]{:S(2)}, u32[]{:S(2)}) collective-permute-start(bf16[256,256]{1,0:T(8,128)(2,1)S(1)} %get-tuple-element.35), channel_id=1, source_target_pairs={{0,192},{64,0},{128,64},{192,128},{1,193},{65,1},{129,65},{193,129... | collective-permute-start | bytes 393224 | tf_op jit(solution)/shard_map/ppermute | solution.py:366
  78.1 6.4 %collective-permute-start.11 = (bf16[256,256]{1,0:T(8,128)(2,1)S(1)}, bf16[256,256]{1,0:T(8,128)(2,1)S(1)}, u32[]{:S(2)}, u32[]{:S(2)}) collective-permute-start(bf16[256,256]{1,0:T(8,128)(2,1)S(1)} %get-tuple-element.36.v0), channel_id=1, source_target_pairs={{0,64},{64,128},{128,192},{192,0},{1,65},{65,129},{129,193},{193,1... | collective-permute-start | bytes 393224 | tf_op jit(solution)/shard_map/ppermute | solution.py:366
  78.7 7.7 %collective-permute-start.10 = (bf16[256,256]{1,0:T(8,128)(2,1)S(1)}, bf16[256,256]{1,0:T(8,128)(2,1)S(1)}, u32[]{:S(2)}, u32[]{:S(2)}) collective-permute-start(bf16[256,256]{1,0:T(8,128)(2,1)S(1)} %get-tuple-element.36.v0), channel_id=1, source_target_pairs={{0,128},{64,192},{128,0},{192,64},{1,129},{65,193},{129,1},{193,65... | collective-permute-start | bytes 393224 | tf_op jit(solution)/shard_map/ppermute | solution.py:366
  80.4 7.8 %collective-permute-start.9 = (bf16[256,256]{1,0:T(8,128)(2,1)S(1)}, bf16[256,256]{1,0:T(8,128)(2,1)S(1)}, u32[]{:S(2)}, u32[]{:S(2)}) collective-permute-start(bf16[256,256]{1,0:T(8,128)(2,1)S(1)} %get-tuple-element.36.v0), channel_id=1, source_target_pairs={{0,192},{64,0},{128,64},{192,128},{1,193},{65,1},{129,65},{193,129... | collective-permute-start | bytes 393224 | tf_op jit(solution)/shard_map/ppermute | solution.py:366
  90.4 1.7 %collective-permute-start.12 = (bf16[32,40,128]{2,1,0:T(8,128)(2,1)S(1)}, bf16[32,40,128]{2,1,0:T(8,128)(2,1)S(1)}, u32[]{:S(2)}, u32[]{:S(2)}) collective-permute-start(bf16[32,40,128]{2,1,0:T(8,128)(2,1)S(1)} %get-tuple-element.38), channel_id=1, source_target_pairs={{0,1},{1,0},{2,3},{3,2},{4,5},{5,4},{6,7},{7,6},{8,9},{9,8},{10,11... | collective-permute-start | bytes 983048 | tf_op jit(solution)/shard_map/ppermute | solution.py:370
  128.6 1.6 %collective-permute-start.13 = (bf16[32,40,128]{2,1,0:T(8,128)(2,1)S(1)}, bf16[32,40,128]{2,1,0:T(8,128)(2,1)S(1)}, u32[]{:S(2)}, u32[]{:S(2)}) collective-permute-start(bf16[32,40,128]{2,1,0:T(8,128)(2,1)S(1)} %all_to_all.23.mine_ref), channel_id=1, source_target_pairs={{0,1},{1,0},{2,3},{3,2},{4,5},{5,4},{6,7},{7,6},{8,9},{9,8},{10,11... | collective-permute-start | bytes 983048 | tf_op jit(solution)/shard_map/ppermute | solution.py:370
  131.0 15.5 %copy-start.1 = (s32[3]{0:T(128)S(1)}, s32[3]{0:T(128)}, u32[]{:S(2)}) copy-start(s32[3]{0:T(128)} %pad_add_fusion.2.place) | copy-start | bytes 40
  138.2 5.3 %collective-permute-start.14 = (bf16[144,256]{1,0:T(8,128)(2,1)}, bf16[144,256]{1,0:T(8,128)(2,1)S(1)}, u32[]{:S(2)}, u32[]{:S(2)}) collective-permute-start(bf16[144,256]{1,0:T(8,128)(2,1)} %get-tuple-element.42), channel_id=1, source_target_pairs={{0,64},{64,128},{128,192},{192,0},{1,65},{65,129},{129,193},{193,1... | collective-permute-start | bytes 221192 | tf_op jit(solution)/shard_map/ppermute | solution.py:366
  139.1 6.6 %collective-permute-start.15 = (bf16[144,256]{1,0:T(8,128)(2,1)}, bf16[144,256]{1,0:T(8,128)(2,1)S(1)}, u32[]{:S(2)}, u32[]{:S(2)}) collective-permute-start(bf16[144,256]{1,0:T(8,128)(2,1)} %get-tuple-element.43), channel_id=1, source_target_pairs={{0,128},{64,192},{128,0},{192,64},{1,129},{65,193},{129,1},{193,65... | collective-permute-start | bytes 221192 | tf_op jit(solution)/shard_map/ppermute | solution.py:366
  140.4 6.1 %collective-permute-start.16 = (bf16[144,256]{1,0:T(8,128)(2,1)}, bf16[144,256]{1,0:T(8,128)(2,1)S(1)}, u32[]{:S(2)}, u32[]{:S(2)}) collective-permute-start(bf16[144,256]{1,0:T(8,128)(2,1)} %get-tuple-element.44), channel_id=1, source_target_pairs={{0,192},{64,0},{128,64},{192,128},{1,193},{65,1},{129,65},{193,129... | collective-permute-start | bytes 221192 | tf_op jit(solution)/shard_map/ppermute | solution.py:366
  (11 other events, 57.8 us)

commit v3 on v2

v3 whole, which is shorter than its diff:
```python
import functools
import math

import jax
import jax.numpy as jnp
from jax import lax
from jax.experimental import pallas as pl
from jax.experimental.pallas import tpu as pltpu
from jax.sharding import Mesh
from jax.sharding import PartitionSpec as P

BOX_LENGTH = 100.0
GAUSSIAN_SIGMAS = (200.0, 100.0)
REACH = 8
SPAN = 2 * REACH + 1
CLASSES = (SPAN**3 + 1) // 2
SLABS = 4
SLAB = 640
TABLE = 2 * SLAB
BLOCK = 256
CHANNELS = 128
ROWS = 40
PIECES = 32
VMEM_LIMIT = 24 * 1024 * 1024
BF16 = jnp.bfloat16
F32 = jnp.float32

COS_SERIES = (
    0.999999660315462,
    -19.739032161520388,
    64.93001235415629,
    -85.28515888817482,
    58.84788533073816,
    -21.15810679384873,
)
SIN_SERIES = (
    6.283183359037432,
    -41.341456424111435,
    81.59687947501621,
    -76.58597187733577,
    41.22756686823296,
    -12.302134397179453,
)


def class_vectors(first_class, shape, axis):
    label = (lax.broadcasted_iota(jnp.int32, shape, axis) + first_class).astype(F32)
    square = SPAN * SPAN
    first = jnp.floor((label + (square // 2 + 0.5)) * (1.0 / square))
    rest = label - square * first
    second = jnp.floor((rest + (REACH + 0.5)) * (1.0 / SPAN))
    return first, second, rest - SPAN * second


def matmul(left, right, left_dim, right_dim):
    return lax.dot_general(
        left, right, (((left_dim,), (right_dim,)), ((), ())), preferred_element_type=F32
    )


def flip(matrix):
    return jnp.transpose(matrix.astype(F32)).astype(BF16)


def gain_columns(multiplier, labels):
    species_count, channels = multiplier.shape
    padding = jnp.zeros((8 - species_count, channels), F32)
    columns = jnp.transpose(jnp.concatenate([multiplier, padding], axis=0))
    result = jnp.zeros((channels, labels.shape[1]), F32)
    for species in range(species_count):
        result = jnp.where(labels == species, columns[:, species : species + 1], result)
    return result


def series(coefficients, square):
    result = coefficients[-1] * square + coefficients[-2]
    for coefficient in coefficients[-3::-1]:
        result = result * square + coefficient
    return result


def write_pieces(place, total_ref, keep_ref, send_ref):
    core = place[2]
    for target, half in ((keep_ref, core), (send_ref, 1 - core)):
        for index in range(PIECES):
            row, side = index // 2, index % 2
            start = pl.multiple_of(half * SLAB + row * ROWS, 8)
            target[index] = total_ref[
                pl.ds(start, ROWS), side * CHANNELS : (side + 1) * CHANNELS
            ].astype(BF16)


def read_pieces(place, mine_ref, other_ref, total_ref):
    core = place[2]
    for source, half in ((mine_ref, core), (other_ref, 1 - core)):
        for index in range(PIECES):
            row, side = index // 2, index % 2
            start = pl.multiple_of(half * SLAB + row * ROWS, 8)
            total_ref[pl.ds(start, ROWS), side * CHANNELS : (side + 1) * CHANNELS] = source[
                index
            ].astype(F32)


def slot(index):
    return slice(index * BLOCK, (index + 1) * BLOCK)


def tables_kernel(
    place,
    coordinates_hbm,
    labels_hbm,
    features_hbm,
    upstream_hbm,
    inward_hbm,
    outward_hbm,
    multiplier_hbm,
    table_ref,
    values_ref,
    keep_ref,
    send_ref,
    coordinates_ref,
    labels_ref,
    features_ref,
    upstream_ref,
    inward_ref,
    outward_ref,
    multiplier_ref,
    total_ref,
    arrivals,
):
    copies = [
        pltpu.make_async_copy(source, target, arrivals.at[index])
        for index, (source, target) in enumerate(
            (
                (coordinates_hbm, coordinates_ref),
                (labels_hbm, labels_ref),
                (features_hbm.at[:, place[1]], features_ref),
                (upstream_hbm.at[:, place[1]], upstream_ref),
                (inward_hbm, inward_ref),
                (outward_hbm, outward_ref),
                (multiplier_hbm, multiplier_ref),
            )
        )
    ]
    for copy in copies:
        copy.start()
    copies[0].wait()
    blocks = [lax.rem(place[0] + index, SLABS) for index in range(SLABS)]
    sides = [
        pl.ds(pl.multiple_of((2 * block + place[1]) * BLOCK + side * CHANNELS, CHANNELS), CHANNELS)
        for block in blocks
        for side in range(BLOCK // CHANNELS)
    ]
    chunk = 64
    for start in range(0, SLAB, chunk):
        vectors = class_vectors(place[0] * SLAB + start, (chunk, CHANNELS), 0)
        for index, side in enumerate(sides):
            columns = slice(index * CHANNELS, (index + 1) * CHANNELS)
            turns = vectors[0] * coordinates_ref[0:1, side]
            turns += vectors[1] * coordinates_ref[1:2, side]
            turns += vectors[2] * coordinates_ref[2:3, side]
            turns -= jnp.floor(turns + 0.5)
            square = turns * turns
            table_ref[start : start + chunk, columns] = series(COS_SERIES, square).astype(BF16)
            table_ref[SLAB + start : SLAB + start + chunk, columns] = (
                turns * series(SIN_SERIES, square)
            ).astype(BF16)
    for copy in copies[1:]:
        copy.wait()
    inward = flip(inward_ref[0])
    for index, block in enumerate(blocks):
        labels = labels_ref[:, pl.ds(pl.multiple_of((2 * block + place[1]) * BLOCK, BLOCK), BLOCK)]
        gains = gain_columns(multiplier_ref[:, 0, :], labels)
        charges = matmul(inward, features_ref[block], 1, 1) * gains
        grad_pot = matmul(outward_ref[1], upstream_ref[block], 1, 1)
        values_ref[:CHANNELS, slot(index)] = charges.astype(BF16)
        values_ref[CHANNELS:, slot(index)] = grad_pot.astype(BF16)
    total_ref[...] = matmul(table_ref[...], values_ref[...], 1, 1)
    write_pieces(place, total_ref, keep_ref, send_ref)


def weights_kernel(prefactor, place, classes_ref, weights_ref):
    chunk = 128
    for start in range(0, SLAB, chunk):
        rows = pl.ds(start, chunk)
        own = lax.broadcasted_iota(jnp.int32, (chunk, CHANNELS), 0) + (place[0] * SLAB + start)
        count = jnp.zeros((chunk, CHANNELS), F32)
        for group in range(classes_ref.shape[0]):
            for offset in range(0, classes_ref.shape[1], CHANNELS):
                classes = classes_ref[group : group + 1, offset : offset + CHANNELS]
                count += jnp.where(classes == own, 1.0, 0.0)
        count = jnp.sum(count, axis=1, keepdims=True)
        vectors = class_vectors(place[0] * SLAB + start, (chunk, CHANNELS), 0)
        norm = vectors[0] * vectors[0] + vectors[1] * vectors[1] + vectors[2] * vectors[2]
        for block, spread in enumerate(GAUSSIAN_SIGMAS):
            weights_ref[block, rows, :] = count * (prefactor * jnp.exp(norm * (-1.0 / spread)))


def weigh(total_ref, weights_ref, first):
    for half in range(2):
        rows = pl.ds(half * SLAB, SLAB)
        for side in range(2):
            columns = pl.ds(side * CHANNELS, CHANNELS)
            total_ref[rows, columns] = total_ref[rows, columns] * weights_ref[(first + side) % 2]


def potential_kernel(
    place, weights_ref, mine_ref, other_ref, table_ref, fields_ref, p0, p1, p2, p3, total_ref
):
    read_pieces(place, mine_ref, other_ref, total_ref)
    weigh(total_ref, weights_ref, 0)
    fields_ref[...] = total_ref[...].astype(BF16)
    flipped = jnp.transpose(total_ref[...]).astype(BF16)
    for index, target in enumerate((p0, p1, p2, p3)):
        target[...] = matmul(flipped, table_ref[:, slot(index)], 1, 0).astype(BF16)


def middle_kernel(
    place,
    q0,
    q1,
    q2,
    q3,
    labels_ref,
    features_ref,
    upstream_ref,
    inward_ref,
    outward_ref,
    multiplier_ref,
    values_ref,
    hidden_grad_ref,
):
    total = (q0[...].astype(F32) + q1[...].astype(F32)) + (q2[...].astype(F32) + q3[...].astype(F32))
    potential = total[:CHANNELS].astype(BF16)
    grad_charge = total[CHANNELS:]
    gains = gain_columns(multiplier_ref[:, 1, :], labels_ref[...])
    hidden = (
        features_ref[...].astype(F32)
        + matmul(jnp.transpose(potential.astype(F32)).astype(BF16), outward_ref[0], 1, 0)
    ).astype(BF16)
    inward_flipped = flip(inward_ref[1])
    charges = matmul(inward_flipped, hidden, 1, 1) * gains
    scaled = jnp.transpose(grad_charge * gains).astype(BF16)
    hidden_grad = (
        upstream_ref[...].astype(F32) + matmul(scaled, inward_flipped, 1, 0)
    ).astype(BF16)
    hidden_grad_ref[...] = hidden_grad
    grad_pot = matmul(outward_ref[0], hidden_grad, 1, 1)
    values_ref[...] = jnp.concatenate([charges, grad_pot], axis=0).astype(BF16)


def second_kernel(place, table_ref, v0, v1, v2, v3, values_ref, keep_ref, send_ref, total_ref):
    for index, source in enumerate((v0, v1, v2, v3)):
        values_ref[:, slot(index)] = source[...]
    total_ref[...] = matmul(table_ref[...], values_ref[...], 1, 1)
    write_pieces(place, total_ref, keep_ref, send_ref)


def gradient_kernel(
    place,
    weights_ref,
    mine_ref,
    other_ref,
    table_ref,
    fields_hbm,
    first_hbm,
    second_hbm,
    o0,
    o1,
    o2,
    o3,
    total_ref,
    pairs_ref,
    values_ref,
    theta_ref,
    fields_ref,
    arrivals,
):
    copies = [
        pltpu.make_async_copy(source, target, arrivals.at[index])
        for index, (source, target) in enumerate(
            (
                (fields_hbm, fields_ref),
                (first_hbm, values_ref.at[:BLOCK]),
                (second_hbm, values_ref.at[BLOCK:]),
            )
        )
    ]
    for copy in copies:
        copy.start()
    read_pieces(place, mine_ref, other_ref, total_ref)
    weigh(total_ref, weights_ref, 1)
    grad_one = total_ref[:, CHANNELS:]
    pairs_ref[:, 0:CHANNELS] = grad_one.astype(BF16)
    pairs_ref[:, CHANNELS : 2 * CHANNELS] = total_ref[:, :CHANNELS].astype(BF16)
    flipped = jnp.transpose(grad_one).astype(BF16)
    vectors = class_vectors(place[0] * SLAB, (16, SLAB), 1)
    row = lax.broadcasted_iota(jnp.int32, (16, SLAB), 0)
    directions = jnp.where(row == 0, vectors[0], jnp.where(row == 1, vectors[1], vectors[2]))
    directions = jnp.where(row < 3, directions, 0.0).astype(BF16)
    for copy in copies:
        copy.wait()
    pairs_ref[:, 2 * CHANNELS : 3 * CHANNELS] = fields_ref[:, CHANNELS:]
    pairs_ref[:, 3 * CHANNELS :] = fields_ref[:, :CHANNELS]
    for index, target in enumerate((o0, o1, o2, o3)):
        columns = slot(index)
        along_real = matmul(pairs_ref[:SLAB], values_ref[:, columns], 1, 0)
        along_imag = matmul(pairs_ref[SLAB:], values_ref[:, columns], 1, 0)
        theta_ref[:, columns] = (
            table_ref[:SLAB, columns].astype(F32) * along_imag
            - table_ref[SLAB:, columns].astype(F32) * along_real
        ).astype(BF16)
        charge = matmul(flipped, table_ref[:, columns], 1, 0)
        position = matmul(directions, theta_ref[:, columns], 1, 0)
        target[:CHANNELS] = charge.astype(BF16)
        target[CHANNELS:] = (position * (2.0 * math.pi / BOX_LENGTH)).astype(BF16)


def final_kernel(
    place, q0, q1, q2, q3, labels_ref, hidden_grad_ref, inward_ref, multiplier_ref, features_ref, positions_ref
):
    total = (q0[...].astype(F32) + q1[...].astype(F32)) + (q2[...].astype(F32) + q3[...].astype(F32))
    gains = gain_columns(multiplier_ref[:, 0, :], labels_ref[...])
    scaled = jnp.transpose(total[:CHANNELS] * gains).astype(BF16)
    features_ref[...] = (
        hidden_grad_ref[...].astype(F32) + matmul(scaled, flip(inward_ref[0]), 1, 0)
    ).astype(BF16)
    positions_ref[...] = total[CHANNELS : CHANNELS + 3]


def shape_of(shape, dtype):
    return jax.ShapeDtypeStruct(shape, dtype)


def far(value):
    return pltpu.with_memory_space_constraint(value, pltpu.HBM)


def near(value):
    return pltpu.with_memory_space_constraint(value, pltpu.VMEM)


def whole(shape):
    return pl.BlockSpec(shape, lambda step, place: (0,) * len(shape))


def compiler(micros):
    return dict(
        compiler_params=pltpu.CompilerParams(vmem_limit_bytes=VMEM_LIMIT),
        cost_estimate=pl.CostEstimate(
            flops=micros * 10**9, bytes_accessed=micros * 10**6, transcendentals=0
        ),
    )


def call(kernel, in_specs, outs, out_specs, operands, micros=2):
    return pl.pallas_call(
        kernel,
        grid_spec=pltpu.PrefetchScalarGridSpec(
            num_scalar_prefetch=1, grid=(1,), in_specs=in_specs, out_specs=out_specs
        ),
        out_shape=outs,
        **compiler(micros),
    )(*operands)


def call_whole(kernel, outs, scratch, place, operands, spaces=None, micros=2):
    spaces = spaces or [pltpu.VMEM] * len(operands)
    return pl.pallas_call(
        kernel,
        in_specs=[pl.BlockSpec(memory_space=pltpu.SMEM)]
        + [pl.BlockSpec(memory_space=space) for space in spaces],
        out_specs=[pl.BlockSpec(memory_space=pltpu.VMEM)] * len(outs),
        out_shape=outs,
        scratch_shapes=scratch,
        **compiler(micros),
    )(place, *operands)


ATOM_REST = ("yh", "yl", "z")


def shifted(value, shift):
    return lax.ppermute(value, "x", [(i, (i + shift) % SLABS) for i in range(SLABS)])


def swapped(value):
    return lax.ppermute(value, "core", [(0, 1), (1, 0)])


def add_halves(keep, send):
    return (keep.astype(F32) + swapped(send).astype(F32)).astype(BF16)


def sum_fields(part):
    parts = lax.all_to_all(part, ATOM_REST, 0, 0, tiled=True)
    total = jnp.sum(parts.astype(F32), axis=0).astype(BF16)
    spread = jnp.broadcast_to(total[None], (PIECES,) + total.shape)
    mine = lax.all_to_all(spread, ATOM_REST, 0, 0, tiled=True)
    return mine, swapped(mine)


def per_device(
    atomic_descriptors,
    unit_cell_coordinates,
    element_labels,
    lattice_momenta,
    feature_to_latent_matrix,
    latent_to_feature_matrix,
    element_latent_multiplier,
    upstream_gradient,
):
    place = jnp.stack(
        [lax.axis_index("x"), lax.axis_index("yh"), lax.axis_index("core")]
    ).astype(jnp.int32)
    prefactor = 1.0 / math.sqrt(
        atomic_descriptors.shape[0]
        * lattice_momenta.shape[1]
        * lax.axis_size(("x", "yh", "yl", "z", "core"))
    )
    labels = element_labels[None, :]
    multiplier = jnp.swapaxes(element_latent_multiplier, 0, 1)
    signed = (
        lattice_momenta[0] * (SPAN * SPAN) + lattice_momenta[1] * SPAN + lattice_momenta[2]
    )
    own = jnp.abs(signed)[None]
    row = jnp.concatenate([own] + [shifted(own, shift) for shift in range(1, SLABS)], axis=0)

    matrices = whole((2, CHANNELS, CHANNELS))
    gains_spec = whole(multiplier.shape)
    pieces_shape = shape_of((PIECES, ROWS, CHANNELS), BF16)
    values_block = whole((BLOCK, BLOCK))
    values_shape = shape_of((BLOCK, BLOCK), BF16)
    atoms_here = SLABS * BLOCK

    blocked = (SLABS, 2, BLOCK, CHANNELS)
    operands = [
        unit_cell_coordinates,
        labels,
        atomic_descriptors.reshape(blocked),
        upstream_gradient.reshape(blocked),
        feature_to_latent_matrix,
        latent_to_feature_matrix,
        multiplier,
    ]
    local = [shape_of(value.shape, value.dtype) for value in operands]
    local[2] = local[3] = shape_of((SLABS, BLOCK, CHANNELS), BF16)
    table, values_one, keep, send = call_whole(
        tables_kernel,
        (
            pltpu.VMEM((TABLE, atoms_here), BF16),
            shape_of((BLOCK, atoms_here), BF16),
            pieces_shape,
            pieces_shape,
        ),
        [pltpu.VMEM(value.shape, value.dtype) for value in local]
        + [pltpu.VMEM((TABLE, BLOCK), F32), pltpu.SemaphoreType.DMA((len(operands),))],
        place,
        [far(value) for value in operands],
        spaces=[pltpu.HBM] * len(operands),
        micros=7,
    )
    keep, send, row = lax.optimization_barrier((keep, send, row))
    part = add_halves(keep, send)
    other_row = lax.ppermute(row, "yh", [(0, 1), (1, 0)])
    part, other_row = lax.optimization_barrier((part, other_row))
    classes = jnp.concatenate([row, other_row], axis=0)
    (weights,) = call_whole(
        functools.partial(weights_kernel, prefactor),
        [shape_of((2, SLAB, CHANNELS), F32)],
        [],
        place,
        [classes],
    )
    mine, other = sum_fields(part)
    fields, *products = call_whole(
        potential_kernel,
        [shape_of((TABLE, BLOCK), BF16)] + [values_shape] * SLABS,
        [pltpu.VMEM((TABLE, BLOCK), F32)],
        place,
        [weights, mine, other, near(table)],
    )
    arrived = [products[0]] + [shifted(products[shift], shift) for shift in range(1, SLABS)]
    own_atoms = pl.BlockSpec((BLOCK, CHANNELS), lambda step, place: (2 * place[0] + place[1], 0))
    own_labels = pl.BlockSpec((1, BLOCK), lambda step, place: (0, 2 * place[0] + place[1]))
    values_own, hidden_grad = call(
        middle_kernel,
        [values_block] * SLABS
        + [own_labels, own_atoms, own_atoms, matrices, matrices, gains_spec],
        (values_shape, shape_of((BLOCK, CHANNELS), BF16)),
        (values_block, whole((BLOCK, CHANNELS))),
        (
            place,
            *arrived,
            labels,
            atomic_descriptors,
            upstream_gradient,
            feature_to_latent_matrix,
            latent_to_feature_matrix,
            multiplier,
        ),
    )
    seconds = [values_own] + [shifted(values_own, SLABS - other) for other in range(1, SLABS)]
    values_two, keep, send = call_whole(
        second_kernel,
        [shape_of((BLOCK, atoms_here), BF16), pieces_shape, pieces_shape],
        [pltpu.VMEM((TABLE, BLOCK), F32)],
        place,
        [near(table), *seconds],
    )
    mine, other = sum_fields(add_halves(keep, send))
    result_shape = shape_of((CHANNELS + 16, BLOCK), BF16)
    result_spec = whole((CHANNELS + 16, BLOCK))
    results = call_whole(
        gradient_kernel,
        [result_shape] * SLABS,
        [
            pltpu.VMEM((TABLE, BLOCK), F32),
            pltpu.VMEM((TABLE, 2 * BLOCK), BF16),
            pltpu.VMEM((2 * BLOCK, atoms_here), BF16),
            pltpu.VMEM((SLAB, atoms_here), BF16),
            pltpu.VMEM((TABLE, BLOCK), BF16),
            pltpu.SemaphoreType.DMA((3,)),
        ],
        place,
        [weights, mine, other, near(table), far(fields), far(values_one), far(values_two)],
        spaces=[pltpu.VMEM] * 4 + [pltpu.HBM] * 3,
        micros=5,
    )
    arrived = [results[0]] + [shifted(results[shift], shift) for shift in range(1, SLABS)]
    return call(
        final_kernel,
        [result_spec] * SLABS
        + [own_labels, whole((BLOCK, CHANNELS)), matrices, gains_spec],
        (shape_of((BLOCK, CHANNELS), BF16), shape_of((3, BLOCK), F32)),
        (whole((BLOCK, CHANNELS)), whole((3, BLOCK))),
        (place, *arrived, labels, hidden_grad, feature_to_latent_matrix, multiplier),
    )


def solution(mesh):
    fine = Mesh(mesh.devices.reshape(SLABS, 2, 2, -1, 2), ("x", "yh", "yl", "z", "core"))
    atom, group = ("yl", "z", "core"), ("x", "yh")
    in_specs = (
        P(atom, None),
        P(None, atom),
        P(atom),
        P(None, group),
        P(),
        P(),
        P(),
        P(atom, None),
    )
    out_specs = (P(atom + group, None), P(None, atom + group))
    return jax.shard_map(
        per_device, mesh=fine, in_specs=in_specs, out_specs=out_specs, check_vma=False
    )
```

time: 150 us -> 141 us (0.940)
  Pallas kernels: 25.7 us -> 18 us
  local copies, waits for them, and re-layouts: 1.79 us -> 0.14 us
    pallas_call x7 -> x2, Pallas kernels: 25.7 us -> 2.93 us  [call(): pl.pallas_call(kernel, grid_spec=pltpu.PrefetchScalarGridSpec(num_scalar_...]
    pallas_call x0 -> x5, Pallas kernels: none -> 15.1 us  [call_whole(): pl.pallas_call(kernel, in_specs=[pl.BlockSpec(memory_space=pltpu.SMEM)] +...]
    unnamed x36 -> x18, local copies, waits for them, and re-layouts: 1.7 us -> 0.05 us
  transfers between devices with their start and end apart: 17 -> 17, of which waited for: 12 -> 12; matrix products, arithmetic and copies ran while one was open for 1% -> 0% of each run, Pallas kernels for 7% -> 6%
where the time goes in v3:
time: 141 us; the launch traced here: 140 us
  blocking collectives  77 us (55%)
  waiting for transfers between devices  24.4 us (17%)
  Pallas kernels  18 us (13%)
  starting transfers between devices  17.6 us (12%)
  other arithmetic  2.19 us (2%)
    all_to_all x2, blocking collectives, sum_fields(): parts = lax.all_to_all(part, ATOM_REST, 0, 0, tiled=True)  42.6 us
    all_to_all x2, blocking collectives, sum_fields(): mine = lax.all_to_all(spread, ATOM_REST, 0, 0, tiled=True)  34.5 us
    ppermute x12, waiting for transfers between devices, shifted(): lax.ppermute(value, 'x', [(i, (i + shift) % SLABS) for i in range(SLABS)])  19.3 us
    pallas_call x5, Pallas kernels, call_whole(): pl.pallas_call(kernel, in_specs=[pl.BlockSpec(memory_space=pltpu.SMEM)] +...  15.1 us
    ppermute x12, starting transfers between devices, shifted(): lax.ppermute(value, 'x', [(i, (i + shift) % SLABS) for i in range(SLABS)])  14.1 us
    ppermute x1, starting transfers between devices, per_device(): other_row = lax.ppermute(row, 'yh', [(0, 1), (1, 0)])  3.28 us
    ppermute x4, waiting for transfers between devices, swapped(): return lax.ppermute(value, 'core', [(0, 1), (1, 0)])  3.25 us
    pallas_call x2, Pallas kernels, call(): pl.pallas_call(kernel, grid_spec=pltpu.PrefetchScalarGridSpec(num_scalar_...  2.93 us
  transfers between devices with their start and end apart: 17, of which 12 were waited for; matrix products, arithmetic and copies ran while one was open for 0% of the time, Pallas kernels for 6%

profile of v3, /device:TPU:6, one launch (start us, length us, event | category | flops | bytes accessed | tf_op | source)
XLA Modules:
  0.0 140.2 jit_solution(12127072171089704568)
XLA Ops:
  2.4 2.8 %collective-permute-start.1 = (s32[1,512]{1,0:T(1,128)S(1)}, s32[1,512]{1,0:T(1,128)S(1)}, u32[]{:S(2)}, u32[]{:S(2)}) collective-permute-start(s32[1,512]{1,0:T(1,128)S(1)} %add_abs_fusion), channel_id=1, source_target_pairs={{0,128},{64,192},{128,0},{192,64},{1,129},{65,193},{129,1},{193,65... | collective-permute-start | bytes 6152 | tf_op jit(solution)/shard_map/ppermute | solution.py:384
  5.6 5.8 %shard_map.95 = (bf16[1280,1024]{1,0:T(8,128)(2,1)S(1)}, bf16[256,1024]{1,0:T(8,128)(2,1)S(1)}, bf16[32,40,128]{2,1,0:T(8,128)(2,1)S(1)}, bf16[32,40,128]{2,1,0:T(8,128)(2,1)S(1)}) custom-call(s32[3]{0:T(128)S(1)} %pad_add_fusion.2.place, f32[3,2048]{1,0:T(4,128)} %coordinates_hbm.1, s32[1,2048]{1,0:T(1,128)} %bitcast.9, bf16[4,2,256,128]{3,2,1,0:T(8,128)(2,1)} %bitcast.7, ...), custom_call_target="tpu_custom_call" | custom-call | flops 7000000000 | bytes 7000000 | tf_op jit(solution)/shard_map/pallas_call | solution.py:369
  11.7 3.3 %collective-permute-start.4 = (s32[4,512]{1,0:T(4,128)S(1)}, s32[4,512]{1,0:T(4,128)S(1)}, u32[]{:S(2)}, u32[]{:S(2)}) collective-permute-start(s32[4,512]{1,0:T(4,128)S(1)} %pad_add_fusion.1), channel_id=1, source_target_pairs={{0,32},{32,0},{1,33},{33,1},{2,34},{34,2},{3,35},{35,3},{4,36},{36... | collective-permute-start | bytes 24584 | tf_op jit(solution)/shard_map/ppermute | solution.py:465
  15.1 1.9 %collective-permute-done.4 = s32[4,512]{1,0:T(4,128)S(1)} collective-permute-done((s32[4,512]{1,0:T(4,128)S(1)}, s32[4,512]{1,0:T(4,128)S(1)}, u32[]{:S(2)}, u32[]{:S(2)}) %collective-permute-start.4) | collective-permute-done | bytes 8224 | tf_op jit(solution)/shard_map/ppermute | solution.py:465
  16.9 24.1 %all_to_all.20 = bf16[32,40,128]{2,1,0:T(8,128)(2,1)S(1)} all-to-all(bf16[32,40,128]{2,1,0:T(8,128)(2,1)S(1)} %add_convert_fusion.1), channel_id=1, replica_groups=mesh['x'=4,'yh'=2,'yl'=2,'z'=8,'core'=2] {'yh','yl','z'}, dimensions={0} | all-to-all | bytes 655360 | tf_op jit(solution)/shard_map/all_to_all | solution.py:396
  41.1 16.6 %all_to_all.21.mine_ref = bf16[32,40,128]{2,1,0:T(8,128)(2,1)S(1)} all-to-all(bf16[32,40,128]{2,1,0:T(8,128)(2,1)S(1)} %broadcast_in_dim.7), channel_id=1, replica_groups=mesh['x'=4,'yh'=2,'yl'=2,'z'=8,'core'=2] {'yh','yl','z'}, dimensions={0} | all-to-all | bytes 655360 | tf_op jit(solution)/shard_map/all_to_all | solution.py:399
  57.7 1.9 %shard_map.96.weights_ref = f32[2,640,128]{2,1,0:T(8,128)S(1)} custom-call(s32[3]{0:T(128)S(1)} %pad_add_fusion.2.place, s32[8,512]{1,0:T(8,128)S(1)} %pad_add_fusion.classes_ref), custom_call_target="tpu_custom_call" | custom-call | flops 2000000000 | bytes 2000000 | tf_op jit(solution)/shard_map/pallas_call | solution.py:369
  59.7 1.6 %shard_map.97 = (bf16[1280,256]{1,0:T(8,128)(2,1)S(1)}, bf16[256,256]{1,0:T(8,128)(2,1)S(1)}, bf16[256,256]{1,0:T(8,128)(2,1)S(1)}, bf16[256,256]{1,0:T(8,128)(2,1)S(1)}, bf16[256,256]{1,0:T(8,128)(2,1)S(1)}) custom-call(s32[3]{0:T(128)S(1)} %pad_add_fusion.2.place, f32[2,640,128]{2,1,0:T(8,128)S(1)} %shard_map.96.weights_ref, ...), custom_call_target="tpu_custom_call" | custom-call | flops 2000000000 | bytes 2000000 | tf_op jit(solution)/shard_map/pallas_call | solution.py:369
  65.1 2.8 %collective-permute-done.6.q1 = bf16[256,256]{1,0:T(8,128)(2,1)S(1)} collective-permute-done((bf16[256,256]{1,0:T(8,128)(2,1)S(1)}, bf16[256,256]{1,0:T(8,128)(2,1)S(1)}, u32[]{:S(2)}, u32[]{:S(2)}) %collective-permute-start.6) | collective-permute-done | bytes 131104 | tf_op jit(solution)/shard_map/ppermute | solution.py:384
  67.8 2.4 %collective-permute-done.7.q2 = bf16[256,256]{1,0:T(8,128)(2,1)S(1)} collective-permute-done((bf16[256,256]{1,0:T(8,128)(2,1)S(1)}, bf16[256,256]{1,0:T(8,128)(2,1)S(1)}, u32[]{:S(2)}, u32[]{:S(2)}) %collective-permute-start.7) | collective-permute-done | bytes 131104 | tf_op jit(solution)/shard_map/ppermute | solution.py:384
  70.3 2.1 %collective-permute-done.8.q3 = bf16[256,256]{1,0:T(8,128)(2,1)S(1)} collective-permute-done((bf16[256,256]{1,0:T(8,128)(2,1)S(1)}, bf16[256,256]{1,0:T(8,128)(2,1)S(1)}, u32[]{:S(2)}, u32[]{:S(2)}) %collective-permute-start.8) | collective-permute-done | bytes 131104 | tf_op jit(solution)/shard_map/ppermute | solution.py:384
  74.3 1.7 %collective-permute-start.10 = (bf16[256,256]{1,0:T(8,128)(2,1)S(1)}, bf16[256,256]{1,0:T(8,128)(2,1)S(1)}, u32[]{:S(2)}, u32[]{:S(2)}) collective-permute-start(bf16[256,256]{1,0:T(8,128)(2,1)S(1)} %get-tuple-element.37.v0), channel_id=1, source_target_pairs={{0,128},{64,192},{128,0},{192,64},{1,129},{65,193},{129,1},{193,65... | collective-permute-start | bytes 393224 | tf_op jit(solution)/shard_map/ppermute | solution.py:384
  76.8 3.3 %collective-permute-done.11.v3 = bf16[256,256]{1,0:T(8,128)(2,1)S(1)} collective-permute-done((bf16[256,256]{1,0:T(8,128)(2,1)S(1)}, bf16[256,256]{1,0:T(8,128)(2,1)S(1)}, u32[]{:S(2)}, u32[]{:S(2)}) %collective-permute-start.11) | collective-permute-done | bytes 131104 | tf_op jit(solution)/shard_map/ppermute | solution.py:384
  80.1 1.6 %collective-permute-done.10.v2 = bf16[256,256]{1,0:T(8,128)(2,1)S(1)} collective-permute-done((bf16[256,256]{1,0:T(8,128)(2,1)S(1)}, bf16[256,256]{1,0:T(8,128)(2,1)S(1)}, u32[]{:S(2)}, u32[]{:S(2)}) %collective-permute-start.10) | collective-permute-done | bytes 131104 | tf_op jit(solution)/shard_map/ppermute | solution.py:384
  81.7 1.9 %collective-permute-done.9.v1 = bf16[256,256]{1,0:T(8,128)(2,1)S(1)} collective-permute-done((bf16[256,256]{1,0:T(8,128)(2,1)S(1)}, bf16[256,256]{1,0:T(8,128)(2,1)S(1)}, u32[]{:S(2)}, u32[]{:S(2)}) %collective-permute-start.9) | collective-permute-done | bytes 131104 | tf_op jit(solution)/shard_map/ppermute | solution.py:384
  83.6 1.5 %shard_map.99 = (bf16[256,1024]{1,0:T(8,128)(2,1)S(1)}, bf16[32,40,128]{2,1,0:T(8,128)(2,1)S(1)}, bf16[32,40,128]{2,1,0:T(8,128)(2,1)S(1)}) custom-call(s32[3]{0:T(128)S(1)} %pad_add_fusion.2.place, bf16[1280,1024]{1,0:T(8,128)(2,1)S(1)} %get-tuple-element.31.table_ref, bf16[256,256]{1,0:T(8,128)(2,1)S(1)} %get-tuple-element.37.v0, ...), custom_call_target="tpu_custom_call" | custom-call | flops 2000000000 | bytes 2000000 | tf_op jit(solution)/shard_map/pallas_call | solution.py:369
  85.2 1.6 %collective-permute-done.12 = bf16[32,40,128]{2,1,0:T(8,128)(2,1)S(1)} collective-permute-done((bf16[32,40,128]{2,1,0:T(8,128)(2,1)S(1)}, bf16[32,40,128]{2,1,0:T(8,128)(2,1)S(1)}, u32[]{:S(2)}, u32[]{:S(2)}) %collective-permute-start.12) | collective-permute-done | bytes 327712 | tf_op jit(solution)/shard_map/ppermute | solution.py:388
  86.9 18.5 %all_to_all.22 = bf16[32,40,128]{2,1,0:T(8,128)(2,1)} all-to-all(bf16[32,40,128]{2,1,0:T(8,128)(2,1)S(1)} %add_convert_fusion), channel_id=1, replica_groups=mesh['x'=4,'yh'=2,'yl'=2,'z'=8,'core'=2] {'yh','yl','z'}, dimensions={0} | all-to-all | bytes 655360 | tf_op jit(solution)/shard_map/all_to_all | solution.py:396
  106.5 17.9 %all_to_all.23.mine_ref = bf16[32,40,128]{2,1,0:T(8,128)(2,1)S(1)} all-to-all(bf16[32,40,128]{2,1,0:T(8,128)(2,1)S(1)} %broadcast_in_dim.8), channel_id=1, replica_groups=mesh['x'=4,'yh'=2,'yl'=2,'z'=8,'core'=2] {'yh','yl','z'}, dimensions={0} | all-to-all | bytes 655360 | tf_op jit(solution)/shard_map/all_to_all | solution.py:399
  124.4 1.6 %collective-permute-done.13.other_ref = bf16[32,40,128]{2,1,0:T(8,128)(2,1)S(1)} collective-permute-done((bf16[32,40,128]{2,1,0:T(8,128)(2,1)S(1)}, bf16[32,40,128]{2,1,0:T(8,128)(2,1)S(1)}, u32[]{:S(2)}, u32[]{:S(2)}) %collective-permute-start.13) | collective-permute-done | bytes 327712 | tf_op jit(solution)/shard_map/ppermute | solution.py:388
  126.0 4.3 %shard_map.100 = (bf16[144,256]{1,0:T(8,128)(2,1)S(1)}, bf16[144,256]{1,0:T(8,128)(2,1)S(1)}, bf16[144,256]{1,0:T(8,128)(2,1)S(1)}, bf16[144,256]{1,0:T(8,128)(2,1)S(1)}) custom-call(s32[3]{0:T(128)S(1)} %pad_add_fusion.2.place, f32[2,640,128]{2,1,0:T(8,128)S(1)} %shard_map.96.weights_ref, bf16[32,40,128]{2,1,0:T(8,128)(2,1)S(1)} %all_to_all.23.mine_ref, ...), custom_call_target="tpu_custom_call" | custom-call | flops 5000000000 | bytes 5000000 | tf_op jit(solution)/shard_map/pallas_call | solution.py:369
  133.3 2.1 %collective-permute-done.14.q1 = bf16[144,256]{1,0:T(8,128)(2,1)S(1)} collective-permute-done((bf16[144,256]{1,0:T(8,128)(2,1)S(1)}, bf16[144,256]{1,0:T(8,128)(2,1)S(1)}, u32[]{:S(2)}, u32[]{:S(2)}) %collective-permute-start.14) | collective-permute-done | bytes 73760 | tf_op jit(solution)/shard_map/ppermute | solution.py:384
  135.4 2.5 %collective-permute-done.15.q2 = bf16[144,256]{1,0:T(8,128)(2,1)S(1)} collective-permute-done((bf16[144,256]{1,0:T(8,128)(2,1)S(1)}, bf16[144,256]{1,0:T(8,128)(2,1)S(1)}, u32[]{:S(2)}, u32[]{:S(2)}) %collective-permute-start.15) | collective-permute-done | bytes 73760 | tf_op jit(solution)/shard_map/ppermute | solution.py:384
  138.5 1.7 %shard_map.101 = (bf16[256,128]{1,0:T(8,128)(2,1)}, f32[3,256]{1,0:T(4,128)}) custom-call(s32[3]{0:T(128)S(1)} %pad_add_fusion.2.place, bf16[144,256]{1,0:T(8,128)(2,1)S(1)} %get-tuple-element.43.q0, bf16[144,256]{1,0:T(8,128)(2,1)S(1)} %collective-permute-done.14.q1, bf16[144,256]{1,0:T(8,128)(2,1)S(1)} %collective-permute-done.15.q2, ...), custom_call_target="tpu_custom_call" | custom-call | flops 2000000000 | bytes 2000000 | tf_op jit(solution)/shard_map/pallas_call | solution.py:357
  (49 shorter events, 14.0 us)
Async XLA Ops:
  1.5 10.1 %collective-permute-start.2 = (s32[1,512]{1,0:T(1,128)S(1)}, s32[1,512]{1,0:T(1,128)S(1)}, u32[]{:S(2)}, u32[]{:S(2)}) collective-permute-start(s32[1,512]{1,0:T(1,128)S(1)} %add_abs_fusion), channel_id=1, source_target_pairs={{0,192},{64,0},{128,64},{192,128},{1,193},{65,1},{129,65},{193,129... | collective-permute-start | bytes 6152 | tf_op jit(solution)/shard_map/ppermute | solution.py:384
  2.4 9.2 %collective-permute-start.1 = (s32[1,512]{1,0:T(1,128)S(1)}, s32[1,512]{1,0:T(1,128)S(1)}, u32[]{:S(2)}, u32[]{:S(2)}) collective-permute-start(s32[1,512]{1,0:T(1,128)S(1)} %add_abs_fusion), channel_id=1, source_target_pairs={{0,128},{64,192},{128,0},{192,64},{1,129},{65,193},{129,1},{193,65... | collective-permute-start | bytes 6152 | tf_op jit(solution)/shard_map/ppermute | solution.py:384
  5.2 6.3 %collective-permute-start = (s32[1,512]{1,0:T(1,128)S(1)}, s32[1,512]{1,0:T(1,128)S(1)}, u32[]{:S(2)}, u32[]{:S(2)}) collective-permute-start(s32[1,512]{1,0:T(1,128)S(1)} %add_abs_fusion), channel_id=1, source_target_pairs={{0,64},{64,128},{128,192},{192,0},{1,65},{65,129},{129,193},{193,1... | collective-permute-start | bytes 6152 | tf_op jit(solution)/shard_map/ppermute | solution.py:384
  11.6 3.4 %collective-permute-start.3 = (bf16[32,40,128]{2,1,0:T(8,128)(2,1)S(1)}, bf16[32,40,128]{2,1,0:T(8,128)(2,1)S(1)}, u32[]{:S(2)}, u32[]{:S(2)}) collective-permute-start(bf16[32,40,128]{2,1,0:T(8,128)(2,1)S(1)} %get-tuple-element.29), channel_id=1, source_target_pairs={{0,1},{1,0},{2,3},{3,2},{4,5},{5,4},{6,7},{7,6},{8,9},{9,8},{10,11... | collective-permute-start | bytes 983048 | tf_op jit(solution)/shard_map/ppermute | solution.py:388
  11.7 5.2 %collective-permute-start.4 = (s32[4,512]{1,0:T(4,128)S(1)}, s32[4,512]{1,0:T(4,128)S(1)}, u32[]{:S(2)}, u32[]{:S(2)}) collective-permute-start(s32[4,512]{1,0:T(4,128)S(1)} %pad_add_fusion.1), channel_id=1, source_target_pairs={{0,32},{32,0},{1,33},{33,1},{2,34},{34,2},{3,35},{35,3},{4,36},{36... | collective-permute-start | bytes 24584 | tf_op jit(solution)/shard_map/ppermute | solution.py:465
  57.7 1.9 %collective-permute-start.5 = (bf16[32,40,128]{2,1,0:T(8,128)(2,1)S(1)}, bf16[32,40,128]{2,1,0:T(8,128)(2,1)S(1)}, u32[]{:S(2)}, u32[]{:S(2)}) collective-permute-start(bf16[32,40,128]{2,1,0:T(8,128)(2,1)S(1)} %all_to_all.21.mine_ref), channel_id=1, source_target_pairs={{0,1},{1,0},{2,3},{3,2},{4,5},{5,4},{6,7},{7,6},{8,9},{9,8},{10,11... | collective-permute-start | bytes 983048 | tf_op jit(solution)/shard_map/ppermute | solution.py:388
  59.6 12.8 %copy-start = (bf16[2048,128]{1,0:T(8,128)(2,1)S(1)}, bf16[2048,128]{1,0:T(8,128)(2,1)}, u32[]{:S(2)}) copy-start(bf16[2048,128]{1,0:T(8,128)(2,1)} %features_ref.1) | copy-start | bytes 1572868
  59.6 12.8 %copy-start.1 = (bf16[2048,128]{1,0:T(8,128)(2,1)S(1)}, bf16[2048,128]{1,0:T(8,128)(2,1)}, u32[]{:S(2)}) copy-start(bf16[2048,128]{1,0:T(8,128)(2,1)} %upstream_ref.1) | copy-start | bytes 1572868
  59.6 12.8 %copy-start.2 = (bf16[2,128,128]{2,1,0:T(8,128)(2,1)S(1)}, bf16[2,128,128]{2,1,0:T(8,128)(2,1)}, u32[]{:S(2)}) copy-start(bf16[2,128,128]{2,1,0:T(8,128)(2,1)} %outward_ref.1) | copy-start | bytes 196612
  59.6 12.7 %copy-start.3 = (bf16[2,128,128]{2,1,0:T(8,128)(2,1)S(1)}, bf16[2,128,128]{2,1,0:T(8,128)(2,1)}, u32[]{:S(2)}) copy-start(bf16[2,128,128]{2,1,0:T(8,128)(2,1)} %inward_ref.3) | copy-start | bytes 196612
  59.6 12.7 %copy-start.4 = (s32[2048]{0:T(1024)S(1)}, s32[2048]{0:T(1024)}, u32[]{:S(2)}) copy-start(s32[2048]{0:T(1024)} %param.10) | copy-start | bytes 24580
  59.7 12.7 %copy-start.5 = (f32[2,6,128]{2,0,1:T(2,128)S(1)}, f32[2,6,128]{2,0,1:T(2,128)}, u32[]{:S(2)}) copy-start(f32[2,6,128]{2,0,1:T(2,128)} %param.14) | copy-start | bytes 18436
  61.3 12.4 %copy-start.6 = (bf16[1280,256]{1,0:T(8,128)(2,1)}, bf16[1280,256]{1,0:T(8,128)(2,1)S(1)}, u32[]{:S(2)}) copy-start(bf16[1280,256]{1,0:T(8,128)(2,1)S(1)} %get-tuple-element.40.fields_hbm) | copy-start | bytes 1966084
  61.3 6.5 %collective-permute-start.6 = (bf16[256,256]{1,0:T(8,128)(2,1)S(1)}, bf16[256,256]{1,0:T(8,128)(2,1)S(1)}, u32[]{:S(2)}, u32[]{:S(2)}) collective-permute-start(bf16[256,256]{1,0:T(8,128)(2,1)S(1)} %get-tuple-element.34), channel_id=1, source_target_pairs={{0,64},{64,128},{128,192},{192,0},{1,65},{65,129},{129,193},{193,1... | collective-permute-start | bytes 393224 | tf_op jit(solution)/shard_map/ppermute | solution.py:384
  62.4 7.8 %collective-permute-start.7 = (bf16[256,256]{1,0:T(8,128)(2,1)S(1)}, bf16[256,256]{1,0:T(8,128)(2,1)S(1)}, u32[]{:S(2)}, u32[]{:S(2)}) collective-permute-start(bf16[256,256]{1,0:T(8,128)(2,1)S(1)} %get-tuple-element.35), channel_id=1, source_target_pairs={{0,128},{64,192},{128,0},{192,64},{1,129},{65,193},{129,1},{193,65... | collective-permute-start | bytes 393224 | tf_op jit(solution)/shard_map/ppermute | solution.py:384
  63.8 8.6 %collective-permute-start.8 = (bf16[256,256]{1,0:T(8,128)(2,1)S(1)}, bf16[256,256]{1,0:T(8,128)(2,1)S(1)}, u32[]{:S(2)}, u32[]{:S(2)}) collective-permute-start(bf16[256,256]{1,0:T(8,128)(2,1)S(1)} %get-tuple-element.36), channel_id=1, source_target_pairs={{0,192},{64,0},{128,64},{192,128},{1,193},{65,1},{129,65},{193,129... | collective-permute-start | bytes 393224 | tf_op jit(solution)/shard_map/ppermute | solution.py:384
  73.7 6.4 %collective-permute-start.11 = (bf16[256,256]{1,0:T(8,128)(2,1)S(1)}, bf16[256,256]{1,0:T(8,128)(2,1)S(1)}, u32[]{:S(2)}, u32[]{:S(2)}) collective-permute-start(bf16[256,256]{1,0:T(8,128)(2,1)S(1)} %get-tuple-element.37.v0), channel_id=1, source_target_pairs={{0,64},{64,128},{128,192},{192,0},{1,65},{65,129},{129,193},{193,1... | collective-permute-start | bytes 393224 | tf_op jit(solution)/shard_map/ppermute | solution.py:384
  74.3 7.4 %collective-permute-start.10 = (bf16[256,256]{1,0:T(8,128)(2,1)S(1)}, bf16[256,256]{1,0:T(8,128)(2,1)S(1)}, u32[]{:S(2)}, u32[]{:S(2)}) collective-permute-start(bf16[256,256]{1,0:T(8,128)(2,1)S(1)} %get-tuple-element.37.v0), channel_id=1, source_target_pairs={{0,128},{64,192},{128,0},{192,64},{1,129},{65,193},{129,1},{193,65... | collective-permute-start | bytes 393224 | tf_op jit(solution)/shard_map/ppermute | solution.py:384
  76.0 7.6 %collective-permute-start.9 = (bf16[256,256]{1,0:T(8,128)(2,1)S(1)}, bf16[256,256]{1,0:T(8,128)(2,1)S(1)}, u32[]{:S(2)}, u32[]{:S(2)}) collective-permute-start(bf16[256,256]{1,0:T(8,128)(2,1)S(1)} %get-tuple-element.37.v0), channel_id=1, source_target_pairs={{0,192},{64,0},{128,64},{192,128},{1,193},{65,1},{129,65},{193,129... | collective-permute-start | bytes 393224 | tf_op jit(solution)/shard_map/ppermute | solution.py:384
  85.1 1.7 %collective-permute-start.12 = (bf16[32,40,128]{2,1,0:T(8,128)(2,1)S(1)}, bf16[32,40,128]{2,1,0:T(8,128)(2,1)S(1)}, u32[]{:S(2)}, u32[]{:S(2)}) collective-permute-start(bf16[32,40,128]{2,1,0:T(8,128)(2,1)S(1)} %get-tuple-element.39), channel_id=1, source_target_pairs={{0,1},{1,0},{2,3},{3,2},{4,5},{5,4},{6,7},{7,6},{8,9},{9,8},{10,11... | collective-permute-start | bytes 983048 | tf_op jit(solution)/shard_map/ppermute | solution.py:388
  124.4 1.6 %collective-permute-start.13 = (bf16[32,40,128]{2,1,0:T(8,128)(2,1)S(1)}, bf16[32,40,128]{2,1,0:T(8,128)(2,1)S(1)}, u32[]{:S(2)}, u32[]{:S(2)}) collective-permute-start(bf16[32,40,128]{2,1,0:T(8,128)(2,1)S(1)} %all_to_all.23.mine_ref), channel_id=1, source_target_pairs={{0,1},{1,0},{2,3},{3,2},{4,5},{5,4},{6,7},{7,6},{8,9},{9,8},{10,11... | collective-permute-start | bytes 983048 | tf_op jit(solution)/shard_map/ppermute | solution.py:388
  130.2 5.2 %collective-permute-start.14 = (bf16[144,256]{1,0:T(8,128)(2,1)S(1)}, bf16[144,256]{1,0:T(8,128)(2,1)S(1)}, u32[]{:S(2)}, u32[]{:S(2)}) collective-permute-start(bf16[144,256]{1,0:T(8,128)(2,1)S(1)} %get-tuple-element.44), channel_id=1, source_target_pairs={{0,64},{64,128},{128,192},{192,0},{1,65},{65,129},{129,193},{193,1... | collective-permute-start | bytes 221192 | tf_op jit(solution)/shard_map/ppermute | solution.py:384
  131.4 6.5 %collective-permute-start.15 = (bf16[144,256]{1,0:T(8,128)(2,1)S(1)}, bf16[144,256]{1,0:T(8,128)(2,1)S(1)}, u32[]{:S(2)}, u32[]{:S(2)}) collective-permute-start(bf16[144,256]{1,0:T(8,128)(2,1)S(1)} %get-tuple-element.45), channel_id=1, source_target_pairs={{0,128},{64,192},{128,0},{192,64},{1,129},{65,193},{129,1},{193,65... | collective-permute-start | bytes 221192 | tf_op jit(solution)/shard_map/ppermute | solution.py:384
  132.5 6.0 %collective-permute-start.16 = (bf16[144,256]{1,0:T(8,128)(2,1)S(1)}, bf16[144,256]{1,0:T(8,128)(2,1)S(1)}, u32[]{:S(2)}, u32[]{:S(2)}) collective-permute-start(bf16[144,256]{1,0:T(8,128)(2,1)S(1)} %get-tuple-element.46), channel_id=1, source_target_pairs={{0,192},{64,0},{128,64},{192,128},{1,193},{65,1},{129,65},{193,129... | collective-permute-start | bytes 221192 | tf_op jit(solution)/shard_map/ppermute | solution.py:384
  (2 other events, 5.4 us)

commit v4 on v3

--- a/solution.py
+++ b/solution.py
@@ -16,12 +16,16 @@
 CLASSES = (SPAN**3 + 1) // 2
 SLABS = 4
 SLAB = 640
+STRIDE = -(-CLASSES // SLABS)
+LAST_FAR = (1, 3, 2)
+COUNT_PIECE = 30
+COUNT_ROW = 32
 TABLE = 2 * SLAB
 BLOCK = 256
 CHANNELS = 128
 ROWS = 40
 PIECES = 32
-VMEM_LIMIT = 24 * 1024 * 1024
+VMEM_LIMIT = 14 * 1024 * 1024
 BF16 = jnp.bfloat16
 F32 = jnp.float32
 
@@ -115,9 +119,10 @@
     outward_hbm,
     multiplier_hbm,
     table_ref,
-    values_ref,
+    values_hbm,
     keep_ref,
     send_ref,
+    values_ref,
     coordinates_ref,
     labels_ref,
     features_ref,
@@ -153,7 +158,7 @@
     ]
     chunk = 64
     for start in range(0, SLAB, chunk):
-        vectors = class_vectors(place[0] * SLAB + start, (chunk, CHANNELS), 0)
+        vectors = class_vectors(place[0] * STRIDE + start, (chunk, CHANNELS), 0)
         for index, side in enumerate(sides):
             columns = slice(index * CHANNELS, (index + 1) * CHANNELS)
             turns = vectors[0] * coordinates_ref[0:1, side]
@@ -175,25 +180,43 @@
         grad_pot = matmul(outward_ref[1], upstream_ref[block], 1, 1)
         values_ref[:CHANNELS, slot(index)] = charges.astype(BF16)
         values_ref[CHANNELS:, slot(index)] = grad_pot.astype(BF16)
+    leaving = pltpu.make_async_copy(values_ref, values_hbm, arrivals.at[len(copies)])
+    leaving.start()
     total_ref[...] = matmul(table_ref[...], values_ref[...], 1, 1)
+    for half in range(2):
+        total_ref[(half + 1) * SLAB - 8 : (half + 1) * SLAB, :CHANNELS] = jnp.zeros((8, CHANNELS), F32)
     write_pieces(place, total_ref, keep_ref, send_ref)
-
-
-def weights_kernel(prefactor, place, classes_ref, weights_ref):
-    chunk = 128
-    for start in range(0, SLAB, chunk):
-        rows = pl.ds(start, chunk)
-        own = lax.broadcasted_iota(jnp.int32, (chunk, CHANNELS), 0) + (place[0] * SLAB + start)
-        count = jnp.zeros((chunk, CHANNELS), F32)
-        for group in range(classes_ref.shape[0]):
-            for offset in range(0, classes_ref.shape[1], CHANNELS):
-                classes = classes_ref[group : group + 1, offset : offset + CHANNELS]
-                count += jnp.where(classes == own, 1.0, 0.0)
-        count = jnp.sum(count, axis=1, keepdims=True)
-        vectors = class_vectors(place[0] * SLAB + start, (chunk, CHANNELS), 0)
+    leaving.wait()
+
+
+def counts_kernel(copies, place, momenta_ref, counts_ref):
+    momenta = momenta_ref[...].astype(F32)
+    label = jnp.abs(
+        momenta[0:1] * float(SPAN * SPAN) + momenta[1:2] * float(SPAN) + momenta[2:3]
+    ) - (place[0] * STRIDE).astype(F32)
+    column = jnp.transpose(jnp.broadcast_to(label, (8, label.shape[1])))[:, 0:1]
+    column = jnp.broadcast_to(column, (column.shape[0], CHANNELS))
+    lane = lax.broadcasted_iota(jnp.int32, column.shape, 1).astype(F32)
+    counts_ref[...] = jnp.zeros(counts_ref.shape, BF16)
+    rows = []
+    for start in range(0, SLAB, CHANNELS):
+        here = (column == lane + float(start)) & (lane < float(STRIDE - start))
+        rows.append(jnp.sum(jnp.where(here, 1.0 / copies, 0.0), axis=0, keepdims=True))
+    rows.append(jnp.zeros((8 - len(rows), CHANNELS), F32))
+    counts_ref[COUNT_PIECE, COUNT_ROW:, :] = jnp.concatenate(rows, axis=0).astype(BF16)
+
+
+def weights_kernel(prefactor, place, pieces_ref, weights_ref):
+    counts = jnp.transpose(pieces_ref[COUNT_PIECE, COUNT_ROW:, :].astype(F32))
+    for index in range(SLAB // CHANNELS):
+        start = index * CHANNELS
+        count = counts[:, index : index + 1]
+        vectors = class_vectors(place[0] * STRIDE + start, (CHANNELS, CHANNELS), 0)
         norm = vectors[0] * vectors[0] + vectors[1] * vectors[1] + vectors[2] * vectors[2]
         for block, spread in enumerate(GAUSSIAN_SIGMAS):
-            weights_ref[block, rows, :] = count * (prefactor * jnp.exp(norm * (-1.0 / spread)))
+            weights_ref[block, start : start + CHANNELS, :] = count * (
+                prefactor * jnp.exp(norm * (-1.0 / spread))
+            )
 
 
 def weigh(total_ref, weights_ref, first):
@@ -250,7 +273,7 @@
 
 
 def second_kernel(place, table_ref, v0, v1, v2, v3, values_ref, keep_ref, send_ref, total_ref):
-    for index, source in enumerate((v0, v1, v2, v3)):
+    for index, source in zip((0, *LAST_FAR), (v0, v1, v2, v3)):
         values_ref[:, slot(index)] = source[...]
     total_ref[...] = matmul(table_ref[...], values_ref[...], 1, 1)
     write_pieces(place, total_ref, keep_ref, send_ref)
@@ -294,7 +317,7 @@
     pairs_ref[:, 0:CHANNELS] = grad_one.astype(BF16)
     pairs_ref[:, CHANNELS : 2 * CHANNELS] = total_ref[:, :CHANNELS].astype(BF16)
     flipped = jnp.transpose(grad_one).astype(BF16)
-    vectors = class_vectors(place[0] * SLAB, (16, SLAB), 1)
+    vectors = class_vectors(place[0] * STRIDE, (16, SLAB), 1)
     row = lax.broadcasted_iota(jnp.int32, (16, SLAB), 0)
     directions = jnp.where(row == 0, vectors[0], jnp.where(row == 1, vectors[1], vectors[2]))
     directions = jnp.where(row < 3, directions, 0.0).astype(BF16)
@@ -364,13 +387,14 @@
     )(*operands)
 
 
-def call_whole(kernel, outs, scratch, place, operands, spaces=None, micros=2):
+def call_whole(kernel, outs, scratch, place, operands, spaces=None, out_spaces=None, micros=2):
     spaces = spaces or [pltpu.VMEM] * len(operands)
+    out_spaces = out_spaces or [pltpu.VMEM] * len(outs)
     return pl.pallas_call(
         kernel,
         in_specs=[pl.BlockSpec(memory_space=pltpu.SMEM)]
         + [pl.BlockSpec(memory_space=space) for space in spaces],
-        out_specs=[pl.BlockSpec(memory_space=pltpu.VMEM)] * len(outs),
+        out_specs=[pl.BlockSpec(memory_space=space) for space in out_spaces],
         out_shape=outs,
         scratch_shapes=scratch,
         **compiler(micros),
@@ -384,12 +408,19 @@
     return lax.ppermute(value, "x", [(i, (i + shift) % SLABS) for i in range(SLABS)])
 
 
+def spread_out(send, own, order):
+    return [own] + [send(shift) for shift in order]
+
+
 def swapped(value):
     return lax.ppermute(value, "core", [(0, 1), (1, 0)])
 
 
-def add_halves(keep, send):
-    return (keep.astype(F32) + swapped(send).astype(F32)).astype(BF16)
+def add_halves(keep, send, *more):
+    total = keep.astype(F32) + swapped(send).astype(F32)
+    for value in more:
+        total = total + value.astype(F32)
+    return total.astype(BF16)
 
 
 def sum_fields(part):
@@ -420,11 +451,15 @@
     )
     labels = element_labels[None, :]
     multiplier = jnp.swapaxes(element_latent_multiplier, 0, 1)
-    signed = (
-        lattice_momenta[0] * (SPAN * SPAN) + lattice_momenta[1] * SPAN + lattice_momenta[2]
-    )
-    own = jnp.abs(signed)[None]
-    row = jnp.concatenate([own] + [shifted(own, shift) for shift in range(1, SLABS)], axis=0)
+    lengths = {axis: lax.axis_size(axis) for axis in ("x", "yl", "z")}
+    copies = lengths["yl"] * lengths["z"] // SLABS
+    pairs = []
+    for yl in range(lengths["yl"]):
+        for z in range(lengths["z"]):
+            for x in range(SLABS):
+                place_of = lambda x: (x * lengths["yl"] + yl) * lengths["z"] + z
+                pairs.append((place_of((x + 2 * (z % 2) + yl) % SLABS), place_of(x)))
+    fetched = lax.ppermute(lattice_momenta, ("x", "yl", "z"), pairs)
 
     matrices = whole((2, CHANNELS, CHANNELS))
     gains_spec = whole(multiplier.shape)
@@ -449,30 +484,31 @@
         tables_kernel,
         (
             pltpu.VMEM((TABLE, atoms_here), BF16),
-            shape_of((BLOCK, atoms_here), BF16),
+            pltpu.HBM((BLOCK, atoms_here), BF16),
             pieces_shape,
             pieces_shape,
         ),
-        [pltpu.VMEM(value.shape, value.dtype) for value in local]
-        + [pltpu.VMEM((TABLE, BLOCK), F32), pltpu.SemaphoreType.DMA((len(operands),))],
+        [pltpu.VMEM((BLOCK, atoms_here), BF16)]
+        + [pltpu.VMEM(value.shape, value.dtype) for value in local]
+        + [pltpu.VMEM((TABLE, BLOCK), F32), pltpu.SemaphoreType.DMA((len(operands) + 1,))],
         place,
         [far(value) for value in operands],
         spaces=[pltpu.HBM] * len(operands),
+        out_spaces=[pltpu.VMEM, pltpu.HBM, pltpu.VMEM, pltpu.VMEM],
         micros=7,
     )
-    keep, send, row = lax.optimization_barrier((keep, send, row))
-    part = add_halves(keep, send)
-    other_row = lax.ppermute(row, "yh", [(0, 1), (1, 0)])
-    part, other_row = lax.optimization_barrier((part, other_row))
-    classes = jnp.concatenate([row, other_row], axis=0)
+    (counts,) = call_whole(
+        functools.partial(counts_kernel, float(copies)), [pieces_shape], [], place, [fetched]
+    )
+    part = add_halves(keep, send, counts)
+    mine, other = sum_fields(part)
     (weights,) = call_whole(
         functools.partial(weights_kernel, prefactor),
         [shape_of((2, SLAB, CHANNELS), F32)],
         [],
         place,
-        [classes],
-    )
-    mine, other = sum_fields(part)
+        [mine],
+    )
     fields, *products = call_whole(
         potential_kernel,
         [shape_of((TABLE, BLOCK), BF16)] + [values_shape] * SLABS,
@@ -480,7 +516,7 @@
         place,
         [weights, mine, other, near(table)],
     )
-    arrived = [products[0]] + [shifted(products[shift], shift) for shift in range(1, SLABS)]
+    arrived = spread_out(lambda shift: shifted(products[shift], shift), products[0], (2, 1, 3))
     own_atoms = pl.BlockSpec((BLOCK, CHANNELS), lambda step, place: (2 * place[0] + place[1], 0))
     own_labels = pl.BlockSpec((1, BLOCK), lambda step, place: (0, 2 * place[0] + place[1]))
     values_own, hidden_grad = call(
@@ -500,7 +536,7 @@
             multiplier,
         ),
     )
-    seconds = [values_own] + [shifted(values_own, SLABS - other) for other in range(1, SLABS)]
+    seconds = spread_out(lambda shift: shifted(values_own, SLABS - shift), values_own, LAST_FAR)
     values_two, keep, send = call_whole(
         second_kernel,
         [shape_of((BLOCK, atoms_here), BF16), pieces_shape, pieces_shape],
@@ -527,7 +563,7 @@
         spaces=[pltpu.VMEM] * 4 + [pltpu.HBM] * 3,
         micros=5,
     )
-    arrived = [results[0]] + [shifted(results[shift], shift) for shift in range(1, SLABS)]
+    arrived = spread_out(lambda shift: shifted(results[shift], shift), results[0], (2, 1, 3))
     return call(
         final_kernel,
         [result_spec] * SLABS

time: 141 us -> 137 us (0.972)
  starting transfers between devices: 17.6 us -> 11.6 us
  blocking collectives: 77 us -> 82.9 us
  waiting for transfers between devices: 24.4 us -> 21.3 us
    all_to_all x2, blocking collectives: 42.6 us -> 48.5 us  [sum_fields(): parts = lax.all_to_all(part, ATOM_REST, 0, 0, tiled=True)]
    ppermute x12 -> x9, starting transfers between devices: 14.1 us -> 10.7 us  [shifted(): lax.ppermute(value, 'x', [(i, (i + shift) % SLABS) for i in range(SLABS)])]
    ppermute x1, starting transfers between devices: 3.28 us -> 0.66 us  [per_device(): fetched = lax.ppermute(lattice_momenta, ('x', 'yl', 'z'), pairs)]
    ppermute x12 -> x9, waiting for transfers between devices: 19.3 us -> 17.3 us  [shifted(): lax.ppermute(value, 'x', [(i, (i + shift) % SLABS) for i in range(SLABS)])]
    ppermute x1, waiting for transfers between devices: 1.85 us -> 0.01 us  [per_device(): fetched = lax.ppermute(lattice_momenta, ('x', 'yl', 'z'), pairs)]
    pallas_call x5 -> x6, Pallas kernels: 15.1 us -> 15.2 us  [call_whole(): pl.pallas_call(kernel, in_specs=[pl.BlockSpec(memory_space=pltpu.SMEM)] +...]
  transfers between devices with their start and end apart: 17 -> 14, of which waited for: 12 -> 10; matrix products, arithmetic and copies ran while one was open for 0% -> 0% of each run, Pallas kernels for 6% -> 1%
where the time goes in v4:
time: 137 us; the launch traced here: 136 us
  blocking collectives  82.9 us (61%)
  waiting for transfers between devices  21.3 us (16%)
  Pallas kernels  18.1 us (13%)
  starting transfers between devices  11.6 us (8%)
  other arithmetic  1.39 us (1%)
    all_to_all x2, blocking collectives, sum_fields(): parts = lax.all_to_all(part, ATOM_REST, 0, 0, tiled=True)  48.5 us
    all_to_all x2, blocking collectives, sum_fields(): mine = lax.all_to_all(spread, ATOM_REST, 0, 0, tiled=True)  34.5 us
    ppermute x9, waiting for transfers between devices, shifted(): lax.ppermute(value, 'x', [(i, (i + shift) % SLABS) for i in range(SLABS)])  17.3 us
    pallas_call x6, Pallas kernels, call_whole(): pl.pallas_call(kernel, in_specs=[pl.BlockSpec(memory_space=pltpu.SMEM)] +...  15.2 us
    ppermute x9, starting transfers between devices, shifted(): lax.ppermute(value, 'x', [(i, (i + shift) % SLABS) for i in range(SLABS)])  10.7 us
    ppermute x4, waiting for transfers between devices, swapped(): return lax.ppermute(value, 'core', [(0, 1), (1, 0)])  4.02 us
    pallas_call x2, Pallas kernels, call(): pl.pallas_call(kernel, grid_spec=pltpu.PrefetchScalarGridSpec(num_scalar_...  2.93 us
  transfers between devices with their start and end apart: 14, of which 10 were waited for; matrix products, arithmetic and copies ran while one was open for 0% of the time, Pallas kernels for 1%

profile of v4, /device:TPU:6, one launch (start us, length us, event | category | flops | bytes accessed | tf_op | source)
XLA Modules:
  0.0 136.3 jit_solution(8055217860550358430)
XLA Ops:
  0.7 6.1 %shard_map.95 = (bf16[1280,1024]{1,0:T(8,128)(2,1)S(1)}, bf16[256,1024]{1,0:T(8,128)(2,1)}, bf16[32,40,128]{2,1,0:T(8,128)(2,1)S(1)}, bf16[32,40,128]{2,1,0:T(8,128)(2,1)S(1)}) custom-call(s32[3]{0:T(128)S(1)} %pad_add_fusion.place, f32[3,2048]{1,0:T(4,128)} %coordinates_hbm.1, s32[1,2048]{1,0:T(1,128)} %bitcast.9, bf16[4,2,256,128]{3,2,1,0:T(8,128)(2,1)} %bitcast.7, ...), custom_call_target="tpu_custom_call" | custom-call | flops 7000000000 | bytes 7000000 | tf_op jit(solution)/shard_map/pallas_call | solution.py:393
  8.7 30.0 %all_to_all.20 = bf16[32,40,128]{2,1,0:T(8,128)(2,1)S(1)} all-to-all(bf16[32,40,128]{2,1,0:T(8,128)(2,1)S(1)} %add_convert_fusion.1), channel_id=1, replica_groups=mesh['x'=4,'yh'=2,'yl'=2,'z'=8,'core'=2] {'yh','yl','z'}, dimensions={0} | all-to-all | bytes 655360 | tf_op jit(solution)/shard_map/all_to_all | solution.py:427
  38.8 16.6 %all_to_all.21.pieces_ref.mine_ref = bf16[32,40,128]{2,1,0:T(8,128)(2,1)S(1)} all-to-all(bf16[32,40,128]{2,1,0:T(8,128)(2,1)S(1)} %broadcast_in_dim.7), channel_id=1, replica_groups=mesh['x'=4,'yh'=2,'yl'=2,'z'=8,'core'=2] {'yh','yl','z'}, dimensions={0} | all-to-all | bytes 655360 | tf_op jit(solution)/shard_map/all_to_all | solution.py:430
  57.0 1.6 %shard_map.98 = (bf16[1280,256]{1,0:T(8,128)(2,1)S(1)}, bf16[256,256]{1,0:T(8,128)(2,1)S(1)}, bf16[256,256]{1,0:T(8,128)(2,1)S(1)}, bf16[256,256]{1,0:T(8,128)(2,1)S(1)}, bf16[256,256]{1,0:T(8,128)(2,1)S(1)}) custom-call(s32[3]{0:T(128)S(1)} %pad_add_fusion.place, f32[2,640,128]{2,1,0:T(8,128)S(1)} %shard_map.97.weights_ref, ...), custom_call_target="tpu_custom_call" | custom-call | flops 2000000000 | bytes 2000000 | tf_op jit(solution)/shard_map/pallas_call | solution.py:393
  58.7 1.5 %collective-permute-start.3 = (bf16[256,256]{1,0:T(8,128)(2,1)S(1)}, bf16[256,256]{1,0:T(8,128)(2,1)S(1)}, u32[]{:S(2)}, u32[]{:S(2)}) collective-permute-start(bf16[256,256]{1,0:T(8,128)(2,1)S(1)} %get-tuple-element.24), channel_id=1, source_target_pairs={{0,128},{64,192},{128,0},{192,64},{1,129},{65,193},{129,1},{193,65... | collective-permute-start | bytes 393224 | tf_op jit(solution)/shard_map/ppermute | solution.py:408
  60.1 2.1 %collective-permute-start.4 = (bf16[256,256]{1,0:T(8,128)(2,1)S(1)}, bf16[256,256]{1,0:T(8,128)(2,1)S(1)}, u32[]{:S(2)}, u32[]{:S(2)}) collective-permute-start(bf16[256,256]{1,0:T(8,128)(2,1)S(1)} %get-tuple-element.25), channel_id=1, source_target_pairs={{0,64},{64,128},{128,192},{192,0},{1,65},{65,129},{129,193},{193,1... | collective-permute-start | bytes 393224 | tf_op jit(solution)/shard_map/ppermute | solution.py:408
  62.2 4.3 %collective-permute-done.3.q1 = bf16[256,256]{1,0:T(8,128)(2,1)S(1)} collective-permute-done((bf16[256,256]{1,0:T(8,128)(2,1)S(1)}, bf16[256,256]{1,0:T(8,128)(2,1)S(1)}, u32[]{:S(2)}, u32[]{:S(2)}) %collective-permute-start.3) | collective-permute-done | bytes 131104 | tf_op jit(solution)/shard_map/ppermute | solution.py:408
  66.6 2.3 %collective-permute-done.5.q3 = bf16[256,256]{1,0:T(8,128)(2,1)S(1)} collective-permute-done((bf16[256,256]{1,0:T(8,128)(2,1)S(1)}, bf16[256,256]{1,0:T(8,128)(2,1)S(1)}, u32[]{:S(2)}, u32[]{:S(2)}) %collective-permute-start.5) | collective-permute-done | bytes 131104 | tf_op jit(solution)/shard_map/ppermute | solution.py:408
  68.9 1.2 shard_map.99
  70.2 1.2 collective-permute-start.8
  71.4 1.2 collective-permute-start.7
  73.5 4.4 %collective-permute-done.8.v3 = bf16[256,256]{1,0:T(8,128)(2,1)S(1)} collective-permute-done((bf16[256,256]{1,0:T(8,128)(2,1)S(1)}, bf16[256,256]{1,0:T(8,128)(2,1)S(1)}, u32[]{:S(2)}, u32[]{:S(2)}) %collective-permute-start.8) | collective-permute-done | bytes 131104 | tf_op jit(solution)/shard_map/ppermute | solution.py:408
  77.8 1.5 %collective-permute-done.6.v1 = bf16[256,256]{1,0:T(8,128)(2,1)S(1)} collective-permute-done((bf16[256,256]{1,0:T(8,128)(2,1)S(1)}, bf16[256,256]{1,0:T(8,128)(2,1)S(1)}, u32[]{:S(2)}, u32[]{:S(2)}) %collective-permute-start.6) | collective-permute-done | bytes 131104 | tf_op jit(solution)/shard_map/ppermute | solution.py:408
  79.4 1.5 %shard_map.100 = (bf16[256,1024]{1,0:T(8,128)(2,1)S(1)}, bf16[32,40,128]{2,1,0:T(8,128)(2,1)S(1)}, bf16[32,40,128]{2,1,0:T(8,128)(2,1)S(1)}) custom-call(s32[3]{0:T(128)S(1)} %pad_add_fusion.place, bf16[1280,1024]{1,0:T(8,128)(2,1)S(1)} %get-tuple-element.22.table_ref, bf16[256,256]{1,0:T(8,128)(2,1)S(1)} %get-tuple-element.27.v0, ...), custom_call_target="tpu_custom_call" | custom-call | flops 2000000000 | bytes 2000000 | tf_op jit(solution)/shard_map/pallas_call | solution.py:393
  81.0 1.6 %collective-permute-done.9 = bf16[32,40,128]{2,1,0:T(8,128)(2,1)S(1)} collective-permute-done((bf16[32,40,128]{2,1,0:T(8,128)(2,1)S(1)}, bf16[32,40,128]{2,1,0:T(8,128)(2,1)S(1)}, u32[]{:S(2)}, u32[]{:S(2)}) %collective-permute-start.9) | collective-permute-done | bytes 327712 | tf_op jit(solution)/shard_map/ppermute | solution.py:416
  82.7 18.4 %all_to_all.22 = bf16[32,40,128]{2,1,0:T(8,128)(2,1)} all-to-all(bf16[32,40,128]{2,1,0:T(8,128)(2,1)S(1)} %add_convert_fusion), channel_id=1, replica_groups=mesh['x'=4,'yh'=2,'yl'=2,'z'=8,'core'=2] {'yh','yl','z'}, dimensions={0} | all-to-all | bytes 655360 | tf_op jit(solution)/shard_map/all_to_all | solution.py:427
  102.2 17.9 %all_to_all.23.mine_ref = bf16[32,40,128]{2,1,0:T(8,128)(2,1)S(1)} all-to-all(bf16[32,40,128]{2,1,0:T(8,128)(2,1)S(1)} %broadcast_in_dim.8), channel_id=1, replica_groups=mesh['x'=4,'yh'=2,'yl'=2,'z'=8,'core'=2] {'yh','yl','z'}, dimensions={0} | all-to-all | bytes 655360 | tf_op jit(solution)/shard_map/all_to_all | solution.py:430
  120.1 1.6 %collective-permute-done.10.other_ref = bf16[32,40,128]{2,1,0:T(8,128)(2,1)S(1)} collective-permute-done((bf16[32,40,128]{2,1,0:T(8,128)(2,1)S(1)}, bf16[32,40,128]{2,1,0:T(8,128)(2,1)S(1)}, u32[]{:S(2)}, u32[]{:S(2)}) %collective-permute-start.10) | collective-permute-done | bytes 327712 | tf_op jit(solution)/shard_map/ppermute | solution.py:416
  121.7 4.3 %shard_map.101 = (bf16[144,256]{1,0:T(8,128)(2,1)S(1)}, bf16[144,256]{1,0:T(8,128)(2,1)S(1)}, bf16[144,256]{1,0:T(8,128)(2,1)S(1)}, bf16[144,256]{1,0:T(8,128)(2,1)S(1)}) custom-call(s32[3]{0:T(128)S(1)} %pad_add_fusion.place, f32[2,640,128]{2,1,0:T(8,128)S(1)} %shard_map.97.weights_ref, bf16[32,40,128]{2,1,0:T(8,128)(2,1)S(1)} %all_to_all.23.mine_ref, ...), custom_call_target="tpu_custom_call" | custom-call | flops 5000000000 | bytes 5000000 | tf_op jit(solution)/shard_map/pallas_call | solution.py:393
  126.0 1.8 %collective-permute-start.11 = (bf16[144,256]{1,0:T(8,128)(2,1)S(1)}, bf16[144,256]{1,0:T(8,128)(2,1)S(1)}, u32[]{:S(2)}, u32[]{:S(2)}) collective-permute-start(bf16[144,256]{1,0:T(8,128)(2,1)S(1)} %get-tuple-element.34), channel_id=1, source_target_pairs={{0,128},{64,192},{128,0},{192,64},{1,129},{65,193},{129,1},{193,65... | collective-permute-start | bytes 221192 | tf_op jit(solution)/shard_map/ppermute | solution.py:408
  127.8 1.2 collective-permute-start.12
  129.9 2.3 %collective-permute-done.11.q1 = bf16[144,256]{1,0:T(8,128)(2,1)S(1)} collective-permute-done((bf16[144,256]{1,0:T(8,128)(2,1)S(1)}, bf16[144,256]{1,0:T(8,128)(2,1)S(1)}, u32[]{:S(2)}, u32[]{:S(2)}) %collective-permute-start.11) | collective-permute-done | bytes 73760 | tf_op jit(solution)/shard_map/ppermute | solution.py:408
  132.2 2.4 %collective-permute-done.13.q3 = bf16[144,256]{1,0:T(8,128)(2,1)S(1)} collective-permute-done((bf16[144,256]{1,0:T(8,128)(2,1)S(1)}, bf16[144,256]{1,0:T(8,128)(2,1)S(1)}, u32[]{:S(2)}, u32[]{:S(2)}) %collective-permute-start.13) | collective-permute-done | bytes 73760 | tf_op jit(solution)/shard_map/ppermute | solution.py:408
  134.6 1.7 %shard_map.102 = (bf16[256,128]{1,0:T(8,128)(2,1)}, f32[3,256]{1,0:T(4,128)}) custom-call(s32[3]{0:T(128)S(1)} %pad_add_fusion.place, bf16[144,256]{1,0:T(8,128)(2,1)S(1)} %get-tuple-element.33.q0, bf16[144,256]{1,0:T(8,128)(2,1)S(1)} %collective-permute-done.11.q1, bf16[144,256]{1,0:T(8,128)(2,1)S(1)} %collective-permute-done.12.q2, ...), custom_call_target="tpu_custom_call" | custom-call | flops 2000000000 | bytes 2000000 | tf_op jit(solution)/shard_map/pallas_call | solution.py:380
  (41 shorter events, 6.6 us)
Async XLA Ops:
  0.7 6.2 %copy-start.8 = (s32[3,512]{1,0:T(4,128)S(1)}, s32[3,512]{1,0:T(4,128)}, u32[]{:S(2)}) copy-start(s32[3,512]{1,0:T(4,128)} %param.11) | copy-start | bytes 18436
  6.8 1.7 %collective-permute-start = (bf16[32,40,128]{2,1,0:T(8,128)(2,1)S(1)}, bf16[32,40,128]{2,1,0:T(8,128)(2,1)S(1)}, u32[]{:S(2)}, u32[]{:S(2)}) collective-permute-start(bf16[32,40,128]{2,1,0:T(8,128)(2,1)S(1)} %get-tuple-element.21), channel_id=1, source_target_pairs={{0,1},{1,0},{2,3},{3,2},{4,5},{5,4},{6,7},{7,6},{8,9},{9,8},{10,11... | collective-permute-start | bytes 983048 | tf_op jit(solution)/shard_map/ppermute | solution.py:416
  6.9 0.7 collective-permute-start.1
  55.4 1.6 %collective-permute-start.2 = (bf16[32,40,128]{2,1,0:T(8,128)(2,1)S(1)}, bf16[32,40,128]{2,1,0:T(8,128)(2,1)S(1)}, u32[]{:S(2)}, u32[]{:S(2)}) collective-permute-start(bf16[32,40,128]{2,1,0:T(8,128)(2,1)S(1)} %all_to_all.21.pieces_ref.mine_ref), channel_id=1, source_target_pairs={{0,1},{1,0},{2,3},{3,2},{4,5},{5,4},{6,7},{7,6},{8,9},{9,8},{10,11... | collective-permute-start | bytes 983048 | tf_op jit(solution)/shard_map/ppermute | solution.py:416
  57.0 11.9 %copy-start = (bf16[2048,128]{1,0:T(8,128)(2,1)S(1)}, bf16[2048,128]{1,0:T(8,128)(2,1)}, u32[]{:S(2)}) copy-start(bf16[2048,128]{1,0:T(8,128)(2,1)} %features_ref.1) | copy-start | bytes 1572868
  57.0 11.9 %copy-start.1 = (bf16[2048,128]{1,0:T(8,128)(2,1)S(1)}, bf16[2048,128]{1,0:T(8,128)(2,1)}, u32[]{:S(2)}) copy-start(bf16[2048,128]{1,0:T(8,128)(2,1)} %upstream_ref.1) | copy-start | bytes 1572868
  57.0 11.9 %copy-start.2 = (bf16[2,128,128]{2,1,0:T(8,128)(2,1)S(1)}, bf16[2,128,128]{2,1,0:T(8,128)(2,1)}, u32[]{:S(2)}) copy-start(bf16[2,128,128]{2,1,0:T(8,128)(2,1)} %outward_ref.1) | copy-start | bytes 196612
  57.0 11.9 %copy-start.3 = (bf16[2,128,128]{2,1,0:T(8,128)(2,1)S(1)}, bf16[2,128,128]{2,1,0:T(8,128)(2,1)}, u32[]{:S(2)}) copy-start(bf16[2,128,128]{2,1,0:T(8,128)(2,1)} %inward_ref.3) | copy-start | bytes 196612
  57.0 11.9 %copy-start.4 = (s32[2048]{0:T(1024)S(1)}, s32[2048]{0:T(1024)}, u32[]{:S(2)}) copy-start(s32[2048]{0:T(1024)} %param.10) | copy-start | bytes 24580
  57.0 11.9 %copy-start.5 = (f32[2,6,128]{2,0,1:T(2,128)S(1)}, f32[2,6,128]{2,0,1:T(2,128)}, u32[]{:S(2)}) copy-start(f32[2,6,128]{2,0,1:T(2,128)} %param.14) | copy-start | bytes 18436
  58.6 11.5 %copy-start.6 = (bf16[1280,256]{1,0:T(8,128)(2,1)}, bf16[1280,256]{1,0:T(8,128)(2,1)S(1)}, u32[]{:S(2)}) copy-start(bf16[1280,256]{1,0:T(8,128)(2,1)S(1)} %get-tuple-element.30.fields_hbm) | copy-start | bytes 1966084
  58.7 7.9 %collective-permute-start.3 = (bf16[256,256]{1,0:T(8,128)(2,1)S(1)}, bf16[256,256]{1,0:T(8,128)(2,1)S(1)}, u32[]{:S(2)}, u32[]{:S(2)}) collective-permute-start(bf16[256,256]{1,0:T(8,128)(2,1)S(1)} %get-tuple-element.24), channel_id=1, source_target_pairs={{0,128},{64,192},{128,0},{192,64},{1,129},{65,193},{129,1},{193,65... | collective-permute-start | bytes 393224 | tf_op jit(solution)/shard_map/ppermute | solution.py:408
  60.1 6.4 %collective-permute-start.4 = (bf16[256,256]{1,0:T(8,128)(2,1)S(1)}, bf16[256,256]{1,0:T(8,128)(2,1)S(1)}, u32[]{:S(2)}, u32[]{:S(2)}) collective-permute-start(bf16[256,256]{1,0:T(8,128)(2,1)S(1)} %get-tuple-element.25), channel_id=1, source_target_pairs={{0,64},{64,128},{128,192},{192,0},{1,65},{65,129},{129,193},{193,1... | collective-permute-start | bytes 393224 | tf_op jit(solution)/shard_map/ppermute | solution.py:408
  62.2 6.7 %collective-permute-start.5 = (bf16[256,256]{1,0:T(8,128)(2,1)S(1)}, bf16[256,256]{1,0:T(8,128)(2,1)S(1)}, u32[]{:S(2)}, u32[]{:S(2)}) collective-permute-start(bf16[256,256]{1,0:T(8,128)(2,1)S(1)} %get-tuple-element.26), channel_id=1, source_target_pairs={{0,192},{64,0},{128,64},{192,128},{1,193},{65,1},{129,65},{193,129... | collective-permute-start | bytes 393224 | tf_op jit(solution)/shard_map/ppermute | solution.py:408
  70.2 7.6 %collective-permute-start.8 = (bf16[256,256]{1,0:T(8,128)(2,1)S(1)}, bf16[256,256]{1,0:T(8,128)(2,1)S(1)}, u32[]{:S(2)}, u32[]{:S(2)}) collective-permute-start(bf16[256,256]{1,0:T(8,128)(2,1)S(1)} %get-tuple-element.27.v0), channel_id=1, source_target_pairs={{0,128},{64,192},{128,0},{192,64},{1,129},{65,193},{129,1},{193,65... | collective-permute-start | bytes 393224 | tf_op jit(solution)/shard_map/ppermute | solution.py:408
  71.4 6.4 %collective-permute-start.7 = (bf16[256,256]{1,0:T(8,128)(2,1)S(1)}, bf16[256,256]{1,0:T(8,128)(2,1)S(1)}, u32[]{:S(2)}, u32[]{:S(2)}) collective-permute-start(bf16[256,256]{1,0:T(8,128)(2,1)S(1)} %get-tuple-element.27.v0), channel_id=1, source_target_pairs={{0,64},{64,128},{128,192},{192,0},{1,65},{65,129},{129,193},{193,1... | collective-permute-start | bytes 393224 | tf_op jit(solution)/shard_map/ppermute | solution.py:408
  72.6 6.8 %collective-permute-start.6 = (bf16[256,256]{1,0:T(8,128)(2,1)S(1)}, bf16[256,256]{1,0:T(8,128)(2,1)S(1)}, u32[]{:S(2)}, u32[]{:S(2)}) collective-permute-start(bf16[256,256]{1,0:T(8,128)(2,1)S(1)} %get-tuple-element.27.v0), channel_id=1, source_target_pairs={{0,192},{64,0},{128,64},{192,128},{1,193},{65,1},{129,65},{193,129... | collective-permute-start | bytes 393224 | tf_op jit(solution)/shard_map/ppermute | solution.py:408
  80.9 1.8 %copy-start.7 = (bf16[256,1024]{1,0:T(8,128)(2,1)}, bf16[256,1024]{1,0:T(8,128)(2,1)S(1)}, u32[]{:S(2)}) copy-start(bf16[256,1024]{1,0:T(8,128)(2,1)S(1)} %get-tuple-element.32.second_hbm) | copy-start | bytes 1572868
  80.9 1.7 %collective-permute-start.9 = (bf16[32,40,128]{2,1,0:T(8,128)(2,1)S(1)}, bf16[32,40,128]{2,1,0:T(8,128)(2,1)S(1)}, u32[]{:S(2)}, u32[]{:S(2)}) collective-permute-start(bf16[32,40,128]{2,1,0:T(8,128)(2,1)S(1)} %get-tuple-element.29), channel_id=1, source_target_pairs={{0,1},{1,0},{2,3},{3,2},{4,5},{5,4},{6,7},{7,6},{8,9},{9,8},{10,11... | collective-permute-start | bytes 983048 | tf_op jit(solution)/shard_map/ppermute | solution.py:416
  120.1 1.6 %collective-permute-start.10 = (bf16[32,40,128]{2,1,0:T(8,128)(2,1)S(1)}, bf16[32,40,128]{2,1,0:T(8,128)(2,1)S(1)}, u32[]{:S(2)}, u32[]{:S(2)}) collective-permute-start(bf16[32,40,128]{2,1,0:T(8,128)(2,1)S(1)} %all_to_all.23.mine_ref), channel_id=1, source_target_pairs={{0,1},{1,0},{2,3},{3,2},{4,5},{5,4},{6,7},{7,6},{8,9},{9,8},{10,11... | collective-permute-start | bytes 983048 | tf_op jit(solution)/shard_map/ppermute | solution.py:416
  126.0 6.2 %collective-permute-start.11 = (bf16[144,256]{1,0:T(8,128)(2,1)S(1)}, bf16[144,256]{1,0:T(8,128)(2,1)S(1)}, u32[]{:S(2)}, u32[]{:S(2)}) collective-permute-start(bf16[144,256]{1,0:T(8,128)(2,1)S(1)} %get-tuple-element.34), channel_id=1, source_target_pairs={{0,128},{64,192},{128,0},{192,64},{1,129},{65,193},{129,1},{193,65... | collective-permute-start | bytes 221192 | tf_op jit(solution)/shard_map/ppermute | solution.py:408
  127.8 4.4 %collective-permute-start.12 = (bf16[144,256]{1,0:T(8,128)(2,1)S(1)}, bf16[144,256]{1,0:T(8,128)(2,1)S(1)}, u32[]{:S(2)}, u32[]{:S(2)}) collective-permute-start(bf16[144,256]{1,0:T(8,128)(2,1)S(1)} %get-tuple-element.35), channel_id=1, source_target_pairs={{0,64},{64,128},{128,192},{192,0},{1,65},{65,129},{129,193},{193,1... | collective-permute-start | bytes 221192 | tf_op jit(solution)/shard_map/ppermute | solution.py:408
  129.0 5.6 %collective-permute-start.13 = (bf16[144,256]{1,0:T(8,128)(2,1)S(1)}, bf16[144,256]{1,0:T(8,128)(2,1)S(1)}, u32[]{:S(2)}, u32[]{:S(2)}) collective-permute-start(bf16[144,256]{1,0:T(8,128)(2,1)S(1)} %get-tuple-element.36), channel_id=1, source_target_pairs={{0,192},{64,0},{128,64},{192,128},{1,193},{65,1},{129,65},{193,129... | collective-permute-start | bytes 221192 | tf_op jit(solution)/shard_map/ppermute | solution.py:408

commit v5 on v4

--- a/solution.py
+++ b/solution.py
@@ -17,7 +17,9 @@
 SLABS = 4
 SLAB = 640
 STRIDE = -(-CLASSES // SLABS)
-LAST_FAR = (1, 3, 2)
+LAST_FAR = (2, 3, 1)
+LEAP = REACH * SPAN
+FIRST_ROWS = ((0, LEAP // 2 + 4), (LEAP // 2 + 4, LEAP))
 COUNT_PIECE = 30
 COUNT_ROW = 32
 TABLE = 2 * SLAB
@@ -83,6 +85,12 @@
     return result
 
 
+def cosine_and_sine(turns):
+    turns = turns - jnp.floor(turns + 0.5)
+    square = turns * turns
+    return series(COS_SERIES, square), turns * series(SIN_SERIES, square)
+
+
 def write_pieces(place, total_ref, keep_ref, send_ref):
     core = place[2]
     for target, half in ((keep_ref, core), (send_ref, 1 - core)):
@@ -94,15 +102,17 @@
             ].astype(BF16)
 
 
-def read_pieces(place, mine_ref, other_ref, total_ref):
-    core = place[2]
-    for source, half in ((mine_ref, core), (other_ref, 1 - core)):
-        for index in range(PIECES):
-            row, side = index // 2, index % 2
-            start = pl.multiple_of(half * SLAB + row * ROWS, 8)
-            total_ref[pl.ds(start, ROWS), side * CHANNELS : (side + 1) * CHANNELS] = source[
-                index
-            ].astype(F32)
+def weigh_pieces(pieces_ref, weights_ref, first, total_ref):
+    for index in range(PIECES):
+        row, side = index // 2, index % 2
+        rows = slice(row * ROWS, (row + 1) * ROWS)
+        total_ref[rows, side * CHANNELS : (side + 1) * CHANNELS] = (
+            pieces_ref[index].astype(F32) * weights_ref[(first + side) % 2, rows]
+        )
+
+
+def half_rows(half):
+    return pl.ds(pl.multiple_of(half * SLAB, SLAB), SLAB)
 
 
 def slot(index):
@@ -131,6 +141,9 @@
     outward_ref,
     multiplier_ref,
     total_ref,
+    cosine_ref,
+    sine_ref,
+    second_ref,
     arrivals,
 ):
     copies = [
@@ -149,27 +162,46 @@
     ]
     for copy in copies:
         copy.start()
-    copies[0].wait()
     blocks = [lax.rem(place[0] + index, SLABS) for index in range(SLABS)]
     sides = [
         pl.ds(pl.multiple_of((2 * block + place[1]) * BLOCK + side * CHANNELS, CHANNELS), CHANNELS)
         for block in blocks
         for side in range(BLOCK // CHANNELS)
     ]
-    chunk = 64
-    for start in range(0, SLAB, chunk):
-        vectors = class_vectors(place[0] * STRIDE + start, (chunk, CHANNELS), 0)
-        for index, side in enumerate(sides):
-            columns = slice(index * CHANNELS, (index + 1) * CHANNELS)
-            turns = vectors[0] * coordinates_ref[0:1, side]
-            turns += vectors[1] * coordinates_ref[1:2, side]
-            turns += vectors[2] * coordinates_ref[2:3, side]
-            turns -= jnp.floor(turns + 0.5)
-            square = turns * turns
-            table_ref[start : start + chunk, columns] = series(COS_SERIES, square).astype(BF16)
-            table_ref[SLAB + start : SLAB + start + chunk, columns] = (
-                turns * series(SIN_SERIES, square)
-            ).astype(BF16)
+    first_vectors = [
+        class_vectors(place[0] * STRIDE + start, (stop - start, CHANNELS), 0)
+        for start, stop in FIRST_ROWS
+    ]
+    for start in range(0, SLAB - LEAP, LEAP):
+        stop = min(start + LEAP, SLAB - LEAP)
+        vectors = class_vectors(place[0] * STRIDE + start, (stop - start, CHANNELS), 0)
+        second_ref[start:stop] = vectors[1]
+    copies[0].wait()
+    for index, side in enumerate(sides):
+        columns = slice(index * CHANNELS, (index + 1) * CHANNELS)
+        where = [coordinates_ref[axis : axis + 1, side] for axis in range(3)]
+        for (start, stop), vectors in zip(FIRST_ROWS, first_vectors):
+            turns = vectors[0] * where[0] + vectors[1] * where[1] + vectors[2] * where[2]
+            cosine, sine = cosine_and_sine(turns)
+            cosine_ref[start:stop, columns] = cosine
+            sine_ref[start:stop, columns] = sine
+            table_ref[start:stop, columns] = cosine.astype(BF16)
+            table_ref[SLAB + start : SLAB + stop, columns] = sine.astype(BF16)
+        plain = cosine_and_sine(REACH * where[1])
+        carried = cosine_and_sine(where[0] - (REACH + 1) * where[1])
+        for start in range(LEAP, SLAB, 72):
+            stop = min(start + 72, SLAB)
+            before = slice(start - LEAP, stop - LEAP)
+            carry = second_ref[before] > 0.5
+            turn_cosine = jnp.where(carry, carried[0], plain[0])
+            turn_sine = jnp.where(carry, carried[1], plain[1])
+            old_cosine, old_sine = cosine_ref[before, columns], sine_ref[before, columns]
+            cosine = old_cosine * turn_cosine - old_sine * turn_sine
+            sine = old_sine * turn_cosine + old_cosine * turn_sine
+            cosine_ref[start:stop, columns] = cosine
+            sine_ref[start:stop, columns] = sine
+            table_ref[start:stop, columns] = cosine.astype(BF16)
+            table_ref[SLAB + start : SLAB + stop, columns] = sine.astype(BF16)
     for copy in copies[1:]:
         copy.wait()
     inward = flip(inward_ref[0])
@@ -206,8 +238,24 @@
     counts_ref[COUNT_PIECE, COUNT_ROW:, :] = jnp.concatenate(rows, axis=0).astype(BF16)
 
 
-def weights_kernel(prefactor, place, pieces_ref, weights_ref):
-    counts = jnp.transpose(pieces_ref[COUNT_PIECE, COUNT_ROW:, :].astype(F32))
+def write_fields(total_ref, fields_ref):
+    fields_ref[:, :CHANNELS] = total_ref[:, CHANNELS:].astype(BF16)
+    fields_ref[:, CHANNELS:] = total_ref[:, :CHANNELS].astype(BF16)
+
+
+def first_potential_kernel(
+    prefactor,
+    place,
+    mine_ref,
+    table_ref,
+    weights_ref,
+    fields_hbm,
+    potential_ref,
+    total_ref,
+    fields_ref,
+    leaves,
+):
+    counts = jnp.transpose(mine_ref[COUNT_PIECE, COUNT_ROW:, :].astype(F32))
     for index in range(SLAB // CHANNELS):
         start = index * CHANNELS
         count = counts[:, index : index + 1]
@@ -217,25 +265,50 @@
             weights_ref[block, start : start + CHANNELS, :] = count * (
                 prefactor * jnp.exp(norm * (-1.0 / spread))
             )
-
-
-def weigh(total_ref, weights_ref, first):
-    for half in range(2):
-        rows = pl.ds(half * SLAB, SLAB)
-        for side in range(2):
-            columns = pl.ds(side * CHANNELS, CHANNELS)
-            total_ref[rows, columns] = total_ref[rows, columns] * weights_ref[(first + side) % 2]
+    weigh_pieces(mine_ref, weights_ref, 0, total_ref)
+    write_fields(total_ref, fields_ref)
+    leaving = pltpu.make_async_copy(fields_ref, fields_hbm, leaves)
+    leaving.start()
+    flipped = jnp.transpose(total_ref[...]).astype(BF16)
+    potential_ref[...] = matmul(flipped, table_ref[half_rows(place[2]), :], 1, 0)
+    leaving.wait()
 
 
 def potential_kernel(
-    place, weights_ref, mine_ref, other_ref, table_ref, fields_ref, p0, p1, p2, p3, total_ref
-):
-    read_pieces(place, mine_ref, other_ref, total_ref)
-    weigh(total_ref, weights_ref, 0)
-    fields_ref[...] = total_ref[...].astype(BF16)
-    flipped = jnp.transpose(total_ref[...]).astype(BF16)
-    for index, target in enumerate((p0, p1, p2, p3)):
-        target[...] = matmul(flipped, table_ref[:, slot(index)], 1, 0).astype(BF16)
+    place, weights_ref, other_ref, table_ref, before_ref, fields_ref, flipped_ref, p2, p1, p3, total_ref
+):
+    weigh_pieces(other_ref, weights_ref, 0, total_ref)
+    write_fields(total_ref, fields_ref)
+    flipped_ref[...] = jnp.transpose(total_ref[...]).astype(BF16)
+    for index, target in ((2, p2), (1, p1), (3, p3)):
+        rest = matmul(flipped_ref[...], table_ref[half_rows(1 - place[2]), slot(index)], 1, 0)
+        target[...] = (before_ref[:, slot(index)] + rest).astype(BF16)
+
+
+def own_potential_kernel(place, table_ref, before_ref, flipped_ref, p0):
+    rest = matmul(flipped_ref[...], table_ref[half_rows(1 - place[2]), slot(0)], 1, 0)
+    p0[...] = (before_ref[:, slot(0)] + rest).astype(BF16)
+
+
+def own_atoms_kernel(
+    place,
+    labels_ref,
+    features_ref,
+    upstream_ref,
+    inward_ref,
+    multiplier_ref,
+    own_features_ref,
+    own_upstream_ref,
+    gains_one_ref,
+    gains_two_ref,
+    flipped_ref,
+):
+    own_features_ref[...] = features_ref[...]
+    own_upstream_ref[...] = upstream_ref[...]
+    gains_one_ref[...] = jnp.transpose(gain_columns(multiplier_ref[:, 0, :], labels_ref[...]))
+    gains_two_ref[...] = gain_columns(multiplier_ref[:, 1, :], labels_ref[...])
+    for block in range(2):
+        flipped_ref[block] = flip(inward_ref[block])
 
 
 def middle_kernel(
@@ -244,32 +317,25 @@
     q1,
     q2,
     q3,
-    labels_ref,
     features_ref,
     upstream_ref,
-    inward_ref,
+    gains_ref,
+    flipped_ref,
     outward_ref,
-    multiplier_ref,
     values_ref,
     hidden_grad_ref,
 ):
     total = (q0[...].astype(F32) + q1[...].astype(F32)) + (q2[...].astype(F32) + q3[...].astype(F32))
-    potential = total[:CHANNELS].astype(BF16)
     grad_charge = total[CHANNELS:]
-    gains = gain_columns(multiplier_ref[:, 1, :], labels_ref[...])
-    hidden = (
-        features_ref[...].astype(F32)
-        + matmul(jnp.transpose(potential.astype(F32)).astype(BF16), outward_ref[0], 1, 0)
-    ).astype(BF16)
-    inward_flipped = flip(inward_ref[1])
-    charges = matmul(inward_flipped, hidden, 1, 1) * gains
-    scaled = jnp.transpose(grad_charge * gains).astype(BF16)
+    scaled = jnp.transpose(grad_charge * gains_ref[...]).astype(BF16)
     hidden_grad = (
-        upstream_ref[...].astype(F32) + matmul(scaled, inward_flipped, 1, 0)
+        upstream_ref[...].astype(F32) + matmul(scaled, flipped_ref[1], 1, 0)
     ).astype(BF16)
     hidden_grad_ref[...] = hidden_grad
-    grad_pot = matmul(outward_ref[0], hidden_grad, 1, 1)
-    values_ref[...] = jnp.concatenate([charges, grad_pot], axis=0).astype(BF16)
+    values_ref[CHANNELS:] = matmul(outward_ref[0], hidden_grad, 1, 1).astype(BF16)
+    potential = jnp.transpose(total[:CHANNELS]).astype(BF16)
+    hidden = (features_ref[...].astype(F32) + matmul(potential, outward_ref[0], 1, 0)).astype(BF16)
+    values_ref[:CHANNELS] = (matmul(flipped_ref[1], hidden, 1, 1) * gains_ref[...]).astype(BF16)
 
 
 def second_kernel(place, table_ref, v0, v1, v2, v3, values_ref, keep_ref, send_ref, total_ref):
@@ -279,23 +345,31 @@
     write_pieces(place, total_ref, keep_ref, send_ref)
 
 
-def gradient_kernel(
+def half_theta(half, table_ref, columns, pairs, values):
+    sign = (2 * half - 1).astype(F32)
+    along = matmul(pairs, values, 1, 0)
+    return (sign * table_ref[half_rows(1 - half), columns].astype(F32)) * along
+
+
+def write_pairs(total_ref, fields_ref, pairs_ref):
+    pairs_ref[:, :CHANNELS] = total_ref[:, CHANNELS:].astype(BF16)
+    pairs_ref[:, CHANNELS : 2 * CHANNELS] = total_ref[:, :CHANNELS].astype(BF16)
+    pairs_ref[:, 2 * CHANNELS :] = fields_ref[...]
+
+
+def first_gradient_kernel(
     place,
     weights_ref,
     mine_ref,
-    other_ref,
     table_ref,
     fields_hbm,
     first_hbm,
     second_hbm,
-    o0,
-    o1,
-    o2,
-    o3,
+    values_ref,
+    theta_ref,
+    charge_ref,
     total_ref,
     pairs_ref,
-    values_ref,
-    theta_ref,
     fields_ref,
     arrivals,
 ):
@@ -311,42 +385,85 @@
     ]
     for copy in copies:
         copy.start()
-    read_pieces(place, mine_ref, other_ref, total_ref)
-    weigh(total_ref, weights_ref, 1)
-    grad_one = total_ref[:, CHANNELS:]
-    pairs_ref[:, 0:CHANNELS] = grad_one.astype(BF16)
-    pairs_ref[:, CHANNELS : 2 * CHANNELS] = total_ref[:, :CHANNELS].astype(BF16)
-    flipped = jnp.transpose(grad_one).astype(BF16)
+    weigh_pieces(mine_ref, weights_ref, 1, total_ref)
+    flipped = jnp.transpose(total_ref[:, CHANNELS:]).astype(BF16)
+    charge_ref[...] = matmul(flipped, table_ref[half_rows(place[2]), :], 1, 0)
+    for copy in copies:
+        copy.wait()
+    write_pairs(total_ref, fields_ref, pairs_ref)
+    for index in range(SLABS):
+        columns = slot(index)
+        theta_ref[:, columns] = half_theta(
+            place[2], table_ref, columns, pairs_ref[...], values_ref[:, columns]
+        )
+
+
+def finish_gradient(
+    index, place, table_ref, pairs_ref, flipped_ref, values_ref, theta_ref, charge_ref, directions, target
+):
+    columns = slot(index)
+    theta = half_theta(1 - place[2], table_ref, columns, pairs_ref[...], values_ref[:, columns])
+    charge = matmul(flipped_ref[...], table_ref[half_rows(1 - place[2]), columns], 1, 0)
+    position = matmul(directions, (theta + theta_ref[:, columns]).astype(BF16), 1, 0)
+    target[:CHANNELS] = (charge + charge_ref[:, columns]).astype(BF16)
+    target[CHANNELS:] = (position * (2.0 * math.pi / BOX_LENGTH)).astype(BF16)
+
+
+def class_directions(place):
     vectors = class_vectors(place[0] * STRIDE, (16, SLAB), 1)
     row = lax.broadcasted_iota(jnp.int32, (16, SLAB), 0)
     directions = jnp.where(row == 0, vectors[0], jnp.where(row == 1, vectors[1], vectors[2]))
-    directions = jnp.where(row < 3, directions, 0.0).astype(BF16)
-    for copy in copies:
-        copy.wait()
-    pairs_ref[:, 2 * CHANNELS : 3 * CHANNELS] = fields_ref[:, CHANNELS:]
-    pairs_ref[:, 3 * CHANNELS :] = fields_ref[:, :CHANNELS]
-    for index, target in enumerate((o0, o1, o2, o3)):
-        columns = slot(index)
-        along_real = matmul(pairs_ref[:SLAB], values_ref[:, columns], 1, 0)
-        along_imag = matmul(pairs_ref[SLAB:], values_ref[:, columns], 1, 0)
-        theta_ref[:, columns] = (
-            table_ref[:SLAB, columns].astype(F32) * along_imag
-            - table_ref[SLAB:, columns].astype(F32) * along_real
-        ).astype(BF16)
-        charge = matmul(flipped, table_ref[:, columns], 1, 0)
-        position = matmul(directions, theta_ref[:, columns], 1, 0)
-        target[:CHANNELS] = charge.astype(BF16)
-        target[CHANNELS:] = (position * (2.0 * math.pi / BOX_LENGTH)).astype(BF16)
+    return jnp.where(row < 3, directions, 0.0).astype(BF16)
+
+
+def gradient_kernel(
+    place,
+    weights_ref,
+    other_ref,
+    table_ref,
+    fields_ref,
+    values_ref,
+    theta_ref,
+    charge_ref,
+    pairs_ref,
+    flipped_ref,
+    o2,
+    o1,
+    o3,
+    total_ref,
+):
+    weigh_pieces(other_ref, weights_ref, 1, total_ref)
+    write_pairs(total_ref, fields_ref, pairs_ref)
+    flipped_ref[...] = jnp.transpose(total_ref[:, CHANNELS:]).astype(BF16)
+    directions = class_directions(place)
+    rest = (place, table_ref, pairs_ref, flipped_ref, values_ref, theta_ref, charge_ref, directions)
+    for index, target in ((2, o2), (1, o1), (3, o3)):
+        finish_gradient(index, *rest, target)
+
+
+def own_gradient_kernel(
+    place, table_ref, pairs_ref, flipped_ref, values_ref, theta_ref, charge_ref, o0
+):
+    rest = (place, table_ref, pairs_ref, flipped_ref, values_ref, theta_ref, charge_ref)
+    finish_gradient(0, *rest, class_directions(place), o0)
+
+
+def sum_kernel(place, parts_ref, spread_ref):
+    total = parts_ref[0].astype(F32)
+    for index in range(1, PIECES):
+        total += parts_ref[index].astype(F32)
+    total = total.astype(BF16)
+    for index in range(PIECES):
+        spread_ref[index] = total
 
 
 def final_kernel(
-    place, q0, q1, q2, q3, labels_ref, hidden_grad_ref, inward_ref, multiplier_ref, features_ref, positions_ref
+    place, q0, q1, q2, q3, gains_ref, hidden_grad_ref, flipped_ref, features_ref, positions_ref
 ):
     total = (q0[...].astype(F32) + q1[...].astype(F32)) + (q2[...].astype(F32) + q3[...].astype(F32))
-    gains = gain_columns(multiplier_ref[:, 0, :], labels_ref[...])
-    scaled = jnp.transpose(total[:CHANNELS] * gains).astype(BF16)
+    scaled = (jnp.transpose(total[:CHANNELS]) * gains_ref[...]).astype(BF16)
     features_ref[...] = (
-        hidden_grad_ref[...].astype(F32) + matmul(scaled, flip(inward_ref[0]), 1, 0)
+        hidden_grad_ref[...].astype(F32) + matmul(scaled, flipped_ref[0], 1, 0)
     ).astype(BF16)
     positions_ref[...] = total[CHANNELS : CHANNELS + 3]
 
@@ -371,7 +488,7 @@
     return dict(
         compiler_params=pltpu.CompilerParams(vmem_limit_bytes=VMEM_LIMIT),
         cost_estimate=pl.CostEstimate(
-            flops=micros * 10**9, bytes_accessed=micros * 10**6, transcendentals=0
+            flops=int(micros * 10**9), bytes_accessed=int(micros * 10**6), transcendentals=0
         ),
     )
 
@@ -423,10 +540,15 @@
     return total.astype(BF16)
 
 
-def sum_fields(part):
+def sum_fields(place, part):
     parts = lax.all_to_all(part, ATOM_REST, 0, 0, tiled=True)
-    total = jnp.sum(parts.astype(F32), axis=0).astype(BF16)
-    spread = jnp.broadcast_to(total[None], (PIECES,) + total.shape)
+    if place is None:
+        total = jnp.sum(parts.astype(F32), axis=0).astype(BF16)
+        spread = jnp.broadcast_to(total[None], parts.shape)
+    else:
+        (spread,) = call_whole(
+            sum_kernel, [pltpu.VMEM(parts.shape, BF16)], [], place, [near(parts)], micros=1
+        )
     mine = lax.all_to_all(spread, ATOM_REST, 0, 0, tiled=True)
     return mine, swapped(mine)
 
@@ -490,7 +612,13 @@
         ),
         [pltpu.VMEM((BLOCK, atoms_here), BF16)]
         + [pltpu.VMEM(value.shape, value.dtype) for value in local]
-        + [pltpu.VMEM((TABLE, BLOCK), F32), pltpu.SemaphoreType.DMA((len(operands) + 1,))],
+        + [
+            pltpu.VMEM((TABLE, BLOCK), F32),
+            pltpu.VMEM((SLAB, atoms_here), F32),
+            pltpu.VMEM((SLAB, atoms_here), F32),
+            pltpu.VMEM((SLAB - LEAP, CHANNELS), F32),
+            pltpu.SemaphoreType.DMA((len(operands) + 1,)),
+        ],
         place,
         [far(value) for value in operands],
         spaces=[pltpu.HBM] * len(operands),
@@ -501,40 +629,74 @@
         functools.partial(counts_kernel, float(copies)), [pieces_shape], [], place, [fetched]
     )
     part = add_halves(keep, send, counts)
-    mine, other = sum_fields(part)
-    (weights,) = call_whole(
-        functools.partial(weights_kernel, prefactor),
-        [shape_of((2, SLAB, CHANNELS), F32)],
+    mine, other = sum_fields(None, part)
+    half = (SLAB, BLOCK)
+    weights, fields_mine, before = call_whole(
+        functools.partial(first_potential_kernel, prefactor),
+        [
+            shape_of((2, SLAB, CHANNELS), F32),
+            pltpu.HBM(half, BF16),
+            shape_of((BLOCK, atoms_here), F32),
+        ],
+        [pltpu.VMEM(half, F32), pltpu.VMEM(half, BF16), pltpu.SemaphoreType.DMA],
+        place,
+        [mine, near(table)],
+        out_spaces=[pltpu.VMEM, pltpu.HBM, pltpu.VMEM],
+    )
+    fields_other, flipped, p2, p1, p3 = call_whole(
+        potential_kernel,
+        [shape_of(half, BF16), shape_of((BLOCK, SLAB), BF16)] + [values_shape] * 3,
+        [pltpu.VMEM(half, F32)],
+        place,
+        [weights, other, near(table), before],
+    )
+    (p0,) = call_whole(
+        own_potential_kernel,
+        [values_shape],
         [],
         place,
-        [mine],
-    )
-    fields, *products = call_whole(
-        potential_kernel,
-        [shape_of((TABLE, BLOCK), BF16)] + [values_shape] * SLABS,
-        [pltpu.VMEM((TABLE, BLOCK), F32)],
-        place,
-        [weights, mine, other, near(table)],
-    )
-    arrived = spread_out(lambda shift: shifted(products[shift], shift), products[0], (2, 1, 3))
+        [near(table), before, flipped],
+        micros=0.1,
+    )
     own_atoms = pl.BlockSpec((BLOCK, CHANNELS), lambda step, place: (2 * place[0] + place[1], 0))
     own_labels = pl.BlockSpec((1, BLOCK), lambda step, place: (0, 2 * place[0] + place[1]))
-    values_own, hidden_grad = call(
-        middle_kernel,
-        [values_block] * SLABS
-        + [own_labels, own_atoms, own_atoms, matrices, matrices, gains_spec],
-        (values_shape, shape_of((BLOCK, CHANNELS), BF16)),
-        (values_block, whole((BLOCK, CHANNELS))),
+    own_block = (BLOCK, CHANNELS)
+    labels, p0 = lax.optimization_barrier((labels, p0))
+    products = (p0, p1, p2, p3)
+    arrived = spread_out(lambda shift: shifted(products[shift], shift), products[0], (2, 1, 3))
+    own_features, own_upstream, gains_one, gains_two, inward_flipped = call(
+        own_atoms_kernel,
+        [own_labels, own_atoms, own_atoms, matrices, gains_spec],
+        (
+            shape_of(own_block, BF16),
+            shape_of(own_block, BF16),
+            shape_of(own_block, F32),
+            shape_of((CHANNELS, BLOCK), F32),
+            shape_of((2, CHANNELS, CHANNELS), BF16),
+        ),
+        (
+            whole(own_block),
+            whole(own_block),
+            whole(own_block),
+            whole((CHANNELS, BLOCK)),
+            matrices,
+        ),
         (
             place,
-            *arrived,
             labels,
             atomic_descriptors,
             upstream_gradient,
             feature_to_latent_matrix,
-            latent_to_feature_matrix,
             multiplier,
         ),
+        micros=0.1,
+    )
+    values_own, hidden_grad = call_whole(
+        middle_kernel,
+        [values_shape, shape_of(own_block, BF16)],
+        [],
+        place,
+        [*arrived, own_features, own_upstream, gains_two, inward_flipped, latent_to_feature_matrix],
     )
     seconds = spread_out(lambda shift: shifted(values_own, SLABS - shift), values_own, LAST_FAR)
     values_two, keep, send = call_whole(
@@ -544,33 +706,51 @@
         place,
         [near(table), *seconds],
     )
-    mine, other = sum_fields(add_halves(keep, send))
+    mine, other = sum_fields(place, add_halves(keep, send))
     result_shape = shape_of((CHANNELS + 16, BLOCK), BF16)
     result_spec = whole((CHANNELS + 16, BLOCK))
-    results = call_whole(
-        gradient_kernel,
-        [result_shape] * SLABS,
+    values, theta, charge = call_whole(
+        first_gradient_kernel,
         [
-            pltpu.VMEM((TABLE, BLOCK), F32),
-            pltpu.VMEM((TABLE, 2 * BLOCK), BF16),
-            pltpu.VMEM((2 * BLOCK, atoms_here), BF16),
-            pltpu.VMEM((SLAB, atoms_here), BF16),
-            pltpu.VMEM((TABLE, BLOCK), BF16),
+            shape_of((2 * BLOCK, atoms_here), BF16),
+            shape_of((SLAB, atoms_here), F32),
+            shape_of((CHANNELS, atoms_here), F32),
+        ],
+        [
+            pltpu.VMEM(half, F32),
+            pltpu.VMEM((SLAB, 2 * BLOCK), BF16),
+            pltpu.VMEM(half, BF16),
             pltpu.SemaphoreType.DMA((3,)),
         ],
         place,
-        [weights, mine, other, near(table), far(fields), far(values_one), far(values_two)],
-        spaces=[pltpu.VMEM] * 4 + [pltpu.HBM] * 3,
-        micros=5,
-    )
+        [weights, mine, near(table), far(fields_mine), far(values_one), far(values_two)],
+        spaces=[pltpu.VMEM] * 3 + [pltpu.HBM] * 3,
+    )
+    pairs, flipped, o2, o1, o3 = call_whole(
+        gradient_kernel,
+        [shape_of((SLAB, 2 * BLOCK), BF16), shape_of((CHANNELS, SLAB), BF16)] + [result_shape] * 3,
+        [pltpu.VMEM(half, F32)],
+        place,
+        [weights, other, near(table), fields_other, values, theta, charge],
+    )
+    (o0,) = call_whole(
+        own_gradient_kernel,
+        [result_shape],
+        [],
+        place,
+        [near(table), pairs, flipped, values, theta, charge],
+        micros=0.1,
+    )
+    results = (o0, o1, o2, o3)
     arrived = spread_out(lambda shift: shifted(results[shift], shift), results[0], (2, 1, 3))
-    return call(
-        final_kernel,
-        [result_spec] * SLABS
-        + [own_labels, whole((BLOCK, CHANNELS)), matrices, gains_spec],
-        (shape_of((BLOCK, CHANNELS), BF16), shape_of((3, BLOCK), F32)),
-        (whole((BLOCK, CHANNELS)), whole((3, BLOCK))),
-        (place, *arrived, labels, hidden_grad, feature_to_latent_matrix, multiplier),
+    return tuple(
+        call_whole(
+            final_kernel,
+            [shape_of(own_block, BF16), shape_of((3, BLOCK), F32)],
+            [],
+            place,
+            [*arrived, gains_one, hidden_grad, inward_flipped],
+        )
     )
 
 

time: 137 us -> 134 us (0.978)
  waiting for transfers between devices: 21.3 us -> 16.1 us
  Pallas kernels: 18.1 us -> 21.5 us
    pallas_call x6 -> x12, Pallas kernels: 15.2 us -> 20.3 us  [call_whole(): pl.pallas_call(kernel, in_specs=[pl.BlockSpec(memory_space=pltpu.SMEM)] +...]
    ppermute x9, waiting for transfers between devices: 17.3 us -> 14.4 us  [shifted(): lax.ppermute(value, 'x', [(i, (i + shift) % SLABS) for i in range(SLABS)])]
    ppermute x4, waiting for transfers between devices: 4.02 us -> 1.69 us  [swapped(): return lax.ppermute(value, 'core', [(0, 1), (1, 0)])]
    pallas_call x2 -> x1, Pallas kernels: 2.93 us -> 1.15 us  [call(): pl.pallas_call(kernel, grid_spec=pltpu.PrefetchScalarGridSpec(num_scalar_...]
  transfers between devices with their start and end apart: 14 -> 14, of which waited for: 10 -> 9; matrix products, arithmetic and copies ran while one was open for 0% -> 0% of each run, Pallas kernels for 1% -> 7%
where the time goes in v5:
time: 134 us; the launch traced here: 133 us
  blocking collectives  82.8 us (62%)
  Pallas kernels  21.5 us (16%)
  waiting for transfers between devices  16.1 us (12%)
  starting transfers between devices  11.6 us (9%)
    all_to_all x2, blocking collectives, sum_fields(): parts = lax.all_to_all(part, ATOM_REST, 0, 0, tiled=True)  48.4 us
    all_to_all x2, blocking collectives, sum_fields(): mine = lax.all_to_all(spread, ATOM_REST, 0, 0, tiled=True)  34.5 us
    pallas_call x12, Pallas kernels, call_whole(): pl.pallas_call(kernel, in_specs=[pl.BlockSpec(memory_space=pltpu.SMEM)] +...  20.3 us
    ppermute x9, waiting for transfers between devices, shifted(): lax.ppermute(value, 'x', [(i, (i + shift) % SLABS) for i in range(SLABS)])  14.4 us
    ppermute x9, starting transfers between devices, shifted(): lax.ppermute(value, 'x', [(i, (i + shift) % SLABS) for i in range(SLABS)])  10.8 us
  transfers between devices with their start and end apart: 14, of which 9 were waited for; matrix products, arithmetic and copies ran while one was open for 0% of the time, Pallas kernels for 7%

profile of v5, /device:TPU:6, one launch (start us, length us, event | category | flops | bytes accessed | tf_op | source)
XLA Modules:
  0.0 133.3 jit_solution(1433176867759921747)
XLA Ops:
  0.7 4.6 %shard_map.95 = (bf16[1280,1024]{1,0:T(8,128)(2,1)S(1)}, bf16[256,1024]{1,0:T(8,128)(2,1)}, bf16[32,40,128]{2,1,0:T(8,128)(2,1)S(1)}, bf16[32,40,128]{2,1,0:T(8,128)(2,1)S(1)}) custom-call(s32[3]{0:T(128)S(1)} %pad_add_fusion.place, f32[3,2048]{1,0:T(4,128)} %coordinates_hbm.1, s32[1,2048]{1,0:T(1,128)} %bitcast.9, bf16[4,2,256,128]{3,2,1,0:T(8,128)(2,1)} %bitcast.7, ...), custom_call_target="tpu_custom_call" | custom-call | flops 7000000000 | bytes 7000000 | tf_op jit(solution)/shard_map/pallas_call | solution.py:510
  7.2 30.0 %all_to_all.20 = bf16[32,40,128]{2,1,0:T(8,128)(2,1)S(1)} all-to-all(bf16[32,40,128]{2,1,0:T(8,128)(2,1)S(1)} %add_convert_fusion.1), channel_id=1, replica_groups=mesh['x'=4,'yh'=2,'yl'=2,'z'=8,'core'=2] {'yh','yl','z'}, dimensions={0} | all-to-all | bytes 655360 | tf_op jit(solution)/shard_map/all_to_all | solution.py:544
  37.4 16.6 %all_to_all.21.mine_ref = bf16[32,40,128]{2,1,0:T(8,128)(2,1)S(1)} all-to-all(bf16[32,40,128]{2,1,0:T(8,128)(2,1)S(1)} %broadcast_in_dim.10), channel_id=1, replica_groups=mesh['x'=4,'yh'=2,'yl'=2,'z'=8,'core'=2] {'yh','yl','z'}, dimensions={0} | all-to-all | bytes 655360 | tf_op jit(solution)/shard_map/all_to_all | solution.py:552
  53.9 2.0 %shard_map.97 = (f32[2,640,128]{2,1,0:T(8,128)S(1)}, bf16[640,256]{1,0:T(8,128)(2,1)}, f32[256,1024]{1,0:T(8,128)S(1)}) custom-call(s32[3]{0:T(128)S(1)} %pad_add_fusion.place, bf16[32,40,128]{2,1,0:T(8,128)(2,1)S(1)} %all_to_all.21.mine_ref, bf16[1280,1024]{1,0:T(8,128)(2,1)S(1)} %get-tuple-element.34.table_ref), custom_call_target="tpu_custom_call" | custom-call | flops 2000000000 | bytes 2000000 | tf_op jit(solution)/shard_map/pallas_call | solution.py:510
  57.1 1.5 %collective-permute-start.3 = (bf16[256,256]{1,0:T(8,128)(2,1)S(1)}, bf16[256,256]{1,0:T(8,128)(2,1)S(1)}, u32[]{:S(2)}, u32[]{:S(2)}) collective-permute-start(bf16[256,256]{1,0:T(8,128)(2,1)S(1)} %get-tuple-element.41), channel_id=1, source_target_pairs={{0,128},{64,192},{128,0},{192,64},{1,129},{65,193},{129,1},{193,65... | collective-permute-start | bytes 393224 | tf_op jit(solution)/shard_map/ppermute | solution.py:525
  58.6 2.1 %collective-permute-start.4 = (bf16[256,256]{1,0:T(8,128)(2,1)S(1)}, bf16[256,256]{1,0:T(8,128)(2,1)S(1)}, u32[]{:S(2)}, u32[]{:S(2)}) collective-permute-start(bf16[256,256]{1,0:T(8,128)(2,1)S(1)} %get-tuple-element.42), channel_id=1, source_target_pairs={{0,64},{64,128},{128,192},{192,0},{1,65},{65,129},{129,193},{193,1... | collective-permute-start | bytes 393224 | tf_op jit(solution)/shard_map/ppermute | solution.py:525
  62.7 2.3 %collective-permute-done.3.q1 = bf16[256,256]{1,0:T(8,128)(2,1)S(1)} collective-permute-done((bf16[256,256]{1,0:T(8,128)(2,1)S(1)}, bf16[256,256]{1,0:T(8,128)(2,1)S(1)}, u32[]{:S(2)}, u32[]{:S(2)}) %collective-permute-start.3) | collective-permute-done | bytes 131104 | tf_op jit(solution)/shard_map/ppermute | solution.py:525
  65.2 2.3 %collective-permute-done.5.q3 = bf16[256,256]{1,0:T(8,128)(2,1)S(1)} collective-permute-done((bf16[256,256]{1,0:T(8,128)(2,1)S(1)}, bf16[256,256]{1,0:T(8,128)(2,1)S(1)}, u32[]{:S(2)}, u32[]{:S(2)}) %collective-permute-start.5) | collective-permute-done | bytes 131104 | tf_op jit(solution)/shard_map/ppermute | solution.py:525
  68.5 1.5 %collective-permute-start.6 = (bf16[256,256]{1,0:T(8,128)(2,1)S(1)}, bf16[256,256]{1,0:T(8,128)(2,1)S(1)}, u32[]{:S(2)}, u32[]{:S(2)}) collective-permute-start(bf16[256,256]{1,0:T(8,128)(2,1)S(1)} %get-tuple-element.49.v0), channel_id=1, source_target_pairs={{0,128},{64,192},{128,0},{192,64},{1,129},{65,193},{129,1},{193,65... | collective-permute-start | bytes 393224 | tf_op jit(solution)/shard_map/ppermute | solution.py:525
  70.0 1.2 collective-permute-start.7
  72.0 4.4 %collective-permute-done.6.v1 = bf16[256,256]{1,0:T(8,128)(2,1)S(1)} collective-permute-done((bf16[256,256]{1,0:T(8,128)(2,1)S(1)}, bf16[256,256]{1,0:T(8,128)(2,1)S(1)}, u32[]{:S(2)}, u32[]{:S(2)}) %collective-permute-start.6) | collective-permute-done | bytes 131104 | tf_op jit(solution)/shard_map/ppermute | solution.py:525
  76.5 1.7 %collective-permute-done.8.v3 = bf16[256,256]{1,0:T(8,128)(2,1)S(1)} collective-permute-done((bf16[256,256]{1,0:T(8,128)(2,1)S(1)}, bf16[256,256]{1,0:T(8,128)(2,1)S(1)}, u32[]{:S(2)}, u32[]{:S(2)}) %collective-permute-start.8) | collective-permute-done | bytes 131104 | tf_op jit(solution)/shard_map/ppermute | solution.py:525
  78.1 1.5 %shard_map.102 = (bf16[256,1024]{1,0:T(8,128)(2,1)S(1)}, bf16[32,40,128]{2,1,0:T(8,128)(2,1)S(1)}, bf16[32,40,128]{2,1,0:T(8,128)(2,1)S(1)}) custom-call(s32[3]{0:T(128)S(1)} %pad_add_fusion.place, bf16[1280,1024]{1,0:T(8,128)(2,1)S(1)} %get-tuple-element.34.table_ref, bf16[256,256]{1,0:T(8,128)(2,1)S(1)} %get-tuple-element.49.v0, ...), custom_call_target="tpu_custom_call" | custom-call | flops 2000000000 | bytes 2000000 | tf_op jit(solution)/shard_map/pallas_call | solution.py:510
  79.7 1.6 %collective-permute-done.9 = bf16[32,40,128]{2,1,0:T(8,128)(2,1)S(1)} collective-permute-done((bf16[32,40,128]{2,1,0:T(8,128)(2,1)S(1)}, bf16[32,40,128]{2,1,0:T(8,128)(2,1)S(1)}, u32[]{:S(2)}, u32[]{:S(2)}) %collective-permute-start.9) | collective-permute-done | bytes 327712 | tf_op jit(solution)/shard_map/ppermute | solution.py:533
  81.4 18.3 %all_to_all.22.parts_ref = bf16[32,40,128]{2,1,0:T(8,128)(2,1)S(1)} all-to-all(bf16[32,40,128]{2,1,0:T(8,128)(2,1)S(1)} %add_convert_fusion), channel_id=1, replica_groups=mesh['x'=4,'yh'=2,'yl'=2,'z'=8,'core'=2] {'yh','yl','z'}, dimensions={0} | all-to-all | bytes 655360 | tf_op jit(solution)/shard_map/all_to_all | solution.py:544
  100.4 17.9 %all_to_all.23.mine_ref = bf16[32,40,128]{2,1,0:T(8,128)(2,1)S(1)} all-to-all(bf16[32,40,128]{2,1,0:T(8,128)(2,1)S(1)} %shard_map.103), channel_id=1, replica_groups=mesh['x'=4,'yh'=2,'yl'=2,'z'=8,'core'=2] {'yh','yl','z'}, dimensions={0} | all-to-all | bytes 655360 | tf_op jit(solution)/shard_map/all_to_all | solution.py:552
  118.3 2.8 %shard_map.104 = (bf16[512,1024]{1,0:T(8,128)(2,1)S(1)}, f32[640,1024]{1,0:T(8,128)S(1)}, f32[128,1024]{1,0:T(8,128)S(1)}) custom-call(s32[3]{0:T(128)S(1)} %pad_add_fusion.place, f32[2,640,128]{2,1,0:T(8,128)S(1)} %get-tuple-element.37.weights_ref, bf16[32,40,128]{2,1,0:T(8,128)(2,1)S(1)} %all_to_all.23.mine_ref, ...), custom_call_target="tpu_custom_call" | custom-call | flops 2000000000 | bytes 2000000 | tf_op jit(solution)/shard_map/pallas_call | solution.py:510
  121.1 2.4 %shard_map.105 = (bf16[640,512]{1,0:T(8,128)(2,1)S(1)}, bf16[128,640]{1,0:T(8,128)(2,1)S(1)}, bf16[144,256]{1,0:T(8,128)(2,1)S(1)}, bf16[144,256]{1,0:T(8,128)(2,1)S(1)}, bf16[144,256]{1,0:T(8,128)(2,1)S(1)}) custom-call(s32[3]{0:T(128)S(1)} %pad_add_fusion.place, f32[2,640,128]{2,1,0:T(8,128)S(1)} %get-tuple-element.37.weights_ref, ...), custom_call_target="tpu_custom_call" | custom-call | flops 2000000000 | bytes 2000000 | tf_op jit(solution)/shard_map/pallas_call | solution.py:510
  123.5 1.6 %collective-permute-start.11 = (bf16[144,256]{1,0:T(8,128)(2,1)S(1)}, bf16[144,256]{1,0:T(8,128)(2,1)S(1)}, u32[]{:S(2)}, u32[]{:S(2)}) collective-permute-start(bf16[144,256]{1,0:T(8,128)(2,1)S(1)} %get-tuple-element.61), channel_id=1, source_target_pairs={{0,128},{64,192},{128,0},{192,64},{1,129},{65,193},{129,1},{193,65... | collective-permute-start | bytes 221192 | tf_op jit(solution)/shard_map/ppermute | solution.py:525
  125.2 1.2 collective-permute-start.12
  127.2 1.2 shard_map.106.q0
  128.4 1.5 %collective-permute-done.11.q1 = bf16[144,256]{1,0:T(8,128)(2,1)S(1)} collective-permute-done((bf16[144,256]{1,0:T(8,128)(2,1)S(1)}, bf16[144,256]{1,0:T(8,128)(2,1)S(1)}, u32[]{:S(2)}, u32[]{:S(2)}) %collective-permute-start.11) | collective-permute-done | bytes 73760 | tf_op jit(solution)/shard_map/ppermute | solution.py:525
  129.9 2.0 %collective-permute-done.13.q3 = bf16[144,256]{1,0:T(8,128)(2,1)S(1)} collective-permute-done((bf16[144,256]{1,0:T(8,128)(2,1)S(1)}, bf16[144,256]{1,0:T(8,128)(2,1)S(1)}, u32[]{:S(2)}, u32[]{:S(2)}) %collective-permute-start.13) | collective-permute-done | bytes 73760 | tf_op jit(solution)/shard_map/ppermute | solution.py:525
  131.9 1.4 %shard_map.107 = (bf16[256,128]{1,0:T(8,128)(2,1)}, f32[3,256]{1,0:T(4,128)}) custom-call(s32[3]{0:T(128)S(1)} %pad_add_fusion.place, bf16[144,256]{1,0:T(8,128)(2,1)S(1)} %shard_map.106.q0, bf16[144,256]{1,0:T(8,128)(2,1)S(1)} %collective-permute-done.11.q1, bf16[144,256]{1,0:T(8,128)(2,1)S(1)} %collective-permute-done.12.q2, ...), custom_call_target="tpu_custom_call" | custom-call | flops 2000000000 | bytes 2000000 | tf_op jit(solution)/shard_map/pallas_call | solution.py:510
  (42 shorter events, 8.9 us)
Async XLA Ops:
  0.7 4.8 %copy-start.7 = (s32[3,512]{1,0:T(4,128)S(1)}, s32[3,512]{1,0:T(4,128)}, u32[]{:S(2)}) copy-start(s32[3,512]{1,0:T(4,128)} %param.11) | copy-start | bytes 18436
  5.4 1.7 %collective-permute-start = (bf16[32,40,128]{2,1,0:T(8,128)(2,1)S(1)}, bf16[32,40,128]{2,1,0:T(8,128)(2,1)S(1)}, u32[]{:S(2)}, u32[]{:S(2)}) collective-permute-start(bf16[32,40,128]{2,1,0:T(8,128)(2,1)S(1)} %get-tuple-element.36), channel_id=1, source_target_pairs={{0,1},{1,0},{2,3},{3,2},{4,5},{5,4},{6,7},{7,6},{8,9},{9,8},{10,11... | collective-permute-start | bytes 983048 | tf_op jit(solution)/shard_map/ppermute | solution.py:533
  5.5 0.7 collective-permute-start.1
  53.9 2.0 %collective-permute-start.2 = (bf16[32,40,128]{2,1,0:T(8,128)(2,1)S(1)}, bf16[32,40,128]{2,1,0:T(8,128)(2,1)S(1)}, u32[]{:S(2)}, u32[]{:S(2)}) collective-permute-start(bf16[32,40,128]{2,1,0:T(8,128)(2,1)S(1)} %all_to_all.21.mine_ref), channel_id=1, source_target_pairs={{0,1},{1,0},{2,3},{3,2},{4,5},{5,4},{6,7},{7,6},{8,9},{9,8},{10,11... | collective-permute-start | bytes 983048 | tf_op jit(solution)/shard_map/ppermute | solution.py:533
  57.1 4.5 %copy-start = (bf16[2048,128]{1,0:T(8,128)(2,1)S(1)}, bf16[2048,128]{1,0:T(8,128)(2,1)}, u32[]{:S(2)}) copy-start(bf16[2048,128]{1,0:T(8,128)(2,1)} %features_ref.1) | copy-start | bytes 1572868
  57.1 4.5 %copy-start.1 = (bf16[2048,128]{1,0:T(8,128)(2,1)S(1)}, bf16[2048,128]{1,0:T(8,128)(2,1)}, u32[]{:S(2)}) copy-start(bf16[2048,128]{1,0:T(8,128)(2,1)} %upstream_ref.1) | copy-start | bytes 1572868
  57.1 4.5 %copy-start.2 = (bf16[2,128,128]{2,1,0:T(8,128)(2,1)S(1)}, bf16[2,128,128]{2,1,0:T(8,128)(2,1)}, u32[]{:S(2)}) copy-start(bf16[2,128,128]{2,1,0:T(8,128)(2,1)} %inward_ref.1) | copy-start | bytes 196612
  57.1 4.5 %copy-start.3 = (s32[2048]{0:T(1024)S(1)}, s32[2048]{0:T(1024)}, u32[]{:S(2)}) copy-start(s32[2048]{0:T(1024)} %param.10) | copy-start | bytes 24580
  57.1 4.5 %copy-start.4 = (f32[2,6,128]{2,0,1:T(2,128)S(1)}, f32[2,6,128]{2,0,1:T(2,128)}, u32[]{:S(2)}) copy-start(f32[2,6,128]{2,0,1:T(2,128)} %param.14) | copy-start | bytes 18436
  57.1 7.9 %collective-permute-start.3 = (bf16[256,256]{1,0:T(8,128)(2,1)S(1)}, bf16[256,256]{1,0:T(8,128)(2,1)S(1)}, u32[]{:S(2)}, u32[]{:S(2)}) collective-permute-start(bf16[256,256]{1,0:T(8,128)(2,1)S(1)} %get-tuple-element.41), channel_id=1, source_target_pairs={{0,128},{64,192},{128,0},{192,64},{1,129},{65,193},{129,1},{193,65... | collective-permute-start | bytes 393224 | tf_op jit(solution)/shard_map/ppermute | solution.py:525
  58.6 6.6 %collective-permute-start.4 = (bf16[256,256]{1,0:T(8,128)(2,1)S(1)}, bf16[256,256]{1,0:T(8,128)(2,1)S(1)}, u32[]{:S(2)}, u32[]{:S(2)}) collective-permute-start(bf16[256,256]{1,0:T(8,128)(2,1)S(1)} %get-tuple-element.42), channel_id=1, source_target_pairs={{0,64},{64,128},{128,192},{192,0},{1,65},{65,129},{129,193},{193,1... | collective-permute-start | bytes 393224 | tf_op jit(solution)/shard_map/ppermute | solution.py:525
  60.7 6.8 %collective-permute-start.5 = (bf16[256,256]{1,0:T(8,128)(2,1)S(1)}, bf16[256,256]{1,0:T(8,128)(2,1)S(1)}, u32[]{:S(2)}, u32[]{:S(2)}) collective-permute-start(bf16[256,256]{1,0:T(8,128)(2,1)S(1)} %get-tuple-element.43), channel_id=1, source_target_pairs={{0,192},{64,0},{128,64},{192,128},{1,193},{65,1},{129,65},{193,129... | collective-permute-start | bytes 393224 | tf_op jit(solution)/shard_map/ppermute | solution.py:525
  60.7 6.8 %copy-start.5 = (bf16[2,128,128]{2,1,0:T(8,128)(2,1)S(1)}, bf16[2,128,128]{2,1,0:T(8,128)(2,1)}, u32[]{:S(2)}) copy-start(bf16[2,128,128]{2,1,0:T(8,128)(2,1)} %outward_ref.1) | copy-start | bytes 196612
  68.5 7.9 %collective-permute-start.6 = (bf16[256,256]{1,0:T(8,128)(2,1)S(1)}, bf16[256,256]{1,0:T(8,128)(2,1)S(1)}, u32[]{:S(2)}, u32[]{:S(2)}) collective-permute-start(bf16[256,256]{1,0:T(8,128)(2,1)S(1)} %get-tuple-element.49.v0), channel_id=1, source_target_pairs={{0,128},{64,192},{128,0},{192,64},{1,129},{65,193},{129,1},{193,65... | collective-permute-start | bytes 393224 | tf_op jit(solution)/shard_map/ppermute | solution.py:525
  70.0 6.5 %collective-permute-start.7 = (bf16[256,256]{1,0:T(8,128)(2,1)S(1)}, bf16[256,256]{1,0:T(8,128)(2,1)S(1)}, u32[]{:S(2)}, u32[]{:S(2)}) collective-permute-start(bf16[256,256]{1,0:T(8,128)(2,1)S(1)} %get-tuple-element.49.v0), channel_id=1, source_target_pairs={{0,64},{64,128},{128,192},{192,0},{1,65},{65,129},{129,193},{193,1... | collective-permute-start | bytes 393224 | tf_op jit(solution)/shard_map/ppermute | solution.py:525
  71.1 7.0 %collective-permute-start.8 = (bf16[256,256]{1,0:T(8,128)(2,1)S(1)}, bf16[256,256]{1,0:T(8,128)(2,1)S(1)}, u32[]{:S(2)}, u32[]{:S(2)}) collective-permute-start(bf16[256,256]{1,0:T(8,128)(2,1)S(1)} %get-tuple-element.49.v0), channel_id=1, source_target_pairs={{0,192},{64,0},{128,64},{192,128},{1,193},{65,1},{129,65},{193,129... | collective-permute-start | bytes 393224 | tf_op jit(solution)/shard_map/ppermute | solution.py:525
  79.6 1.8 %copy-start.6 = (bf16[256,1024]{1,0:T(8,128)(2,1)}, bf16[256,1024]{1,0:T(8,128)(2,1)S(1)}, u32[]{:S(2)}) copy-start(bf16[256,1024]{1,0:T(8,128)(2,1)S(1)} %get-tuple-element.55.second_hbm) | copy-start | bytes 1572868
  79.6 1.7 %collective-permute-start.9 = (bf16[32,40,128]{2,1,0:T(8,128)(2,1)S(1)}, bf16[32,40,128]{2,1,0:T(8,128)(2,1)S(1)}, u32[]{:S(2)}, u32[]{:S(2)}) collective-permute-start(bf16[32,40,128]{2,1,0:T(8,128)(2,1)S(1)} %get-tuple-element.51), channel_id=1, source_target_pairs={{0,1},{1,0},{2,3},{3,2},{4,5},{5,4},{6,7},{7,6},{8,9},{9,8},{10,11... | collective-permute-start | bytes 983048 | tf_op jit(solution)/shard_map/ppermute | solution.py:533
  118.3 2.8 %collective-permute-start.10 = (bf16[32,40,128]{2,1,0:T(8,128)(2,1)S(1)}, bf16[32,40,128]{2,1,0:T(8,128)(2,1)S(1)}, u32[]{:S(2)}, u32[]{:S(2)}) collective-permute-start(bf16[32,40,128]{2,1,0:T(8,128)(2,1)S(1)} %all_to_all.23.mine_ref), channel_id=1, source_target_pairs={{0,1},{1,0},{2,3},{3,2},{4,5},{5,4},{6,7},{7,6},{8,9},{9,8},{10,11... | collective-permute-start | bytes 983048 | tf_op jit(solution)/shard_map/ppermute | solution.py:533
  123.5 6.4 %collective-permute-start.11 = (bf16[144,256]{1,0:T(8,128)(2,1)S(1)}, bf16[144,256]{1,0:T(8,128)(2,1)S(1)}, u32[]{:S(2)}, u32[]{:S(2)}) collective-permute-start(bf16[144,256]{1,0:T(8,128)(2,1)S(1)} %get-tuple-element.61), channel_id=1, source_target_pairs={{0,128},{64,192},{128,0},{192,64},{1,129},{65,193},{129,1},{193,65... | collective-permute-start | bytes 221192 | tf_op jit(solution)/shard_map/ppermute | solution.py:525
  125.2 4.7 %collective-permute-start.12 = (bf16[144,256]{1,0:T(8,128)(2,1)S(1)}, bf16[144,256]{1,0:T(8,128)(2,1)S(1)}, u32[]{:S(2)}, u32[]{:S(2)}) collective-permute-start(bf16[144,256]{1,0:T(8,128)(2,1)S(1)} %get-tuple-element.62), channel_id=1, source_target_pairs={{0,64},{64,128},{128,192},{192,0},{1,65},{65,129},{129,193},{193,1... | collective-permute-start | bytes 221192 | tf_op jit(solution)/shard_map/ppermute | solution.py:525
  126.4 5.6 %collective-permute-start.13 = (bf16[144,256]{1,0:T(8,128)(2,1)S(1)}, bf16[144,256]{1,0:T(8,128)(2,1)S(1)}, u32[]{:S(2)}, u32[]{:S(2)}) collective-permute-start(bf16[144,256]{1,0:T(8,128)(2,1)S(1)} %get-tuple-element.63), channel_id=1, source_target_pairs={{0,192},{64,0},{128,64},{192,128},{1,193},{65,1},{129,65},{193,129... | collective-permute-start | bytes 221192 | tf_op jit(solution)/shard_map/ppermute | solution.py:525

commit v6 on v5

--- a/solution.py
+++ b/solution.py
@@ -91,15 +91,18 @@
     return series(COS_SERIES, square), turns * series(SIN_SERIES, square)
 
 
-def write_pieces(place, total_ref, keep_ref, send_ref):
-    core = place[2]
-    for target, half in ((keep_ref, core), (send_ref, 1 - core)):
-        for index in range(PIECES):
-            row, side = index // 2, index % 2
-            start = pl.multiple_of(half * SLAB + row * ROWS, 8)
-            target[index] = total_ref[
-                pl.ds(start, ROWS), side * CHANNELS : (side + 1) * CHANNELS
-            ].astype(BF16)
+def write_half(half, table_ref, values_ref, pieces_ref, total_ref):
+    total_ref[...] = matmul(table_ref[half_rows(half), :], values_ref[...], 1, 1)
+    total_ref[SLAB - 8 :, :CHANNELS] = jnp.zeros((8, CHANNELS), F32)
+    for index in range(PIECES):
+        row, side = index // 2, index % 2
+        pieces_ref[index] = total_ref[
+            row * ROWS : (row + 1) * ROWS, side * CHANNELS : (side + 1) * CHANNELS
+        ].astype(BF16)
+
+
+def keep_kernel(place, table_ref, values_ref, keep_ref, total_ref):
+    write_half(place[2], table_ref, values_ref, keep_ref, total_ref)
 
 
 def weigh_pieces(pieces_ref, weights_ref, first, total_ref):
@@ -129,10 +132,8 @@
     outward_hbm,
     multiplier_hbm,
     table_ref,
-    values_hbm,
     keep_ref,
     send_ref,
-    values_ref,
     coordinates_ref,
     labels_ref,
     features_ref,
@@ -204,21 +205,19 @@
             table_ref[SLAB + start : SLAB + stop, columns] = sine.astype(BF16)
     for copy in copies[1:]:
         copy.wait()
-    inward = flip(inward_ref[0])
-    for index, block in enumerate(blocks):
+    atoms = (SLABS * BLOCK, CHANNELS)
+    charges = matmul(flip(inward_ref[0]), features_ref[...].reshape(atoms), 1, 1)
+    grad_pot = matmul(outward_ref[1], upstream_ref[...].reshape(atoms), 1, 1).astype(BF16)
+    for block in range(SLABS):
         labels = labels_ref[:, pl.ds(pl.multiple_of((2 * block + place[1]) * BLOCK, BLOCK), BLOCK)]
         gains = gain_columns(multiplier_ref[:, 0, :], labels)
-        charges = matmul(inward, features_ref[block], 1, 1) * gains
-        grad_pot = matmul(outward_ref[1], upstream_ref[block], 1, 1)
-        values_ref[:CHANNELS, slot(index)] = charges.astype(BF16)
-        values_ref[CHANNELS:, slot(index)] = grad_pot.astype(BF16)
-    leaving = pltpu.make_async_copy(values_ref, values_hbm, arrivals.at[len(copies)])
-    leaving.start()
-    total_ref[...] = matmul(table_ref[...], values_ref[...], 1, 1)
-    for half in range(2):
-        total_ref[(half + 1) * SLAB - 8 : (half + 1) * SLAB, :CHANNELS] = jnp.zeros((8, CHANNELS), F32)
-    write_pieces(place, total_ref, keep_ref, send_ref)
-    leaving.wait()
+        target = lax.rem(block - place[0] + SLABS, SLABS)
+        columns = pl.ds(pl.multiple_of(target * BLOCK, BLOCK), BLOCK)
+        table_ref[TABLE : TABLE + CHANNELS, columns] = (charges[:, slot(block)] * gains).astype(BF16)
+        table_ref[TABLE + CHANNELS :, columns] = grad_pot[:, slot(block)]
+    values_ref = table_ref.at[TABLE:]
+    write_half(1 - place[2], table_ref, values_ref, send_ref, total_ref)
+    write_half(place[2], table_ref, values_ref, keep_ref, total_ref)
 
 
 def counts_kernel(copies, place, momenta_ref, counts_ref):
@@ -338,23 +337,20 @@
     values_ref[:CHANNELS] = (matmul(flipped_ref[1], hidden, 1, 1) * gains_ref[...]).astype(BF16)
 
 
-def second_kernel(place, table_ref, v0, v1, v2, v3, values_ref, keep_ref, send_ref, total_ref):
+def second_kernel(place, table_ref, v0, v1, v2, v3, values_ref, send_ref, total_ref):
     for index, source in zip((0, *LAST_FAR), (v0, v1, v2, v3)):
         values_ref[:, slot(index)] = source[...]
-    total_ref[...] = matmul(table_ref[...], values_ref[...], 1, 1)
-    write_pieces(place, total_ref, keep_ref, send_ref)
-
-
-def half_theta(half, table_ref, columns, pairs, values):
+    write_half(1 - place[2], table_ref, values_ref, send_ref, total_ref)
+
+
+def half_theta(half, table_ref, columns, along):
     sign = (2 * half - 1).astype(F32)
-    along = matmul(pairs, values, 1, 0)
     return (sign * table_ref[half_rows(1 - half), columns].astype(F32)) * along
 
 
-def write_pairs(total_ref, fields_ref, pairs_ref):
+def write_pairs(total_ref, pairs_ref):
     pairs_ref[:, :CHANNELS] = total_ref[:, CHANNELS:].astype(BF16)
     pairs_ref[:, CHANNELS : 2 * CHANNELS] = total_ref[:, :CHANNELS].astype(BF16)
-    pairs_ref[:, 2 * CHANNELS :] = fields_ref[...]
 
 
 def first_gradient_kernel(
@@ -363,7 +359,6 @@
     mine_ref,
     table_ref,
     fields_hbm,
-    first_hbm,
     second_hbm,
     values_ref,
     theta_ref,
@@ -374,46 +369,45 @@
     arrivals,
 ):
     copies = [
-        pltpu.make_async_copy(source, target, arrivals.at[index])
-        for index, (source, target) in enumerate(
-            (
-                (fields_hbm, fields_ref),
-                (first_hbm, values_ref.at[:BLOCK]),
-                (second_hbm, values_ref.at[BLOCK:]),
-            )
-        )
+        pltpu.make_async_copy(fields_hbm, fields_ref, arrivals.at[0]),
+        pltpu.make_async_copy(second_hbm, values_ref.at[BLOCK:], arrivals.at[1]),
     ]
     for copy in copies:
         copy.start()
     weigh_pieces(mine_ref, weights_ref, 1, total_ref)
+    write_pairs(total_ref, pairs_ref)
     flipped = jnp.transpose(total_ref[:, CHANNELS:]).astype(BF16)
     charge_ref[...] = matmul(flipped, table_ref[half_rows(place[2]), :], 1, 0)
+    values_ref[:BLOCK] = table_ref[TABLE:]
+    for index in range(SLABS):
+        columns = slot(index)
+        along = matmul(pairs_ref[...], table_ref[TABLE:, columns], 1, 0)
+        theta_ref[:, columns] = half_theta(place[2], table_ref, columns, along)
     for copy in copies:
         copy.wait()
-    write_pairs(total_ref, fields_ref, pairs_ref)
     for index in range(SLABS):
         columns = slot(index)
-        theta_ref[:, columns] = half_theta(
-            place[2], table_ref, columns, pairs_ref[...], values_ref[:, columns]
-        )
+        along = matmul(fields_ref[...], values_ref[BLOCK:, columns], 1, 0)
+        theta_ref[:, columns] += half_theta(place[2], table_ref, columns, along)
 
 
 def finish_gradient(
     index, place, table_ref, pairs_ref, flipped_ref, values_ref, theta_ref, charge_ref, directions, target
 ):
     columns = slot(index)
-    theta = half_theta(1 - place[2], table_ref, columns, pairs_ref[...], values_ref[:, columns])
+    pairs = pairs_ref[...]
+    theta = theta_ref[:, columns] + half_theta(
+        1 - place[2], table_ref, columns, matmul(pairs, values_ref[:, columns], 1, 0)
+    )
     charge = matmul(flipped_ref[...], table_ref[half_rows(1 - place[2]), columns], 1, 0)
-    position = matmul(directions, (theta + theta_ref[:, columns]).astype(BF16), 1, 0)
     target[:CHANNELS] = (charge + charge_ref[:, columns]).astype(BF16)
-    target[CHANNELS:] = (position * (2.0 * math.pi / BOX_LENGTH)).astype(BF16)
-
-
-def class_directions(place):
-    vectors = class_vectors(place[0] * STRIDE, (16, SLAB), 1)
-    row = lax.broadcasted_iota(jnp.int32, (16, SLAB), 0)
-    directions = jnp.where(row == 0, vectors[0], jnp.where(row == 1, vectors[1], vectors[2]))
-    return jnp.where(row < 3, directions, 0.0).astype(BF16)
+    for side in range(BLOCK // CHANNELS):
+        part = slice(side * CHANNELS, (side + 1) * CHANNELS)
+        sums = [
+            jnp.sum(direction * theta[:, part], axis=0, keepdims=True) for direction in directions
+        ]
+        position = jnp.concatenate(sums + [jnp.zeros((13, CHANNELS), F32)], axis=0)
+        target[CHANNELS:, part] = (position * (2.0 * math.pi / BOX_LENGTH)).astype(BF16)
 
 
 def gradient_kernel(
@@ -433,9 +427,10 @@
     total_ref,
 ):
     weigh_pieces(other_ref, weights_ref, 1, total_ref)
-    write_pairs(total_ref, fields_ref, pairs_ref)
+    write_pairs(total_ref, pairs_ref)
+    pairs_ref[:, 2 * CHANNELS :] = fields_ref[...]
     flipped_ref[...] = jnp.transpose(total_ref[:, CHANNELS:]).astype(BF16)
-    directions = class_directions(place)
+    directions = class_vectors(place[0] * STRIDE, (SLAB, CHANNELS), 0)
     rest = (place, table_ref, pairs_ref, flipped_ref, values_ref, theta_ref, charge_ref, directions)
     for index, target in ((2, o2), (1, o1), (3, o3)):
         finish_gradient(index, *rest, target)
@@ -445,7 +440,8 @@
     place, table_ref, pairs_ref, flipped_ref, values_ref, theta_ref, charge_ref, o0
 ):
     rest = (place, table_ref, pairs_ref, flipped_ref, values_ref, theta_ref, charge_ref)
-    finish_gradient(0, *rest, class_directions(place), o0)
+    directions = class_vectors(place[0] * STRIDE, (SLAB, CHANNELS), 0)
+    finish_gradient(0, *rest, directions, o0)
 
 
 def sum_kernel(place, parts_ref, spread_ref):
@@ -602,27 +598,24 @@
     ]
     local = [shape_of(value.shape, value.dtype) for value in operands]
     local[2] = local[3] = shape_of((SLABS, BLOCK, CHANNELS), BF16)
-    table, values_one, keep, send = call_whole(
+    table, keep, send = call_whole(
         tables_kernel,
         (
-            pltpu.VMEM((TABLE, atoms_here), BF16),
-            pltpu.HBM((BLOCK, atoms_here), BF16),
+            pltpu.VMEM((TABLE + BLOCK, atoms_here), BF16),
             pieces_shape,
             pieces_shape,
         ),
-        [pltpu.VMEM((BLOCK, atoms_here), BF16)]
-        + [pltpu.VMEM(value.shape, value.dtype) for value in local]
+        [pltpu.VMEM(value.shape, value.dtype) for value in local]
         + [
-            pltpu.VMEM((TABLE, BLOCK), F32),
+            pltpu.VMEM((SLAB, BLOCK), F32),
             pltpu.VMEM((SLAB, atoms_here), F32),
             pltpu.VMEM((SLAB, atoms_here), F32),
             pltpu.VMEM((SLAB - LEAP, CHANNELS), F32),
-            pltpu.SemaphoreType.DMA((len(operands) + 1,)),
+            pltpu.SemaphoreType.DMA((len(operands),)),
         ],
         place,
         [far(value) for value in operands],
         spaces=[pltpu.HBM] * len(operands),
-        out_spaces=[pltpu.VMEM, pltpu.HBM, pltpu.VMEM, pltpu.VMEM],
         micros=7,
     )
     (counts,) = call_whole(
@@ -699,12 +692,20 @@
         [*arrived, own_features, own_upstream, gains_two, inward_flipped, latent_to_feature_matrix],
     )
     seconds = spread_out(lambda shift: shifted(values_own, SLABS - shift), values_own, LAST_FAR)
-    values_two, keep, send = call_whole(
+    values_two, send = call_whole(
         second_kernel,
-        [shape_of((BLOCK, atoms_here), BF16), pieces_shape, pieces_shape],
-        [pltpu.VMEM((TABLE, BLOCK), F32)],
+        [shape_of((BLOCK, atoms_here), BF16), pieces_shape],
+        [pltpu.VMEM((SLAB, BLOCK), F32)],
         place,
         [near(table), *seconds],
+    )
+    (keep,) = call_whole(
+        keep_kernel,
+        [pieces_shape],
+        [pltpu.VMEM((SLAB, BLOCK), F32)],
+        place,
+        [near(table), near(values_two)],
+        micros=0.1,
     )
     mine, other = sum_fields(place, add_halves(keep, send))
     result_shape = shape_of((CHANNELS + 16, BLOCK), BF16)
@@ -718,13 +719,13 @@
         ],
         [
             pltpu.VMEM(half, F32),
-            pltpu.VMEM((SLAB, 2 * BLOCK), BF16),
             pltpu.VMEM(half, BF16),
-            pltpu.SemaphoreType.DMA((3,)),
+            pltpu.VMEM(half, BF16),
+            pltpu.SemaphoreType.DMA((2,)),
         ],
         place,
-        [weights, mine, near(table), far(fields_mine), far(values_one), far(values_two)],
-        spaces=[pltpu.VMEM] * 3 + [pltpu.HBM] * 3,
+        [weights, mine, near(table), far(fields_mine), far(values_two)],
+        spaces=[pltpu.VMEM] * 3 + [pltpu.HBM] * 2,
     )
     pairs, flipped, o2, o1, o3 = call_whole(
         gradient_kernel,

time: 134 us -> 132 us (0.985)
    pallas_call x12 -> x13, Pallas kernels: 20.3 us -> 19.8 us  [call_whole(): pl.pallas_call(kernel, in_specs=[pl.BlockSpec(memory_space=pltpu.SMEM)] +...]
where the time goes in v6:
time: 132 us
  blocking collectives  82.9 us (63%)
  Pallas kernels  21 us (16%)
  waiting for transfers between devices  15.1 us (11%)
  starting transfers between devices  11.6 us (9%)
    all_to_all x2, blocking collectives, sum_fields(): parts = lax.all_to_all(part, ATOM_REST, 0, 0, tiled=True)  48.4 us
    all_to_all x2, blocking collectives, sum_fields(): mine = lax.all_to_all(spread, ATOM_REST, 0, 0, tiled=True)  34.5 us
    pallas_call x13, Pallas kernels, call_whole(): pl.pallas_call(kernel, in_specs=[pl.BlockSpec(memory_space=pltpu.SMEM)] +...  19.8 us
    ppermute x9, waiting for transfers between devices, shifted(): lax.ppermute(value, 'x', [(i, (i + shift) % SLABS) for i in range(SLABS)])  14.5 us
    ppermute x9, starting transfers between devices, shifted(): lax.ppermute(value, 'x', [(i, (i + shift) % SLABS) for i in range(SLABS)])  10.7 us
  transfers between devices with their start and end apart: 14, of which 9 were waited for; matrix products, arithmetic and copies ran while one was open for 0% of the time, Pallas kernels for 7%

profile of v6, /device:TPU:6, one launch (start us, length us, event | category | flops | bytes accessed | tf_op | source)
XLA Modules:
  0.0 131.9 jit_solution(9699728849646531410)
XLA Ops:
  0.7 4.6 %shard_map.95 = (bf16[1536,1024]{1,0:T(8,128)(2,1)S(1)}, bf16[32,40,128]{2,1,0:T(8,128)(2,1)S(1)}, bf16[32,40,128]{2,1,0:T(8,128)(2,1)S(1)}) custom-call(s32[3]{0:T(128)S(1)} %pad_add_fusion.place, f32[3,2048]{1,0:T(4,128)} %coordinates_hbm.1, s32[1,2048]{1,0:T(1,128)} %bitcast.9, bf16[4,2,256,128]{3,2,1,0:T(8,128)(2,1)} %bitcast.7, ...), custom_call_target="tpu_custom_call" | custom-call | flops 7000000000 | bytes 7000000 | tf_op jit(solution)/shard_map/pallas_call | solution.py:506
  7.2 30.0 %all_to_all.20 = bf16[32,40,128]{2,1,0:T(8,128)(2,1)S(1)} all-to-all(bf16[32,40,128]{2,1,0:T(8,128)(2,1)S(1)} %add_convert_fusion.1), channel_id=1, replica_groups=mesh['x'=4,'yh'=2,'yl'=2,'z'=8,'core'=2] {'yh','yl','z'}, dimensions={0} | all-to-all | bytes 655360 | tf_op jit(solution)/shard_map/all_to_all | solution.py:540
  37.4 16.6 %all_to_all.21.mine_ref = bf16[32,40,128]{2,1,0:T(8,128)(2,1)S(1)} all-to-all(bf16[32,40,128]{2,1,0:T(8,128)(2,1)S(1)} %broadcast_in_dim.10), channel_id=1, replica_groups=mesh['x'=4,'yh'=2,'yl'=2,'z'=8,'core'=2] {'yh','yl','z'}, dimensions={0} | all-to-all | bytes 655360 | tf_op jit(solution)/shard_map/all_to_all | solution.py:548
  53.9 2.0 %shard_map.97 = (f32[2,640,128]{2,1,0:T(8,128)S(1)}, bf16[640,256]{1,0:T(8,128)(2,1)}, f32[256,1024]{1,0:T(8,128)S(1)}) custom-call(s32[3]{0:T(128)S(1)} %pad_add_fusion.place, bf16[32,40,128]{2,1,0:T(8,128)(2,1)S(1)} %all_to_all.21.mine_ref, bf16[1536,1024]{1,0:T(8,128)(2,1)S(1)} %get-tuple-element.32.table_ref), custom_call_target="tpu_custom_call" | custom-call | flops 2000000000 | bytes 2000000 | tf_op jit(solution)/shard_map/pallas_call | solution.py:506
  56.0 1.1 shard_map.98
  57.2 1.5 %collective-permute-start.3 = (bf16[256,256]{1,0:T(8,128)(2,1)S(1)}, bf16[256,256]{1,0:T(8,128)(2,1)S(1)}, u32[]{:S(2)}, u32[]{:S(2)}) collective-permute-start(bf16[256,256]{1,0:T(8,128)(2,1)S(1)} %get-tuple-element.39), channel_id=1, source_target_pairs={{0,128},{64,192},{128,0},{192,64},{1,129},{65,193},{129,1},{193,65... | collective-permute-start | bytes 393224 | tf_op jit(solution)/shard_map/ppermute | solution.py:521
  58.6 2.1 %collective-permute-start.4 = (bf16[256,256]{1,0:T(8,128)(2,1)S(1)}, bf16[256,256]{1,0:T(8,128)(2,1)S(1)}, u32[]{:S(2)}, u32[]{:S(2)}) collective-permute-start(bf16[256,256]{1,0:T(8,128)(2,1)S(1)} %get-tuple-element.40), channel_id=1, source_target_pairs={{0,64},{64,128},{128,192},{192,0},{1,65},{65,129},{129,193},{193,1... | collective-permute-start | bytes 393224 | tf_op jit(solution)/shard_map/ppermute | solution.py:521
  61.6 1.1 shard_map.100
  62.7 2.3 %collective-permute-done.3.q1 = bf16[256,256]{1,0:T(8,128)(2,1)S(1)} collective-permute-done((bf16[256,256]{1,0:T(8,128)(2,1)S(1)}, bf16[256,256]{1,0:T(8,128)(2,1)S(1)}, u32[]{:S(2)}, u32[]{:S(2)}) %collective-permute-start.3) | collective-permute-done | bytes 131104 | tf_op jit(solution)/shard_map/ppermute | solution.py:521
  65.3 2.3 %collective-permute-done.5.q3 = bf16[256,256]{1,0:T(8,128)(2,1)S(1)} collective-permute-done((bf16[256,256]{1,0:T(8,128)(2,1)S(1)}, bf16[256,256]{1,0:T(8,128)(2,1)S(1)}, u32[]{:S(2)}, u32[]{:S(2)}) %collective-permute-start.5) | collective-permute-done | bytes 131104 | tf_op jit(solution)/shard_map/ppermute | solution.py:521
  68.6 1.4 %collective-permute-start.6 = (bf16[256,256]{1,0:T(8,128)(2,1)S(1)}, bf16[256,256]{1,0:T(8,128)(2,1)S(1)}, u32[]{:S(2)}, u32[]{:S(2)}) collective-permute-start(bf16[256,256]{1,0:T(8,128)(2,1)S(1)} %get-tuple-element.47.v0), channel_id=1, source_target_pairs={{0,128},{64,192},{128,0},{192,64},{1,129},{65,193},{129,1},{193,65... | collective-permute-start | bytes 393224 | tf_op jit(solution)/shard_map/ppermute | solution.py:521
  70.0 1.2 collective-permute-start.7
  72.0 4.5 %collective-permute-done.6.v1 = bf16[256,256]{1,0:T(8,128)(2,1)S(1)} collective-permute-done((bf16[256,256]{1,0:T(8,128)(2,1)S(1)}, bf16[256,256]{1,0:T(8,128)(2,1)S(1)}, u32[]{:S(2)}, u32[]{:S(2)}) %collective-permute-start.6) | collective-permute-done | bytes 131104 | tf_op jit(solution)/shard_map/ppermute | solution.py:521
  76.5 1.6 %collective-permute-done.8.v3 = bf16[256,256]{1,0:T(8,128)(2,1)S(1)} collective-permute-done((bf16[256,256]{1,0:T(8,128)(2,1)S(1)}, bf16[256,256]{1,0:T(8,128)(2,1)S(1)}, u32[]{:S(2)}, u32[]{:S(2)}) %collective-permute-start.8) | collective-permute-done | bytes 131104 | tf_op jit(solution)/shard_map/ppermute | solution.py:521
  81.0 18.4 %all_to_all.22.parts_ref = bf16[32,40,128]{2,1,0:T(8,128)(2,1)S(1)} all-to-all(bf16[32,40,128]{2,1,0:T(8,128)(2,1)S(1)} %add_convert_fusion), channel_id=1, replica_groups=mesh['x'=4,'yh'=2,'yl'=2,'z'=8,'core'=2] {'yh','yl','z'}, dimensions={0} | all-to-all | bytes 655360 | tf_op jit(solution)/shard_map/all_to_all | solution.py:540
  100.0 17.9 %all_to_all.23.mine_ref = bf16[32,40,128]{2,1,0:T(8,128)(2,1)S(1)} all-to-all(bf16[32,40,128]{2,1,0:T(8,128)(2,1)S(1)} %shard_map.104), channel_id=1, replica_groups=mesh['x'=4,'yh'=2,'yl'=2,'z'=8,'core'=2] {'yh','yl','z'}, dimensions={0} | all-to-all | bytes 655360 | tf_op jit(solution)/shard_map/all_to_all | solution.py:548
  117.9 2.3 %shard_map.105 = (bf16[512,1024]{1,0:T(8,128)(2,1)S(1)}, f32[640,1024]{1,0:T(8,128)S(1)}, f32[128,1024]{1,0:T(8,128)S(1)}) custom-call(s32[3]{0:T(128)S(1)} %pad_add_fusion.place, f32[2,640,128]{2,1,0:T(8,128)S(1)} %get-tuple-element.35.weights_ref, bf16[32,40,128]{2,1,0:T(8,128)(2,1)S(1)} %all_to_all.23.mine_ref, ...), custom_call_target="tpu_custom_call" | custom-call | flops 2000000000 | bytes 2000000 | tf_op jit(solution)/shard_map/pallas_call | solution.py:506
  120.2 1.9 %shard_map.106 = (bf16[640,512]{1,0:T(8,128)(2,1)S(1)}, bf16[128,640]{1,0:T(8,128)(2,1)S(1)}, bf16[144,256]{1,0:T(8,128)(2,1)S(1)}, bf16[144,256]{1,0:T(8,128)(2,1)S(1)}, bf16[144,256]{1,0:T(8,128)(2,1)S(1)}) custom-call(s32[3]{0:T(128)S(1)} %pad_add_fusion.place, f32[2,640,128]{2,1,0:T(8,128)S(1)} %get-tuple-element.35.weights_ref, ...), custom_call_target="tpu_custom_call" | custom-call | flops 2000000000 | bytes 2000000 | tf_op jit(solution)/shard_map/pallas_call | solution.py:506
  122.1 1.6 %collective-permute-start.11 = (bf16[144,256]{1,0:T(8,128)(2,1)S(1)}, bf16[144,256]{1,0:T(8,128)(2,1)S(1)}, u32[]{:S(2)}, u32[]{:S(2)}) collective-permute-start(bf16[144,256]{1,0:T(8,128)(2,1)S(1)} %get-tuple-element.57), channel_id=1, source_target_pairs={{0,128},{64,192},{128,0},{192,64},{1,129},{65,193},{129,1},{193,65... | collective-permute-start | bytes 221192 | tf_op jit(solution)/shard_map/ppermute | solution.py:521
  123.7 1.2 collective-permute-start.12
  125.7 1.1 shard_map.107.q0
  126.9 1.6 %collective-permute-done.11.q1 = bf16[144,256]{1,0:T(8,128)(2,1)S(1)} collective-permute-done((bf16[144,256]{1,0:T(8,128)(2,1)S(1)}, bf16[144,256]{1,0:T(8,128)(2,1)S(1)}, u32[]{:S(2)}, u32[]{:S(2)}) %collective-permute-start.11) | collective-permute-done | bytes 73760 | tf_op jit(solution)/shard_map/ppermute | solution.py:521
  128.5 2.0 %collective-permute-done.13.q3 = bf16[144,256]{1,0:T(8,128)(2,1)S(1)} collective-permute-done((bf16[144,256]{1,0:T(8,128)(2,1)S(1)}, bf16[144,256]{1,0:T(8,128)(2,1)S(1)}, u32[]{:S(2)}, u32[]{:S(2)}) %collective-permute-start.13) | collective-permute-done | bytes 73760 | tf_op jit(solution)/shard_map/ppermute | solution.py:521
  130.5 1.4 %shard_map.108 = (bf16[256,128]{1,0:T(8,128)(2,1)}, f32[3,256]{1,0:T(4,128)}) custom-call(s32[3]{0:T(128)S(1)} %pad_add_fusion.place, bf16[144,256]{1,0:T(8,128)(2,1)S(1)} %shard_map.107.q0, bf16[144,256]{1,0:T(8,128)(2,1)S(1)} %collective-permute-done.11.q1, bf16[144,256]{1,0:T(8,128)(2,1)S(1)} %collective-permute-done.12.q2, ...), custom_call_target="tpu_custom_call" | custom-call | flops 2000000000 | bytes 2000000 | tf_op jit(solution)/shard_map/pallas_call | solution.py:506
  (43 shorter events, 9.2 us)
Async XLA Ops:
  0.7 4.8 %copy-start.7 = (s32[3,512]{1,0:T(4,128)S(1)}, s32[3,512]{1,0:T(4,128)}, u32[]{:S(2)}) copy-start(s32[3,512]{1,0:T(4,128)} %param.11) | copy-start | bytes 18436
  5.4 1.7 %collective-permute-start = (bf16[32,40,128]{2,1,0:T(8,128)(2,1)S(1)}, bf16[32,40,128]{2,1,0:T(8,128)(2,1)S(1)}, u32[]{:S(2)}, u32[]{:S(2)}) collective-permute-start(bf16[32,40,128]{2,1,0:T(8,128)(2,1)S(1)} %get-tuple-element.34), channel_id=1, source_target_pairs={{0,1},{1,0},{2,3},{3,2},{4,5},{5,4},{6,7},{7,6},{8,9},{9,8},{10,11... | collective-permute-start | bytes 983048 | tf_op jit(solution)/shard_map/ppermute | solution.py:529
  5.5 0.7 collective-permute-start.1
  53.9 2.0 %collective-permute-start.2 = (bf16[32,40,128]{2,1,0:T(8,128)(2,1)S(1)}, bf16[32,40,128]{2,1,0:T(8,128)(2,1)S(1)}, u32[]{:S(2)}, u32[]{:S(2)}) collective-permute-start(bf16[32,40,128]{2,1,0:T(8,128)(2,1)S(1)} %all_to_all.21.mine_ref), channel_id=1, source_target_pairs={{0,1},{1,0},{2,3},{3,2},{4,5},{5,4},{6,7},{7,6},{8,9},{9,8},{10,11... | collective-permute-start | bytes 983048 | tf_op jit(solution)/shard_map/ppermute | solution.py:529
  57.1 4.5 %copy-start.1 = (bf16[2048,128]{1,0:T(8,128)(2,1)S(1)}, bf16[2048,128]{1,0:T(8,128)(2,1)}, u32[]{:S(2)}) copy-start(bf16[2048,128]{1,0:T(8,128)(2,1)} %features_ref.1) | copy-start | bytes 1572868
  57.1 4.5 %copy-start.2 = (bf16[2048,128]{1,0:T(8,128)(2,1)S(1)}, bf16[2048,128]{1,0:T(8,128)(2,1)}, u32[]{:S(2)}) copy-start(bf16[2048,128]{1,0:T(8,128)(2,1)} %upstream_ref.1) | copy-start | bytes 1572868
  57.1 4.5 %copy-start.3 = (bf16[2,128,128]{2,1,0:T(8,128)(2,1)S(1)}, bf16[2,128,128]{2,1,0:T(8,128)(2,1)}, u32[]{:S(2)}) copy-start(bf16[2,128,128]{2,1,0:T(8,128)(2,1)} %inward_ref.1) | copy-start | bytes 196612
  57.1 4.5 %copy-start.4 = (s32[2048]{0:T(1024)S(1)}, s32[2048]{0:T(1024)}, u32[]{:S(2)}) copy-start(s32[2048]{0:T(1024)} %param.10) | copy-start | bytes 24580
  57.1 4.5 %copy-start.5 = (f32[2,6,128]{2,0,1:T(2,128)S(1)}, f32[2,6,128]{2,0,1:T(2,128)}, u32[]{:S(2)}) copy-start(f32[2,6,128]{2,0,1:T(2,128)} %param.14) | copy-start | bytes 18436
  57.1 10.4 %copy-start.6 = (bf16[2,128,128]{2,1,0:T(8,128)(2,1)S(1)}, bf16[2,128,128]{2,1,0:T(8,128)(2,1)}, u32[]{:S(2)}) copy-start(bf16[2,128,128]{2,1,0:T(8,128)(2,1)} %outward_ref.1) | copy-start | bytes 196612
  57.2 7.9 %collective-permute-start.3 = (bf16[256,256]{1,0:T(8,128)(2,1)S(1)}, bf16[256,256]{1,0:T(8,128)(2,1)S(1)}, u32[]{:S(2)}, u32[]{:S(2)}) collective-permute-start(bf16[256,256]{1,0:T(8,128)(2,1)S(1)} %get-tuple-element.39), channel_id=1, source_target_pairs={{0,128},{64,192},{128,0},{192,64},{1,129},{65,193},{129,1},{193,65... | collective-permute-start | bytes 393224 | tf_op jit(solution)/shard_map/ppermute | solution.py:521
  58.6 6.6 %collective-permute-start.4 = (bf16[256,256]{1,0:T(8,128)(2,1)S(1)}, bf16[256,256]{1,0:T(8,128)(2,1)S(1)}, u32[]{:S(2)}, u32[]{:S(2)}) collective-permute-start(bf16[256,256]{1,0:T(8,128)(2,1)S(1)} %get-tuple-element.40), channel_id=1, source_target_pairs={{0,64},{64,128},{128,192},{192,0},{1,65},{65,129},{129,193},{193,1... | collective-permute-start | bytes 393224 | tf_op jit(solution)/shard_map/ppermute | solution.py:521
  60.7 6.8 %collective-permute-start.5 = (bf16[256,256]{1,0:T(8,128)(2,1)S(1)}, bf16[256,256]{1,0:T(8,128)(2,1)S(1)}, u32[]{:S(2)}, u32[]{:S(2)}) collective-permute-start(bf16[256,256]{1,0:T(8,128)(2,1)S(1)} %get-tuple-element.41), channel_id=1, source_target_pairs={{0,192},{64,0},{128,64},{192,128},{1,193},{65,1},{129,65},{193,129... | collective-permute-start | bytes 393224 | tf_op jit(solution)/shard_map/ppermute | solution.py:521
  68.6 7.9 %collective-permute-start.6 = (bf16[256,256]{1,0:T(8,128)(2,1)S(1)}, bf16[256,256]{1,0:T(8,128)(2,1)S(1)}, u32[]{:S(2)}, u32[]{:S(2)}) collective-permute-start(bf16[256,256]{1,0:T(8,128)(2,1)S(1)} %get-tuple-element.47.v0), channel_id=1, source_target_pairs={{0,128},{64,192},{128,0},{192,64},{1,129},{65,193},{129,1},{193,65... | collective-permute-start | bytes 393224 | tf_op jit(solution)/shard_map/ppermute | solution.py:521
  70.0 6.5 %collective-permute-start.7 = (bf16[256,256]{1,0:T(8,128)(2,1)S(1)}, bf16[256,256]{1,0:T(8,128)(2,1)S(1)}, u32[]{:S(2)}, u32[]{:S(2)}) collective-permute-start(bf16[256,256]{1,0:T(8,128)(2,1)S(1)} %get-tuple-element.47.v0), channel_id=1, source_target_pairs={{0,64},{64,128},{128,192},{192,0},{1,65},{65,129},{129,193},{193,1... | collective-permute-start | bytes 393224 | tf_op jit(solution)/shard_map/ppermute | solution.py:521
  71.2 7.0 %collective-permute-start.8 = (bf16[256,256]{1,0:T(8,128)(2,1)S(1)}, bf16[256,256]{1,0:T(8,128)(2,1)S(1)}, u32[]{:S(2)}, u32[]{:S(2)}) collective-permute-start(bf16[256,256]{1,0:T(8,128)(2,1)S(1)} %get-tuple-element.47.v0), channel_id=1, source_target_pairs={{0,192},{64,0},{128,64},{192,128},{1,193},{65,1},{129,65},{193,129... | collective-permute-start | bytes 393224 | tf_op jit(solution)/shard_map/ppermute | solution.py:521
  79.2 20.8 %copy-start = (bf16[256,1024]{1,0:T(8,128)(2,1)}, bf16[256,1024]{1,0:T(8,128)(2,1)S(1)}, u32[]{:S(2)}) copy-start(bf16[256,1024]{1,0:T(8,128)(2,1)S(1)} %get-tuple-element.48.values_ref.second_hbm) | copy-start | bytes 1572868
  79.2 1.7 %collective-permute-start.9 = (bf16[32,40,128]{2,1,0:T(8,128)(2,1)S(1)}, bf16[32,40,128]{2,1,0:T(8,128)(2,1)S(1)}, u32[]{:S(2)}, u32[]{:S(2)}) collective-permute-start(bf16[32,40,128]{2,1,0:T(8,128)(2,1)S(1)} %get-tuple-element.49), channel_id=1, source_target_pairs={{0,1},{1,0},{2,3},{3,2},{4,5},{5,4},{6,7},{7,6},{8,9},{9,8},{10,11... | collective-permute-start | bytes 983048 | tf_op jit(solution)/shard_map/ppermute | solution.py:529
  117.9 2.3 %collective-permute-start.10 = (bf16[32,40,128]{2,1,0:T(8,128)(2,1)S(1)}, bf16[32,40,128]{2,1,0:T(8,128)(2,1)S(1)}, u32[]{:S(2)}, u32[]{:S(2)}) collective-permute-start(bf16[32,40,128]{2,1,0:T(8,128)(2,1)S(1)} %all_to_all.23.mine_ref), channel_id=1, source_target_pairs={{0,1},{1,0},{2,3},{3,2},{4,5},{5,4},{6,7},{7,6},{8,9},{9,8},{10,11... | collective-permute-start | bytes 983048 | tf_op jit(solution)/shard_map/ppermute | solution.py:529
  122.1 6.4 %collective-permute-start.11 = (bf16[144,256]{1,0:T(8,128)(2,1)S(1)}, bf16[144,256]{1,0:T(8,128)(2,1)S(1)}, u32[]{:S(2)}, u32[]{:S(2)}) collective-permute-start(bf16[144,256]{1,0:T(8,128)(2,1)S(1)} %get-tuple-element.57), channel_id=1, source_target_pairs={{0,128},{64,192},{128,0},{192,64},{1,129},{65,193},{129,1},{193,65... | collective-permute-start | bytes 221192 | tf_op jit(solution)/shard_map/ppermute | solution.py:521
  123.7 4.8 %collective-permute-start.12 = (bf16[144,256]{1,0:T(8,128)(2,1)S(1)}, bf16[144,256]{1,0:T(8,128)(2,1)S(1)}, u32[]{:S(2)}, u32[]{:S(2)}) collective-permute-start(bf16[144,256]{1,0:T(8,128)(2,1)S(1)} %get-tuple-element.58), channel_id=1, source_target_pairs={{0,64},{64,128},{128,192},{192,0},{1,65},{65,129},{129,193},{193,1... | collective-permute-start | bytes 221192 | tf_op jit(solution)/shard_map/ppermute | solution.py:521
  124.9 5.6 %collective-permute-start.13 = (bf16[144,256]{1,0:T(8,128)(2,1)S(1)}, bf16[144,256]{1,0:T(8,128)(2,1)S(1)}, u32[]{:S(2)}, u32[]{:S(2)}) collective-permute-start(bf16[144,256]{1,0:T(8,128)(2,1)S(1)} %get-tuple-element.59), channel_id=1, source_target_pairs={{0,192},{64,0},{128,64},{192,128},{1,193},{65,1},{129,65},{193,129... | collective-permute-start | bytes 221192 | tf_op jit(solution)/shard_map/ppermute | solution.py:521

commit v7 on v6

--- a/solution.py
+++ b/solution.py
@@ -19,7 +19,7 @@
 STRIDE = -(-CLASSES // SLABS)
 LAST_FAR = (2, 3, 1)
 LEAP = REACH * SPAN
-FIRST_ROWS = ((0, LEAP // 2 + 4), (LEAP // 2 + 4, LEAP))
+FIRST_ROWS = ((0, 64), (64, 144))
 COUNT_PIECE = 30
 COUNT_ROW = 32
 TABLE = 2 * SLAB
@@ -190,8 +190,8 @@
             table_ref[SLAB + start : SLAB + stop, columns] = sine.astype(BF16)
         plain = cosine_and_sine(REACH * where[1])
         carried = cosine_and_sine(where[0] - (REACH + 1) * where[1])
-        for start in range(LEAP, SLAB, 72):
-            stop = min(start + 72, SLAB)
+        for start in range(FIRST_ROWS[-1][1], SLAB, 80):
+            stop = min(start + 80, SLAB)
             before = slice(start - LEAP, stop - LEAP)
             carry = second_ref[before] > 0.5
             turn_cosine = jnp.where(carry, carried[0], plain[0])
@@ -233,8 +233,9 @@
     for start in range(0, SLAB, CHANNELS):
         here = (column == lane + float(start)) & (lane < float(STRIDE - start))
         rows.append(jnp.sum(jnp.where(here, 1.0 / copies, 0.0), axis=0, keepdims=True))
-    rows.append(jnp.zeros((8 - len(rows), CHANNELS), F32))
-    counts_ref[COUNT_PIECE, COUNT_ROW:, :] = jnp.concatenate(rows, axis=0).astype(BF16)
+    rows = [jnp.zeros((COUNT_ROW, CHANNELS), F32)] + rows
+    rows.append(jnp.zeros((ROWS + 1 - COUNT_ROW - len(rows), CHANNELS), F32))
+    counts_ref[COUNT_PIECE] = jnp.concatenate(rows, axis=0).astype(BF16)
 
 
 def write_fields(total_ref, fields_ref):
@@ -254,7 +255,7 @@
     fields_ref,
     leaves,
 ):
-    counts = jnp.transpose(mine_ref[COUNT_PIECE, COUNT_ROW:, :].astype(F32))
+    counts = jnp.transpose(mine_ref[COUNT_PIECE].astype(F32)[COUNT_ROW:])
     for index in range(SLAB // CHANNELS):
         start = index * CHANNELS
         count = counts[:, index : index + 1]

time: 132 us -> 132 us (level)
  no operation moved by 1% of the time
where the time goes in v7:
time: 132 us
  blocking collectives  82.9 us (63%)
  Pallas kernels  21 us (16%)
  waiting for transfers between devices  15.1 us (11%)
  starting transfers between devices  11.6 us (9%)
    all_to_all x2, blocking collectives, sum_fields(): parts = lax.all_to_all(part, ATOM_REST, 0, 0, tiled=True)  48.4 us
    all_to_all x2, blocking collectives, sum_fields(): mine = lax.all_to_all(spread, ATOM_REST, 0, 0, tiled=True)  34.5 us
    pallas_call x13, Pallas kernels, call_whole(): pl.pallas_call(kernel, in_specs=[pl.BlockSpec(memory_space=pltpu.SMEM)] +...  19.9 us
    ppermute x9, waiting for transfers between devices, shifted(): lax.ppermute(value, 'x', [(i, (i + shift) % SLABS) for i in range(SLABS)])  14.5 us
    ppermute x9, starting transfers between devices, shifted(): lax.ppermute(value, 'x', [(i, (i + shift) % SLABS) for i in range(SLABS)])  10.7 us
  transfers between devices with their start and end apart: 14, of which 9 were waited for; matrix products, arithmetic and copies ran while one was open for 0% of the time, Pallas kernels for 7%

profile of v7, /device:TPU:6, one launch (start us, length us, event | category | flops | bytes accessed | tf_op | source)
XLA Modules:
  0.0 131.9 jit_solution(17453692847152257845)
XLA Ops:
  0.7 4.7 %shard_map.95 = (bf16[1536,1024]{1,0:T(8,128)(2,1)S(1)}, bf16[32,40,128]{2,1,0:T(8,128)(2,1)S(1)}, bf16[32,40,128]{2,1,0:T(8,128)(2,1)S(1)}) custom-call(s32[3]{0:T(128)S(1)} %pad_add_fusion.place, f32[3,2048]{1,0:T(4,128)} %coordinates_hbm.1, s32[1,2048]{1,0:T(1,128)} %bitcast.9, bf16[4,2,256,128]{3,2,1,0:T(8,128)(2,1)} %bitcast.7, ...), custom_call_target="tpu_custom_call" | custom-call | flops 7000000000 | bytes 7000000 | tf_op jit(solution)/shard_map/pallas_call | solution.py:507
  7.2 30.0 %all_to_all.20 = bf16[32,40,128]{2,1,0:T(8,128)(2,1)S(1)} all-to-all(bf16[32,40,128]{2,1,0:T(8,128)(2,1)S(1)} %add_convert_fusion.1), channel_id=1, replica_groups=mesh['x'=4,'yh'=2,'yl'=2,'z'=8,'core'=2] {'yh','yl','z'}, dimensions={0} | all-to-all | bytes 655360 | tf_op jit(solution)/shard_map/all_to_all | solution.py:541
  37.4 16.6 %all_to_all.21.mine_ref = bf16[32,40,128]{2,1,0:T(8,128)(2,1)S(1)} all-to-all(bf16[32,40,128]{2,1,0:T(8,128)(2,1)S(1)} %broadcast_in_dim.10), channel_id=1, replica_groups=mesh['x'=4,'yh'=2,'yl'=2,'z'=8,'core'=2] {'yh','yl','z'}, dimensions={0} | all-to-all | bytes 655360 | tf_op jit(solution)/shard_map/all_to_all | solution.py:549
  54.0 2.0 %shard_map.97 = (f32[2,640,128]{2,1,0:T(8,128)S(1)}, bf16[640,256]{1,0:T(8,128)(2,1)}, f32[256,1024]{1,0:T(8,128)S(1)}) custom-call(s32[3]{0:T(128)S(1)} %pad_add_fusion.place, bf16[32,40,128]{2,1,0:T(8,128)(2,1)S(1)} %all_to_all.21.mine_ref, bf16[1536,1024]{1,0:T(8,128)(2,1)S(1)} %get-tuple-element.32.table_ref), custom_call_target="tpu_custom_call" | custom-call | flops 2000000000 | bytes 2000000 | tf_op jit(solution)/shard_map/pallas_call | solution.py:507
  56.0 1.1 shard_map.98
  57.2 1.5 %collective-permute-start.3 = (bf16[256,256]{1,0:T(8,128)(2,1)S(1)}, bf16[256,256]{1,0:T(8,128)(2,1)S(1)}, u32[]{:S(2)}, u32[]{:S(2)}) collective-permute-start(bf16[256,256]{1,0:T(8,128)(2,1)S(1)} %get-tuple-element.39), channel_id=1, source_target_pairs={{0,128},{64,192},{128,0},{192,64},{1,129},{65,193},{129,1},{193,65... | collective-permute-start | bytes 393224 | tf_op jit(solution)/shard_map/ppermute | solution.py:522
  58.7 2.1 %collective-permute-start.4 = (bf16[256,256]{1,0:T(8,128)(2,1)S(1)}, bf16[256,256]{1,0:T(8,128)(2,1)S(1)}, u32[]{:S(2)}, u32[]{:S(2)}) collective-permute-start(bf16[256,256]{1,0:T(8,128)(2,1)S(1)} %get-tuple-element.40), channel_id=1, source_target_pairs={{0,64},{64,128},{128,192},{192,0},{1,65},{65,129},{129,193},{193,1... | collective-permute-start | bytes 393224 | tf_op jit(solution)/shard_map/ppermute | solution.py:522
  61.7 1.1 shard_map.100
  62.8 2.3 %collective-permute-done.3.q1 = bf16[256,256]{1,0:T(8,128)(2,1)S(1)} collective-permute-done((bf16[256,256]{1,0:T(8,128)(2,1)S(1)}, bf16[256,256]{1,0:T(8,128)(2,1)S(1)}, u32[]{:S(2)}, u32[]{:S(2)}) %collective-permute-start.3) | collective-permute-done | bytes 131104 | tf_op jit(solution)/shard_map/ppermute | solution.py:522
  65.3 2.3 %collective-permute-done.5.q3 = bf16[256,256]{1,0:T(8,128)(2,1)S(1)} collective-permute-done((bf16[256,256]{1,0:T(8,128)(2,1)S(1)}, bf16[256,256]{1,0:T(8,128)(2,1)S(1)}, u32[]{:S(2)}, u32[]{:S(2)}) %collective-permute-start.5) | collective-permute-done | bytes 131104 | tf_op jit(solution)/shard_map/ppermute | solution.py:522
  68.6 1.5 %collective-permute-start.6 = (bf16[256,256]{1,0:T(8,128)(2,1)S(1)}, bf16[256,256]{1,0:T(8,128)(2,1)S(1)}, u32[]{:S(2)}, u32[]{:S(2)}) collective-permute-start(bf16[256,256]{1,0:T(8,128)(2,1)S(1)} %get-tuple-element.47.v0), channel_id=1, source_target_pairs={{0,128},{64,192},{128,0},{192,64},{1,129},{65,193},{129,1},{193,65... | collective-permute-start | bytes 393224 | tf_op jit(solution)/shard_map/ppermute | solution.py:522
  70.0 1.2 collective-permute-start.7
  72.1 4.4 %collective-permute-done.6.v1 = bf16[256,256]{1,0:T(8,128)(2,1)S(1)} collective-permute-done((bf16[256,256]{1,0:T(8,128)(2,1)S(1)}, bf16[256,256]{1,0:T(8,128)(2,1)S(1)}, u32[]{:S(2)}, u32[]{:S(2)}) %collective-permute-start.6) | collective-permute-done | bytes 131104 | tf_op jit(solution)/shard_map/ppermute | solution.py:522
  76.5 1.6 %collective-permute-done.8.v3 = bf16[256,256]{1,0:T(8,128)(2,1)S(1)} collective-permute-done((bf16[256,256]{1,0:T(8,128)(2,1)S(1)}, bf16[256,256]{1,0:T(8,128)(2,1)S(1)}, u32[]{:S(2)}, u32[]{:S(2)}) %collective-permute-start.8) | collective-permute-done | bytes 131104 | tf_op jit(solution)/shard_map/ppermute | solution.py:522
  81.1 18.4 %all_to_all.22.parts_ref = bf16[32,40,128]{2,1,0:T(8,128)(2,1)S(1)} all-to-all(bf16[32,40,128]{2,1,0:T(8,128)(2,1)S(1)} %add_convert_fusion), channel_id=1, replica_groups=mesh['x'=4,'yh'=2,'yl'=2,'z'=8,'core'=2] {'yh','yl','z'}, dimensions={0} | all-to-all | bytes 655360 | tf_op jit(solution)/shard_map/all_to_all | solution.py:541
  100.1 17.9 %all_to_all.23.mine_ref = bf16[32,40,128]{2,1,0:T(8,128)(2,1)S(1)} all-to-all(bf16[32,40,128]{2,1,0:T(8,128)(2,1)S(1)} %shard_map.104), channel_id=1, replica_groups=mesh['x'=4,'yh'=2,'yl'=2,'z'=8,'core'=2] {'yh','yl','z'}, dimensions={0} | all-to-all | bytes 655360 | tf_op jit(solution)/shard_map/all_to_all | solution.py:549
  118.0 2.3 %shard_map.105 = (bf16[512,1024]{1,0:T(8,128)(2,1)S(1)}, f32[640,1024]{1,0:T(8,128)S(1)}, f32[128,1024]{1,0:T(8,128)S(1)}) custom-call(s32[3]{0:T(128)S(1)} %pad_add_fusion.place, f32[2,640,128]{2,1,0:T(8,128)S(1)} %get-tuple-element.35.weights_ref, bf16[32,40,128]{2,1,0:T(8,128)(2,1)S(1)} %all_to_all.23.mine_ref, ...), custom_call_target="tpu_custom_call" | custom-call | flops 2000000000 | bytes 2000000 | tf_op jit(solution)/shard_map/pallas_call | solution.py:507
  120.2 1.9 %shard_map.106 = (bf16[640,512]{1,0:T(8,128)(2,1)S(1)}, bf16[128,640]{1,0:T(8,128)(2,1)S(1)}, bf16[144,256]{1,0:T(8,128)(2,1)S(1)}, bf16[144,256]{1,0:T(8,128)(2,1)S(1)}, bf16[144,256]{1,0:T(8,128)(2,1)S(1)}) custom-call(s32[3]{0:T(128)S(1)} %pad_add_fusion.place, f32[2,640,128]{2,1,0:T(8,128)S(1)} %get-tuple-element.35.weights_ref, ...), custom_call_target="tpu_custom_call" | custom-call | flops 2000000000 | bytes 2000000 | tf_op jit(solution)/shard_map/pallas_call | solution.py:507
  122.1 1.6 %collective-permute-start.11 = (bf16[144,256]{1,0:T(8,128)(2,1)S(1)}, bf16[144,256]{1,0:T(8,128)(2,1)S(1)}, u32[]{:S(2)}, u32[]{:S(2)}) collective-permute-start(bf16[144,256]{1,0:T(8,128)(2,1)S(1)} %get-tuple-element.57), channel_id=1, source_target_pairs={{0,128},{64,192},{128,0},{192,64},{1,129},{65,193},{129,1},{193,65... | collective-permute-start | bytes 221192 | tf_op jit(solution)/shard_map/ppermute | solution.py:522
  123.7 1.2 collective-permute-start.12
  125.8 1.1 shard_map.107.q0
  126.9 1.6 %collective-permute-done.11.q1 = bf16[144,256]{1,0:T(8,128)(2,1)S(1)} collective-permute-done((bf16[144,256]{1,0:T(8,128)(2,1)S(1)}, bf16[144,256]{1,0:T(8,128)(2,1)S(1)}, u32[]{:S(2)}, u32[]{:S(2)}) %collective-permute-start.11) | collective-permute-done | bytes 73760 | tf_op jit(solution)/shard_map/ppermute | solution.py:522
  128.5 2.0 %collective-permute-done.13.q3 = bf16[144,256]{1,0:T(8,128)(2,1)S(1)} collective-permute-done((bf16[144,256]{1,0:T(8,128)(2,1)S(1)}, bf16[144,256]{1,0:T(8,128)(2,1)S(1)}, u32[]{:S(2)}, u32[]{:S(2)}) %collective-permute-start.13) | collective-permute-done | bytes 73760 | tf_op jit(solution)/shard_map/ppermute | solution.py:522
  130.5 1.4 %shard_map.108 = (bf16[256,128]{1,0:T(8,128)(2,1)}, f32[3,256]{1,0:T(4,128)}) custom-call(s32[3]{0:T(128)S(1)} %pad_add_fusion.place, bf16[144,256]{1,0:T(8,128)(2,1)S(1)} %shard_map.107.q0, bf16[144,256]{1,0:T(8,128)(2,1)S(1)} %collective-permute-done.11.q1, bf16[144,256]{1,0:T(8,128)(2,1)S(1)} %collective-permute-done.12.q2, ...), custom_call_target="tpu_custom_call" | custom-call | flops 2000000000 | bytes 2000000 | tf_op jit(solution)/shard_map/pallas_call | solution.py:507
  (43 shorter events, 9.3 us)
Async XLA Ops:
  0.7 4.8 %copy-start.7 = (s32[3,512]{1,0:T(4,128)S(1)}, s32[3,512]{1,0:T(4,128)}, u32[]{:S(2)}) copy-start(s32[3,512]{1,0:T(4,128)} %param.11) | copy-start | bytes 18436
  5.4 1.7 %collective-permute-start = (bf16[32,40,128]{2,1,0:T(8,128)(2,1)S(1)}, bf16[32,40,128]{2,1,0:T(8,128)(2,1)S(1)}, u32[]{:S(2)}, u32[]{:S(2)}) collective-permute-start(bf16[32,40,128]{2,1,0:T(8,128)(2,1)S(1)} %get-tuple-element.34), channel_id=1, source_target_pairs={{0,1},{1,0},{2,3},{3,2},{4,5},{5,4},{6,7},{7,6},{8,9},{9,8},{10,11... | collective-permute-start | bytes 983048 | tf_op jit(solution)/shard_map/ppermute | solution.py:530
  5.5 0.7 collective-permute-start.1
  54.0 2.0 %collective-permute-start.2 = (bf16[32,40,128]{2,1,0:T(8,128)(2,1)S(1)}, bf16[32,40,128]{2,1,0:T(8,128)(2,1)S(1)}, u32[]{:S(2)}, u32[]{:S(2)}) collective-permute-start(bf16[32,40,128]{2,1,0:T(8,128)(2,1)S(1)} %all_to_all.21.mine_ref), channel_id=1, source_target_pairs={{0,1},{1,0},{2,3},{3,2},{4,5},{5,4},{6,7},{7,6},{8,9},{9,8},{10,11... | collective-permute-start | bytes 983048 | tf_op jit(solution)/shard_map/ppermute | solution.py:530
  57.1 4.5 %copy-start.1 = (bf16[2048,128]{1,0:T(8,128)(2,1)S(1)}, bf16[2048,128]{1,0:T(8,128)(2,1)}, u32[]{:S(2)}) copy-start(bf16[2048,128]{1,0:T(8,128)(2,1)} %features_ref.1) | copy-start | bytes 1572868
  57.1 4.5 %copy-start.2 = (bf16[2048,128]{1,0:T(8,128)(2,1)S(1)}, bf16[2048,128]{1,0:T(8,128)(2,1)}, u32[]{:S(2)}) copy-start(bf16[2048,128]{1,0:T(8,128)(2,1)} %upstream_ref.1) | copy-start | bytes 1572868
  57.1 4.5 %copy-start.3 = (bf16[2,128,128]{2,1,0:T(8,128)(2,1)S(1)}, bf16[2,128,128]{2,1,0:T(8,128)(2,1)}, u32[]{:S(2)}) copy-start(bf16[2,128,128]{2,1,0:T(8,128)(2,1)} %inward_ref.1) | copy-start | bytes 196612
  57.2 4.5 %copy-start.4 = (s32[2048]{0:T(1024)S(1)}, s32[2048]{0:T(1024)}, u32[]{:S(2)}) copy-start(s32[2048]{0:T(1024)} %param.10) | copy-start | bytes 24580
  57.2 4.5 %copy-start.5 = (f32[2,6,128]{2,0,1:T(2,128)S(1)}, f32[2,6,128]{2,0,1:T(2,128)}, u32[]{:S(2)}) copy-start(f32[2,6,128]{2,0,1:T(2,128)} %param.14) | copy-start | bytes 18436
  57.2 10.4 %copy-start.6 = (bf16[2,128,128]{2,1,0:T(8,128)(2,1)S(1)}, bf16[2,128,128]{2,1,0:T(8,128)(2,1)}, u32[]{:S(2)}) copy-start(bf16[2,128,128]{2,1,0:T(8,128)(2,1)} %outward_ref.1) | copy-start | bytes 196612
  57.2 7.9 %collective-permute-start.3 = (bf16[256,256]{1,0:T(8,128)(2,1)S(1)}, bf16[256,256]{1,0:T(8,128)(2,1)S(1)}, u32[]{:S(2)}, u32[]{:S(2)}) collective-permute-start(bf16[256,256]{1,0:T(8,128)(2,1)S(1)} %get-tuple-element.39), channel_id=1, source_target_pairs={{0,128},{64,192},{128,0},{192,64},{1,129},{65,193},{129,1},{193,65... | collective-permute-start | bytes 393224 | tf_op jit(solution)/shard_map/ppermute | solution.py:522
  58.7 6.6 %collective-permute-start.4 = (bf16[256,256]{1,0:T(8,128)(2,1)S(1)}, bf16[256,256]{1,0:T(8,128)(2,1)S(1)}, u32[]{:S(2)}, u32[]{:S(2)}) collective-permute-start(bf16[256,256]{1,0:T(8,128)(2,1)S(1)} %get-tuple-element.40), channel_id=1, source_target_pairs={{0,64},{64,128},{128,192},{192,0},{1,65},{65,129},{129,193},{193,1... | collective-permute-start | bytes 393224 | tf_op jit(solution)/shard_map/ppermute | solution.py:522
  60.8 6.8 %collective-permute-start.5 = (bf16[256,256]{1,0:T(8,128)(2,1)S(1)}, bf16[256,256]{1,0:T(8,128)(2,1)S(1)}, u32[]{:S(2)}, u32[]{:S(2)}) collective-permute-start(bf16[256,256]{1,0:T(8,128)(2,1)S(1)} %get-tuple-element.41), channel_id=1, source_target_pairs={{0,192},{64,0},{128,64},{192,128},{1,193},{65,1},{129,65},{193,129... | collective-permute-start | bytes 393224 | tf_op jit(solution)/shard_map/ppermute | solution.py:522
  68.6 7.9 %collective-permute-start.6 = (bf16[256,256]{1,0:T(8,128)(2,1)S(1)}, bf16[256,256]{1,0:T(8,128)(2,1)S(1)}, u32[]{:S(2)}, u32[]{:S(2)}) collective-permute-start(bf16[256,256]{1,0:T(8,128)(2,1)S(1)} %get-tuple-element.47.v0), channel_id=1, source_target_pairs={{0,128},{64,192},{128,0},{192,64},{1,129},{65,193},{129,1},{193,65... | collective-permute-start | bytes 393224 | tf_op jit(solution)/shard_map/ppermute | solution.py:522
  70.0 6.5 %collective-permute-start.7 = (bf16[256,256]{1,0:T(8,128)(2,1)S(1)}, bf16[256,256]{1,0:T(8,128)(2,1)S(1)}, u32[]{:S(2)}, u32[]{:S(2)}) collective-permute-start(bf16[256,256]{1,0:T(8,128)(2,1)S(1)} %get-tuple-element.47.v0), channel_id=1, source_target_pairs={{0,64},{64,128},{128,192},{192,0},{1,65},{65,129},{129,193},{193,1... | collective-permute-start | bytes 393224 | tf_op jit(solution)/shard_map/ppermute | solution.py:522
  71.2 7.0 %collective-permute-start.8 = (bf16[256,256]{1,0:T(8,128)(2,1)S(1)}, bf16[256,256]{1,0:T(8,128)(2,1)S(1)}, u32[]{:S(2)}, u32[]{:S(2)}) collective-permute-start(bf16[256,256]{1,0:T(8,128)(2,1)S(1)} %get-tuple-element.47.v0), channel_id=1, source_target_pairs={{0,192},{64,0},{128,64},{192,128},{1,193},{65,1},{129,65},{193,129... | collective-permute-start | bytes 393224 | tf_op jit(solution)/shard_map/ppermute | solution.py:522
  79.3 20.8 %copy-start = (bf16[256,1024]{1,0:T(8,128)(2,1)}, bf16[256,1024]{1,0:T(8,128)(2,1)S(1)}, u32[]{:S(2)}) copy-start(bf16[256,1024]{1,0:T(8,128)(2,1)S(1)} %get-tuple-element.48.values_ref.second_hbm) | copy-start | bytes 1572868
  79.3 1.7 %collective-permute-start.9 = (bf16[32,40,128]{2,1,0:T(8,128)(2,1)S(1)}, bf16[32,40,128]{2,1,0:T(8,128)(2,1)S(1)}, u32[]{:S(2)}, u32[]{:S(2)}) collective-permute-start(bf16[32,40,128]{2,1,0:T(8,128)(2,1)S(1)} %get-tuple-element.49), channel_id=1, source_target_pairs={{0,1},{1,0},{2,3},{3,2},{4,5},{5,4},{6,7},{7,6},{8,9},{9,8},{10,11... | collective-permute-start | bytes 983048 | tf_op jit(solution)/shard_map/ppermute | solution.py:530
  118.0 2.3 %collective-permute-start.10 = (bf16[32,40,128]{2,1,0:T(8,128)(2,1)S(1)}, bf16[32,40,128]{2,1,0:T(8,128)(2,1)S(1)}, u32[]{:S(2)}, u32[]{:S(2)}) collective-permute-start(bf16[32,40,128]{2,1,0:T(8,128)(2,1)S(1)} %all_to_all.23.mine_ref), channel_id=1, source_target_pairs={{0,1},{1,0},{2,3},{3,2},{4,5},{5,4},{6,7},{7,6},{8,9},{9,8},{10,11... | collective-permute-start | bytes 983048 | tf_op jit(solution)/shard_map/ppermute | solution.py:530
  122.1 6.4 %collective-permute-start.11 = (bf16[144,256]{1,0:T(8,128)(2,1)S(1)}, bf16[144,256]{1,0:T(8,128)(2,1)S(1)}, u32[]{:S(2)}, u32[]{:S(2)}) collective-permute-start(bf16[144,256]{1,0:T(8,128)(2,1)S(1)} %get-tuple-element.57), channel_id=1, source_target_pairs={{0,128},{64,192},{128,0},{192,64},{1,129},{65,193},{129,1},{193,65... | collective-permute-start | bytes 221192 | tf_op jit(solution)/shard_map/ppermute | solution.py:522
  123.7 4.8 %collective-permute-start.12 = (bf16[144,256]{1,0:T(8,128)(2,1)S(1)}, bf16[144,256]{1,0:T(8,128)(2,1)S(1)}, u32[]{:S(2)}, u32[]{:S(2)}) collective-permute-start(bf16[144,256]{1,0:T(8,128)(2,1)S(1)} %get-tuple-element.58), channel_id=1, source_target_pairs={{0,64},{64,128},{128,192},{192,0},{1,65},{65,129},{129,193},{193,1... | collective-permute-start | bytes 221192 | tf_op jit(solution)/shard_map/ppermute | solution.py:522
  124.9 5.6 %collective-permute-start.13 = (bf16[144,256]{1,0:T(8,128)(2,1)S(1)}, bf16[144,256]{1,0:T(8,128)(2,1)S(1)}, u32[]{:S(2)}, u32[]{:S(2)}) collective-permute-start(bf16[144,256]{1,0:T(8,128)(2,1)S(1)} %get-tuple-element.59), channel_id=1, source_target_pairs={{0,192},{64,0},{128,64},{192,128},{1,193},{65,1},{129,65},{193,129... | collective-permute-start | bytes 221192 | tf_op jit(solution)/shard_map/ppermute | solution.py:522

commit v8 on v7

--- a/solution.py
+++ b/solution.py
@@ -21,7 +21,8 @@
 LEAP = REACH * SPAN
 FIRST_ROWS = ((0, 64), (64, 144))
 COUNT_PIECE = 30
-COUNT_ROW = 32
+COUNT_BASE = 8
+COUNT_ROWS = (16, 24, 32)
 TABLE = 2 * SLAB
 BLOCK = 256
 CHANNELS = 128
@@ -93,7 +94,8 @@
 
 def write_half(half, table_ref, values_ref, pieces_ref, total_ref):
     total_ref[...] = matmul(table_ref[half_rows(half), :], values_ref[...], 1, 1)
-    total_ref[SLAB - 8 :, :CHANNELS] = jnp.zeros((8, CHANNELS), F32)
+    spare = ROWS - COUNT_ROWS[0]
+    total_ref[SLAB - spare :, :CHANNELS] = jnp.zeros((spare, CHANNELS), F32)
     for index in range(PIECES):
         row, side = index // 2, index % 2
         pieces_ref[index] = total_ref[
@@ -232,10 +234,16 @@
     rows = []
     for start in range(0, SLAB, CHANNELS):
         here = (column == lane + float(start)) & (lane < float(STRIDE - start))
-        rows.append(jnp.sum(jnp.where(here, 1.0 / copies, 0.0), axis=0, keepdims=True))
-    rows = [jnp.zeros((COUNT_ROW, CHANNELS), F32)] + rows
-    rows.append(jnp.zeros((ROWS + 1 - COUNT_ROW - len(rows), CHANNELS), F32))
-    counts_ref[COUNT_PIECE] = jnp.concatenate(rows, axis=0).astype(BF16)
+        rows.append(jnp.sum(jnp.where(here, 1.0, 0.0), axis=0, keepdims=True))
+    rows.append(jnp.zeros((8 - len(rows), CHANNELS), F32))
+    rest = jnp.concatenate(rows, axis=0)
+    digits = [jnp.zeros((COUNT_ROWS[0], CHANNELS), F32)]
+    for _ in COUNT_ROWS[1:]:
+        higher = jnp.floor(rest * (1.0 / COUNT_BASE))
+        digits.append((rest - COUNT_BASE * higher) * (1.0 / copies))
+        rest = higher
+    digits.append(rest * (1.0 / copies))
+    counts_ref[COUNT_PIECE] = jnp.concatenate(digits, axis=0).astype(BF16)
 
 
 def write_fields(total_ref, fields_ref):
@@ -255,7 +263,9 @@
     fields_ref,
     leaves,
 ):
-    counts = jnp.transpose(mine_ref[COUNT_PIECE].astype(F32)[COUNT_ROW:])
+    digits = mine_ref[COUNT_PIECE].astype(F32)
+    counts = sum(digits[row : row + 8] * COUNT_BASE**power for power, row in enumerate(COUNT_ROWS))
+    counts = jnp.transpose(counts)
     for index in range(SLAB // CHANNELS):
         start = index * CHANNELS
         count = counts[:, index : index + 1]

time: 132 us -> 132 us (level)
  no operation moved by 1% of the time
where the time goes in v8:
time: 132 us
  blocking collectives  82.9 us (63%)
  Pallas kernels  21.1 us (16%)
  waiting for transfers between devices  15.1 us (11%)
  starting transfers between devices  11.6 us (9%)
    all_to_all x2, blocking collectives, sum_fields(): parts = lax.all_to_all(part, ATOM_REST, 0, 0, tiled=True)  48.4 us
    all_to_all x2, blocking collectives, sum_fields(): mine = lax.all_to_all(spread, ATOM_REST, 0, 0, tiled=True)  34.5 us
    pallas_call x13, Pallas kernels, call_whole(): pl.pallas_call(kernel, in_specs=[pl.BlockSpec(memory_space=pltpu.SMEM)] +...  19.9 us
    ppermute x9, waiting for transfers between devices, shifted(): lax.ppermute(value, 'x', [(i, (i + shift) % SLABS) for i in range(SLABS)])  14.5 us
    ppermute x9, starting transfers between devices, shifted(): lax.ppermute(value, 'x', [(i, (i + shift) % SLABS) for i in range(SLABS)])  10.7 us
  transfers between devices with their start and end apart: 14, of which 9 were waited for; matrix products, arithmetic and copies ran while one was open for 0% of the time, Pallas kernels for 7%

profile of v8, /device:TPU:6, one launch (start us, length us, event | category | flops | bytes accessed | tf_op | source)
XLA Modules:
  0.0 131.9 jit_solution(10313559964539684163)
XLA Ops:
  0.7 4.7 %shard_map.95 = (bf16[1536,1024]{1,0:T(8,128)(2,1)S(1)}, bf16[32,40,128]{2,1,0:T(8,128)(2,1)S(1)}, bf16[32,40,128]{2,1,0:T(8,128)(2,1)S(1)}) custom-call(s32[3]{0:T(128)S(1)} %pad_add_fusion.place, f32[3,2048]{1,0:T(4,128)} %coordinates_hbm.1, s32[1,2048]{1,0:T(1,128)} %bitcast.9, bf16[4,2,256,128]{3,2,1,0:T(8,128)(2,1)} %bitcast.7, ...), custom_call_target="tpu_custom_call" | custom-call | flops 7000000000 | bytes 7000000 | tf_op jit(solution)/shard_map/pallas_call | solution.py:517
  7.2 30.0 %all_to_all.20 = bf16[32,40,128]{2,1,0:T(8,128)(2,1)S(1)} all-to-all(bf16[32,40,128]{2,1,0:T(8,128)(2,1)S(1)} %add_convert_fusion.1), channel_id=1, replica_groups=mesh['x'=4,'yh'=2,'yl'=2,'z'=8,'core'=2] {'yh','yl','z'}, dimensions={0} | all-to-all | bytes 655360 | tf_op jit(solution)/shard_map/all_to_all | solution.py:551
  37.4 16.6 %all_to_all.21.mine_ref = bf16[32,40,128]{2,1,0:T(8,128)(2,1)S(1)} all-to-all(bf16[32,40,128]{2,1,0:T(8,128)(2,1)S(1)} %broadcast_in_dim.10), channel_id=1, replica_groups=mesh['x'=4,'yh'=2,'yl'=2,'z'=8,'core'=2] {'yh','yl','z'}, dimensions={0} | all-to-all | bytes 655360 | tf_op jit(solution)/shard_map/all_to_all | solution.py:559
  54.0 2.1 %shard_map.97 = (f32[2,640,128]{2,1,0:T(8,128)S(1)}, bf16[640,256]{1,0:T(8,128)(2,1)}, f32[256,1024]{1,0:T(8,128)S(1)}) custom-call(s32[3]{0:T(128)S(1)} %pad_add_fusion.place, bf16[32,40,128]{2,1,0:T(8,128)(2,1)S(1)} %all_to_all.21.mine_ref, bf16[1536,1024]{1,0:T(8,128)(2,1)S(1)} %get-tuple-element.32.table_ref), custom_call_target="tpu_custom_call" | custom-call | flops 2000000000 | bytes 2000000 | tf_op jit(solution)/shard_map/pallas_call | solution.py:517
  56.1 1.1 shard_map.98
  57.3 1.5 %collective-permute-start.3 = (bf16[256,256]{1,0:T(8,128)(2,1)S(1)}, bf16[256,256]{1,0:T(8,128)(2,1)S(1)}, u32[]{:S(2)}, u32[]{:S(2)}) collective-permute-start(bf16[256,256]{1,0:T(8,128)(2,1)S(1)} %get-tuple-element.39), channel_id=1, source_target_pairs={{0,128},{64,192},{128,0},{192,64},{1,129},{65,193},{129,1},{193,65... | collective-permute-start | bytes 393224 | tf_op jit(solution)/shard_map/ppermute | solution.py:532
  58.7 2.1 %collective-permute-start.4 = (bf16[256,256]{1,0:T(8,128)(2,1)S(1)}, bf16[256,256]{1,0:T(8,128)(2,1)S(1)}, u32[]{:S(2)}, u32[]{:S(2)}) collective-permute-start(bf16[256,256]{1,0:T(8,128)(2,1)S(1)} %get-tuple-element.40), channel_id=1, source_target_pairs={{0,64},{64,128},{128,192},{192,0},{1,65},{65,129},{129,193},{193,1... | collective-permute-start | bytes 393224 | tf_op jit(solution)/shard_map/ppermute | solution.py:532
  61.7 1.1 shard_map.100
  62.9 2.3 %collective-permute-done.3.q1 = bf16[256,256]{1,0:T(8,128)(2,1)S(1)} collective-permute-done((bf16[256,256]{1,0:T(8,128)(2,1)S(1)}, bf16[256,256]{1,0:T(8,128)(2,1)S(1)}, u32[]{:S(2)}, u32[]{:S(2)}) %collective-permute-start.3) | collective-permute-done | bytes 131104 | tf_op jit(solution)/shard_map/ppermute | solution.py:532
  65.4 2.3 %collective-permute-done.5.q3 = bf16[256,256]{1,0:T(8,128)(2,1)S(1)} collective-permute-done((bf16[256,256]{1,0:T(8,128)(2,1)S(1)}, bf16[256,256]{1,0:T(8,128)(2,1)S(1)}, u32[]{:S(2)}, u32[]{:S(2)}) %collective-permute-start.5) | collective-permute-done | bytes 131104 | tf_op jit(solution)/shard_map/ppermute | solution.py:532
  68.7 1.5 %collective-permute-start.6 = (bf16[256,256]{1,0:T(8,128)(2,1)S(1)}, bf16[256,256]{1,0:T(8,128)(2,1)S(1)}, u32[]{:S(2)}, u32[]{:S(2)}) collective-permute-start(bf16[256,256]{1,0:T(8,128)(2,1)S(1)} %get-tuple-element.47.v0), channel_id=1, source_target_pairs={{0,128},{64,192},{128,0},{192,64},{1,129},{65,193},{129,1},{193,65... | collective-permute-start | bytes 393224 | tf_op jit(solution)/shard_map/ppermute | solution.py:532
  70.1 1.2 collective-permute-start.7
  72.1 4.4 %collective-permute-done.6.v1 = bf16[256,256]{1,0:T(8,128)(2,1)S(1)} collective-permute-done((bf16[256,256]{1,0:T(8,128)(2,1)S(1)}, bf16[256,256]{1,0:T(8,128)(2,1)S(1)}, u32[]{:S(2)}, u32[]{:S(2)}) %collective-permute-start.6) | collective-permute-done | bytes 131104 | tf_op jit(solution)/shard_map/ppermute | solution.py:532
  76.6 1.7 %collective-permute-done.8.v3 = bf16[256,256]{1,0:T(8,128)(2,1)S(1)} collective-permute-done((bf16[256,256]{1,0:T(8,128)(2,1)S(1)}, bf16[256,256]{1,0:T(8,128)(2,1)S(1)}, u32[]{:S(2)}, u32[]{:S(2)}) %collective-permute-start.8) | collective-permute-done | bytes 131104 | tf_op jit(solution)/shard_map/ppermute | solution.py:532
  81.1 18.4 %all_to_all.22.parts_ref = bf16[32,40,128]{2,1,0:T(8,128)(2,1)S(1)} all-to-all(bf16[32,40,128]{2,1,0:T(8,128)(2,1)S(1)} %add_convert_fusion), channel_id=1, replica_groups=mesh['x'=4,'yh'=2,'yl'=2,'z'=8,'core'=2] {'yh','yl','z'}, dimensions={0} | all-to-all | bytes 655360 | tf_op jit(solution)/shard_map/all_to_all | solution.py:551
  100.1 17.9 %all_to_all.23.mine_ref = bf16[32,40,128]{2,1,0:T(8,128)(2,1)S(1)} all-to-all(bf16[32,40,128]{2,1,0:T(8,128)(2,1)S(1)} %shard_map.104), channel_id=1, replica_groups=mesh['x'=4,'yh'=2,'yl'=2,'z'=8,'core'=2] {'yh','yl','z'}, dimensions={0} | all-to-all | bytes 655360 | tf_op jit(solution)/shard_map/all_to_all | solution.py:559
  118.0 2.3 %shard_map.105 = (bf16[512,1024]{1,0:T(8,128)(2,1)S(1)}, f32[640,1024]{1,0:T(8,128)S(1)}, f32[128,1024]{1,0:T(8,128)S(1)}) custom-call(s32[3]{0:T(128)S(1)} %pad_add_fusion.place, f32[2,640,128]{2,1,0:T(8,128)S(1)} %get-tuple-element.35.weights_ref, bf16[32,40,128]{2,1,0:T(8,128)(2,1)S(1)} %all_to_all.23.mine_ref, ...), custom_call_target="tpu_custom_call" | custom-call | flops 2000000000 | bytes 2000000 | tf_op jit(solution)/shard_map/pallas_call | solution.py:517
  120.3 1.9 %shard_map.106 = (bf16[640,512]{1,0:T(8,128)(2,1)S(1)}, bf16[128,640]{1,0:T(8,128)(2,1)S(1)}, bf16[144,256]{1,0:T(8,128)(2,1)S(1)}, bf16[144,256]{1,0:T(8,128)(2,1)S(1)}, bf16[144,256]{1,0:T(8,128)(2,1)S(1)}) custom-call(s32[3]{0:T(128)S(1)} %pad_add_fusion.place, f32[2,640,128]{2,1,0:T(8,128)S(1)} %get-tuple-element.35.weights_ref, ...), custom_call_target="tpu_custom_call" | custom-call | flops 2000000000 | bytes 2000000 | tf_op jit(solution)/shard_map/pallas_call | solution.py:517
  122.2 1.6 %collective-permute-start.11 = (bf16[144,256]{1,0:T(8,128)(2,1)S(1)}, bf16[144,256]{1,0:T(8,128)(2,1)S(1)}, u32[]{:S(2)}, u32[]{:S(2)}) collective-permute-start(bf16[144,256]{1,0:T(8,128)(2,1)S(1)} %get-tuple-element.57), channel_id=1, source_target_pairs={{0,128},{64,192},{128,0},{192,64},{1,129},{65,193},{129,1},{193,65... | collective-permute-start | bytes 221192 | tf_op jit(solution)/shard_map/ppermute | solution.py:532
  123.8 1.2 collective-permute-start.12
  125.8 1.1 shard_map.107.q0
  127.0 1.6 %collective-permute-done.11.q1 = bf16[144,256]{1,0:T(8,128)(2,1)S(1)} collective-permute-done((bf16[144,256]{1,0:T(8,128)(2,1)S(1)}, bf16[144,256]{1,0:T(8,128)(2,1)S(1)}, u32[]{:S(2)}, u32[]{:S(2)}) %collective-permute-start.11) | collective-permute-done | bytes 73760 | tf_op jit(solution)/shard_map/ppermute | solution.py:532
  128.6 2.0 %collective-permute-done.13.q3 = bf16[144,256]{1,0:T(8,128)(2,1)S(1)} collective-permute-done((bf16[144,256]{1,0:T(8,128)(2,1)S(1)}, bf16[144,256]{1,0:T(8,128)(2,1)S(1)}, u32[]{:S(2)}, u32[]{:S(2)}) %collective-permute-start.13) | collective-permute-done | bytes 73760 | tf_op jit(solution)/shard_map/ppermute | solution.py:532
  130.5 1.4 %shard_map.108 = (bf16[256,128]{1,0:T(8,128)(2,1)}, f32[3,256]{1,0:T(4,128)}) custom-call(s32[3]{0:T(128)S(1)} %pad_add_fusion.place, bf16[144,256]{1,0:T(8,128)(2,1)S(1)} %shard_map.107.q0, bf16[144,256]{1,0:T(8,128)(2,1)S(1)} %collective-permute-done.11.q1, bf16[144,256]{1,0:T(8,128)(2,1)S(1)} %collective-permute-done.12.q2, ...), custom_call_target="tpu_custom_call" | custom-call | flops 2000000000 | bytes 2000000 | tf_op jit(solution)/shard_map/pallas_call | solution.py:517
  (43 shorter events, 9.3 us)
Async XLA Ops:
  0.7 4.8 %copy-start.7 = (s32[3,512]{1,0:T(4,128)S(1)}, s32[3,512]{1,0:T(4,128)}, u32[]{:S(2)}) copy-start(s32[3,512]{1,0:T(4,128)} %param.11) | copy-start | bytes 18436
  5.4 1.7 %collective-permute-start = (bf16[32,40,128]{2,1,0:T(8,128)(2,1)S(1)}, bf16[32,40,128]{2,1,0:T(8,128)(2,1)S(1)}, u32[]{:S(2)}, u32[]{:S(2)}) collective-permute-start(bf16[32,40,128]{2,1,0:T(8,128)(2,1)S(1)} %get-tuple-element.34), channel_id=1, source_target_pairs={{0,1},{1,0},{2,3},{3,2},{4,5},{5,4},{6,7},{7,6},{8,9},{9,8},{10,11... | collective-permute-start | bytes 983048 | tf_op jit(solution)/shard_map/ppermute | solution.py:540
  5.5 0.7 collective-permute-start.1
  54.0 2.1 %collective-permute-start.2 = (bf16[32,40,128]{2,1,0:T(8,128)(2,1)S(1)}, bf16[32,40,128]{2,1,0:T(8,128)(2,1)S(1)}, u32[]{:S(2)}, u32[]{:S(2)}) collective-permute-start(bf16[32,40,128]{2,1,0:T(8,128)(2,1)S(1)} %all_to_all.21.mine_ref), channel_id=1, source_target_pairs={{0,1},{1,0},{2,3},{3,2},{4,5},{5,4},{6,7},{7,6},{8,9},{9,8},{10,11... | collective-permute-start | bytes 983048 | tf_op jit(solution)/shard_map/ppermute | solution.py:540
  57.2 4.5 %copy-start.1 = (bf16[2048,128]{1,0:T(8,128)(2,1)S(1)}, bf16[2048,128]{1,0:T(8,128)(2,1)}, u32[]{:S(2)}) copy-start(bf16[2048,128]{1,0:T(8,128)(2,1)} %features_ref.1) | copy-start | bytes 1572868
  57.2 4.5 %copy-start.2 = (bf16[2048,128]{1,0:T(8,128)(2,1)S(1)}, bf16[2048,128]{1,0:T(8,128)(2,1)}, u32[]{:S(2)}) copy-start(bf16[2048,128]{1,0:T(8,128)(2,1)} %upstream_ref.1) | copy-start | bytes 1572868
  57.2 4.5 %copy-start.3 = (bf16[2,128,128]{2,1,0:T(8,128)(2,1)S(1)}, bf16[2,128,128]{2,1,0:T(8,128)(2,1)}, u32[]{:S(2)}) copy-start(bf16[2,128,128]{2,1,0:T(8,128)(2,1)} %inward_ref.1) | copy-start | bytes 196612
  57.2 4.5 %copy-start.4 = (s32[2048]{0:T(1024)S(1)}, s32[2048]{0:T(1024)}, u32[]{:S(2)}) copy-start(s32[2048]{0:T(1024)} %param.10) | copy-start | bytes 24580
  57.2 4.5 %copy-start.5 = (f32[2,6,128]{2,0,1:T(2,128)S(1)}, f32[2,6,128]{2,0,1:T(2,128)}, u32[]{:S(2)}) copy-start(f32[2,6,128]{2,0,1:T(2,128)} %param.14) | copy-start | bytes 18436
  57.2 10.4 %copy-start.6 = (bf16[2,128,128]{2,1,0:T(8,128)(2,1)S(1)}, bf16[2,128,128]{2,1,0:T(8,128)(2,1)}, u32[]{:S(2)}) copy-start(bf16[2,128,128]{2,1,0:T(8,128)(2,1)} %outward_ref.1) | copy-start | bytes 196612
  57.3 7.9 %collective-permute-start.3 = (bf16[256,256]{1,0:T(8,128)(2,1)S(1)}, bf16[256,256]{1,0:T(8,128)(2,1)S(1)}, u32[]{:S(2)}, u32[]{:S(2)}) collective-permute-start(bf16[256,256]{1,0:T(8,128)(2,1)S(1)} %get-tuple-element.39), channel_id=1, source_target_pairs={{0,128},{64,192},{128,0},{192,64},{1,129},{65,193},{129,1},{193,65... | collective-permute-start | bytes 393224 | tf_op jit(solution)/shard_map/ppermute | solution.py:532
  58.7 6.6 %collective-permute-start.4 = (bf16[256,256]{1,0:T(8,128)(2,1)S(1)}, bf16[256,256]{1,0:T(8,128)(2,1)S(1)}, u32[]{:S(2)}, u32[]{:S(2)}) collective-permute-start(bf16[256,256]{1,0:T(8,128)(2,1)S(1)} %get-tuple-element.40), channel_id=1, source_target_pairs={{0,64},{64,128},{128,192},{192,0},{1,65},{65,129},{129,193},{193,1... | collective-permute-start | bytes 393224 | tf_op jit(solution)/shard_map/ppermute | solution.py:532
  60.8 6.8 %collective-permute-start.5 = (bf16[256,256]{1,0:T(8,128)(2,1)S(1)}, bf16[256,256]{1,0:T(8,128)(2,1)S(1)}, u32[]{:S(2)}, u32[]{:S(2)}) collective-permute-start(bf16[256,256]{1,0:T(8,128)(2,1)S(1)} %get-tuple-element.41), channel_id=1, source_target_pairs={{0,192},{64,0},{128,64},{192,128},{1,193},{65,1},{129,65},{193,129... | collective-permute-start | bytes 393224 | tf_op jit(solution)/shard_map/ppermute | solution.py:532
  68.7 7.9 %collective-permute-start.6 = (bf16[256,256]{1,0:T(8,128)(2,1)S(1)}, bf16[256,256]{1,0:T(8,128)(2,1)S(1)}, u32[]{:S(2)}, u32[]{:S(2)}) collective-permute-start(bf16[256,256]{1,0:T(8,128)(2,1)S(1)} %get-tuple-element.47.v0), channel_id=1, source_target_pairs={{0,128},{64,192},{128,0},{192,64},{1,129},{65,193},{129,1},{193,65... | collective-permute-start | bytes 393224 | tf_op jit(solution)/shard_map/ppermute | solution.py:532
  70.1 6.5 %collective-permute-start.7 = (bf16[256,256]{1,0:T(8,128)(2,1)S(1)}, bf16[256,256]{1,0:T(8,128)(2,1)S(1)}, u32[]{:S(2)}, u32[]{:S(2)}) collective-permute-start(bf16[256,256]{1,0:T(8,128)(2,1)S(1)} %get-tuple-element.47.v0), channel_id=1, source_target_pairs={{0,64},{64,128},{128,192},{192,0},{1,65},{65,129},{129,193},{193,1... | collective-permute-start | bytes 393224 | tf_op jit(solution)/shard_map/ppermute | solution.py:532
  71.3 7.0 %collective-permute-start.8 = (bf16[256,256]{1,0:T(8,128)(2,1)S(1)}, bf16[256,256]{1,0:T(8,128)(2,1)S(1)}, u32[]{:S(2)}, u32[]{:S(2)}) collective-permute-start(bf16[256,256]{1,0:T(8,128)(2,1)S(1)} %get-tuple-element.47.v0), channel_id=1, source_target_pairs={{0,192},{64,0},{128,64},{192,128},{1,193},{65,1},{129,65},{193,129... | collective-permute-start | bytes 393224 | tf_op jit(solution)/shard_map/ppermute | solution.py:532
  79.3 20.8 %copy-start = (bf16[256,1024]{1,0:T(8,128)(2,1)}, bf16[256,1024]{1,0:T(8,128)(2,1)S(1)}, u32[]{:S(2)}) copy-start(bf16[256,1024]{1,0:T(8,128)(2,1)S(1)} %get-tuple-element.48.values_ref.second_hbm) | copy-start | bytes 1572868
  79.3 1.7 %collective-permute-start.9 = (bf16[32,40,128]{2,1,0:T(8,128)(2,1)S(1)}, bf16[32,40,128]{2,1,0:T(8,128)(2,1)S(1)}, u32[]{:S(2)}, u32[]{:S(2)}) collective-permute-start(bf16[32,40,128]{2,1,0:T(8,128)(2,1)S(1)} %get-tuple-element.49), channel_id=1, source_target_pairs={{0,1},{1,0},{2,3},{3,2},{4,5},{5,4},{6,7},{7,6},{8,9},{9,8},{10,11... | collective-permute-start | bytes 983048 | tf_op jit(solution)/shard_map/ppermute | solution.py:540
  118.0 2.3 %collective-permute-start.10 = (bf16[32,40,128]{2,1,0:T(8,128)(2,1)S(1)}, bf16[32,40,128]{2,1,0:T(8,128)(2,1)S(1)}, u32[]{:S(2)}, u32[]{:S(2)}) collective-permute-start(bf16[32,40,128]{2,1,0:T(8,128)(2,1)S(1)} %all_to_all.23.mine_ref), channel_id=1, source_target_pairs={{0,1},{1,0},{2,3},{3,2},{4,5},{5,4},{6,7},{7,6},{8,9},{9,8},{10,11... | collective-permute-start | bytes 983048 | tf_op jit(solution)/shard_map/ppermute | solution.py:540
  122.2 6.4 %collective-permute-start.11 = (bf16[144,256]{1,0:T(8,128)(2,1)S(1)}, bf16[144,256]{1,0:T(8,128)(2,1)S(1)}, u32[]{:S(2)}, u32[]{:S(2)}) collective-permute-start(bf16[144,256]{1,0:T(8,128)(2,1)S(1)} %get-tuple-element.57), channel_id=1, source_target_pairs={{0,128},{64,192},{128,0},{192,64},{1,129},{65,193},{129,1},{193,65... | collective-permute-start | bytes 221192 | tf_op jit(solution)/shard_map/ppermute | solution.py:532
  123.8 4.8 %collective-permute-start.12 = (bf16[144,256]{1,0:T(8,128)(2,1)S(1)}, bf16[144,256]{1,0:T(8,128)(2,1)S(1)}, u32[]{:S(2)}, u32[]{:S(2)}) collective-permute-start(bf16[144,256]{1,0:T(8,128)(2,1)S(1)} %get-tuple-element.58), channel_id=1, source_target_pairs={{0,64},{64,128},{128,192},{192,0},{1,65},{65,129},{129,193},{193,1... | collective-permute-start | bytes 221192 | tf_op jit(solution)/shard_map/ppermute | solution.py:532
  125.0 5.6 %collective-permute-start.13 = (bf16[144,256]{1,0:T(8,128)(2,1)S(1)}, bf16[144,256]{1,0:T(8,128)(2,1)S(1)}, u32[]{:S(2)}, u32[]{:S(2)}) collective-permute-start(bf16[144,256]{1,0:T(8,128)(2,1)S(1)} %get-tuple-element.59), channel_id=1, source_target_pairs={{0,192},{64,0},{128,64},{192,128},{1,193},{65,1},{129,65},{193,129... | collective-permute-start | bytes 221192 | tf_op jit(solution)/shard_map/ppermute | solution.py:532

commit v9 on v8

--- a/solution.py
+++ b/solution.py
@@ -257,11 +257,9 @@
     mine_ref,
     table_ref,
     weights_ref,
-    fields_hbm,
+    fields_ref,
     potential_ref,
     total_ref,
-    fields_ref,
-    leaves,
 ):
     digits = mine_ref[COUNT_PIECE].astype(F32)
     counts = sum(digits[row : row + 8] * COUNT_BASE**power for power, row in enumerate(COUNT_ROWS))
@@ -277,11 +275,8 @@
             )
     weigh_pieces(mine_ref, weights_ref, 0, total_ref)
     write_fields(total_ref, fields_ref)
-    leaving = pltpu.make_async_copy(fields_ref, fields_hbm, leaves)
-    leaving.start()
     flipped = jnp.transpose(total_ref[...]).astype(BF16)
     potential_ref[...] = matmul(flipped, table_ref[half_rows(place[2]), :], 1, 0)
-    leaving.wait()
 
 
 def potential_kernel(
@@ -295,9 +290,14 @@
         target[...] = (before_ref[:, slot(index)] + rest).astype(BF16)
 
 
-def own_potential_kernel(place, table_ref, before_ref, flipped_ref, p0):
+def own_potential_kernel(
+    place, table_ref, before_ref, flipped_ref, fields_ref, p0, fields_hbm, leaves
+):
+    leaving = pltpu.make_async_copy(fields_ref, fields_hbm, leaves)
+    leaving.start()
     rest = matmul(flipped_ref[...], table_ref[half_rows(1 - place[2]), slot(0)], 1, 0)
     p0[...] = (before_ref[:, slot(0)] + rest).astype(BF16)
+    leaving.wait()
 
 
 def own_atoms_kernel(
@@ -639,13 +639,12 @@
         functools.partial(first_potential_kernel, prefactor),
         [
             shape_of((2, SLAB, CHANNELS), F32),
-            pltpu.HBM(half, BF16),
+            shape_of(half, BF16),
             shape_of((BLOCK, atoms_here), F32),
         ],
-        [pltpu.VMEM(half, F32), pltpu.VMEM(half, BF16), pltpu.SemaphoreType.DMA],
+        [pltpu.VMEM(half, F32)],
         place,
         [mine, near(table)],
-        out_spaces=[pltpu.VMEM, pltpu.HBM, pltpu.VMEM],
     )
     fields_other, flipped, p2, p1, p3 = call_whole(
         potential_kernel,
@@ -654,12 +653,13 @@
         place,
         [weights, other, near(table), before],
     )
-    (p0,) = call_whole(
+    p0, fields_mine = call_whole(
         own_potential_kernel,
-        [values_shape],
-        [],
-        place,
-        [near(table), before, flipped],
+        [values_shape, pltpu.HBM(half, BF16)],
+        [pltpu.SemaphoreType.DMA],
+        place,
+        [near(table), before, flipped, near(fields_mine)],
+        out_spaces=[pltpu.VMEM, pltpu.HBM],
         micros=0.1,
     )
     own_atoms = pl.BlockSpec((BLOCK, CHANNELS), lambda step, place: (2 * place[0] + place[1], 0))

time: 132 us -> 132 us (level)
  transfers between devices with their start and end apart: 14 -> 14, of which waited for: 9 -> 10; matrix products, arithmetic and copies ran while one was open for 0% -> 0% of each run, Pallas kernels for 7% -> 7%
where the time goes in v9:
time: 132 us; the launch traced here: 131 us
  blocking collectives  82.9 us (63%)
  Pallas kernels  21 us (16%)
  waiting for transfers between devices  14.6 us (11%)
  starting transfers between devices  11.6 us (9%)
    all_to_all x2, blocking collectives, sum_fields(): parts = lax.all_to_all(part, ATOM_REST, 0, 0, tiled=True)  48.4 us
    all_to_all x2, blocking collectives, sum_fields(): mine = lax.all_to_all(spread, ATOM_REST, 0, 0, tiled=True)  34.5 us
    pallas_call x13, Pallas kernels, call_whole(): pl.pallas_call(kernel, in_specs=[pl.BlockSpec(memory_space=pltpu.SMEM)] +...  19.9 us
    ppermute x9, waiting for transfers between devices, shifted(): lax.ppermute(value, 'x', [(i, (i + shift) % SLABS) for i in range(SLABS)])  14 us
    ppermute x9, starting transfers between devices, shifted(): lax.ppermute(value, 'x', [(i, (i + shift) % SLABS) for i in range(SLABS)])  10.7 us
  transfers between devices with their start and end apart: 14, of which 10 were waited for; matrix products, arithmetic and copies ran while one was open for 0% of the time, Pallas kernels for 7%

profile of v9, /device:TPU:6, one launch (start us, length us, event | category | flops | bytes accessed | tf_op | source)
XLA Modules:
  0.0 131.4 jit_solution(12995412533000541774)
XLA Ops:
  0.7 4.7 %shard_map.95 = (bf16[1536,1024]{1,0:T(8,128)(2,1)S(1)}, bf16[32,40,128]{2,1,0:T(8,128)(2,1)S(1)}, bf16[32,40,128]{2,1,0:T(8,128)(2,1)S(1)}) custom-call(s32[3]{0:T(128)S(1)} %pad_add_fusion.place, f32[3,2048]{1,0:T(4,128)} %coordinates_hbm.1, s32[1,2048]{1,0:T(1,128)} %bitcast.9, bf16[4,2,256,128]{3,2,1,0:T(8,128)(2,1)} %bitcast.7, ...), custom_call_target="tpu_custom_call" | custom-call | flops 7000000000 | bytes 7000000 | tf_op jit(solution)/shard_map/pallas_call | solution.py:517
  7.2 30.0 %all_to_all.20 = bf16[32,40,128]{2,1,0:T(8,128)(2,1)S(1)} all-to-all(bf16[32,40,128]{2,1,0:T(8,128)(2,1)S(1)} %add_convert_fusion.1), channel_id=1, replica_groups=mesh['x'=4,'yh'=2,'yl'=2,'z'=8,'core'=2] {'yh','yl','z'}, dimensions={0} | all-to-all | bytes 655360 | tf_op jit(solution)/shard_map/all_to_all | solution.py:551
  37.4 16.6 %all_to_all.21.mine_ref = bf16[32,40,128]{2,1,0:T(8,128)(2,1)S(1)} all-to-all(bf16[32,40,128]{2,1,0:T(8,128)(2,1)S(1)} %broadcast_in_dim.10), channel_id=1, replica_groups=mesh['x'=4,'yh'=2,'yl'=2,'z'=8,'core'=2] {'yh','yl','z'}, dimensions={0} | all-to-all | bytes 655360 | tf_op jit(solution)/shard_map/all_to_all | solution.py:559
  54.0 1.6 %shard_map.97 = (f32[2,640,128]{2,1,0:T(8,128)S(1)}, bf16[640,256]{1,0:T(8,128)(2,1)S(1)}, f32[256,1024]{1,0:T(8,128)S(1)}) custom-call(s32[3]{0:T(128)S(1)} %pad_add_fusion.place, bf16[32,40,128]{2,1,0:T(8,128)(2,1)S(1)} %all_to_all.21.mine_ref, bf16[1536,1024]{1,0:T(8,128)(2,1)S(1)} %get-tuple-element.34.table_ref), custom_call_target="tpu_custom_call" | custom-call | flops 2000000000 | bytes 2000000 | tf_op jit(solution)/shard_map/pallas_call | solution.py:517
  56.8 1.5 %collective-permute-start.3 = (bf16[256,256]{1,0:T(8,128)(2,1)S(1)}, bf16[256,256]{1,0:T(8,128)(2,1)S(1)}, u32[]{:S(2)}, u32[]{:S(2)}) collective-permute-start(bf16[256,256]{1,0:T(8,128)(2,1)S(1)} %get-tuple-element.43), channel_id=1, source_target_pairs={{0,128},{64,192},{128,0},{192,64},{1,129},{65,193},{129,1},{193,65... | collective-permute-start | bytes 393224 | tf_op jit(solution)/shard_map/ppermute | solution.py:532
  58.3 2.1 %collective-permute-start.4 = (bf16[256,256]{1,0:T(8,128)(2,1)S(1)}, bf16[256,256]{1,0:T(8,128)(2,1)S(1)}, u32[]{:S(2)}, u32[]{:S(2)}) collective-permute-start(bf16[256,256]{1,0:T(8,128)(2,1)S(1)} %get-tuple-element.44), channel_id=1, source_target_pairs={{0,64},{64,128},{128,192},{192,0},{1,65},{65,129},{129,193},{193,1... | collective-permute-start | bytes 393224 | tf_op jit(solution)/shard_map/ppermute | solution.py:532
  60.4 1.3 shard_map.99
  61.7 1.1 shard_map.100
  62.9 1.8 %collective-permute-done.3.q1 = bf16[256,256]{1,0:T(8,128)(2,1)S(1)} collective-permute-done((bf16[256,256]{1,0:T(8,128)(2,1)S(1)}, bf16[256,256]{1,0:T(8,128)(2,1)S(1)}, u32[]{:S(2)}, u32[]{:S(2)}) %collective-permute-start.3) | collective-permute-done | bytes 131104 | tf_op jit(solution)/shard_map/ppermute | solution.py:532
  64.8 2.3 %collective-permute-done.5.q3 = bf16[256,256]{1,0:T(8,128)(2,1)S(1)} collective-permute-done((bf16[256,256]{1,0:T(8,128)(2,1)S(1)}, bf16[256,256]{1,0:T(8,128)(2,1)S(1)}, u32[]{:S(2)}, u32[]{:S(2)}) %collective-permute-start.5) | collective-permute-done | bytes 131104 | tf_op jit(solution)/shard_map/ppermute | solution.py:532
  68.2 1.4 %collective-permute-start.6 = (bf16[256,256]{1,0:T(8,128)(2,1)S(1)}, bf16[256,256]{1,0:T(8,128)(2,1)S(1)}, u32[]{:S(2)}, u32[]{:S(2)}) collective-permute-start(bf16[256,256]{1,0:T(8,128)(2,1)S(1)} %get-tuple-element.51.v0), channel_id=1, source_target_pairs={{0,128},{64,192},{128,0},{192,64},{1,129},{65,193},{129,1},{193,65... | collective-permute-start | bytes 393224 | tf_op jit(solution)/shard_map/ppermute | solution.py:532
  69.6 1.2 collective-permute-start.7
  71.6 4.4 %collective-permute-done.6.v1 = bf16[256,256]{1,0:T(8,128)(2,1)S(1)} collective-permute-done((bf16[256,256]{1,0:T(8,128)(2,1)S(1)}, bf16[256,256]{1,0:T(8,128)(2,1)S(1)}, u32[]{:S(2)}, u32[]{:S(2)}) %collective-permute-start.6) | collective-permute-done | bytes 131104 | tf_op jit(solution)/shard_map/ppermute | solution.py:532
  76.1 1.6 %collective-permute-done.8.v3 = bf16[256,256]{1,0:T(8,128)(2,1)S(1)} collective-permute-done((bf16[256,256]{1,0:T(8,128)(2,1)S(1)}, bf16[256,256]{1,0:T(8,128)(2,1)S(1)}, u32[]{:S(2)}, u32[]{:S(2)}) %collective-permute-start.8) | collective-permute-done | bytes 131104 | tf_op jit(solution)/shard_map/ppermute | solution.py:532
  80.6 18.3 %all_to_all.22.parts_ref = bf16[32,40,128]{2,1,0:T(8,128)(2,1)S(1)} all-to-all(bf16[32,40,128]{2,1,0:T(8,128)(2,1)S(1)} %add_convert_fusion), channel_id=1, replica_groups=mesh['x'=4,'yh'=2,'yl'=2,'z'=8,'core'=2] {'yh','yl','z'}, dimensions={0} | all-to-all | bytes 655360 | tf_op jit(solution)/shard_map/all_to_all | solution.py:551
  99.6 17.9 %all_to_all.23.mine_ref = bf16[32,40,128]{2,1,0:T(8,128)(2,1)S(1)} all-to-all(bf16[32,40,128]{2,1,0:T(8,128)(2,1)S(1)} %shard_map.104), channel_id=1, replica_groups=mesh['x'=4,'yh'=2,'yl'=2,'z'=8,'core'=2] {'yh','yl','z'}, dimensions={0} | all-to-all | bytes 655360 | tf_op jit(solution)/shard_map/all_to_all | solution.py:559
  117.5 2.3 %shard_map.105 = (bf16[512,1024]{1,0:T(8,128)(2,1)S(1)}, f32[640,1024]{1,0:T(8,128)S(1)}, f32[128,1024]{1,0:T(8,128)S(1)}) custom-call(s32[3]{0:T(128)S(1)} %pad_add_fusion.place, f32[2,640,128]{2,1,0:T(8,128)S(1)} %get-tuple-element.37.weights_ref, bf16[32,40,128]{2,1,0:T(8,128)(2,1)S(1)} %all_to_all.23.mine_ref, ...), custom_call_target="tpu_custom_call" | custom-call | flops 2000000000 | bytes 2000000 | tf_op jit(solution)/shard_map/pallas_call | solution.py:517
  119.8 1.9 %shard_map.106 = (bf16[640,512]{1,0:T(8,128)(2,1)S(1)}, bf16[128,640]{1,0:T(8,128)(2,1)S(1)}, bf16[144,256]{1,0:T(8,128)(2,1)S(1)}, bf16[144,256]{1,0:T(8,128)(2,1)S(1)}, bf16[144,256]{1,0:T(8,128)(2,1)S(1)}) custom-call(s32[3]{0:T(128)S(1)} %pad_add_fusion.place, f32[2,640,128]{2,1,0:T(8,128)S(1)} %get-tuple-element.37.weights_ref, ...), custom_call_target="tpu_custom_call" | custom-call | flops 2000000000 | bytes 2000000 | tf_op jit(solution)/shard_map/pallas_call | solution.py:517
  121.6 1.6 %collective-permute-start.11 = (bf16[144,256]{1,0:T(8,128)(2,1)S(1)}, bf16[144,256]{1,0:T(8,128)(2,1)S(1)}, u32[]{:S(2)}, u32[]{:S(2)}) collective-permute-start(bf16[144,256]{1,0:T(8,128)(2,1)S(1)} %get-tuple-element.61), channel_id=1, source_target_pairs={{0,128},{64,192},{128,0},{192,64},{1,129},{65,193},{129,1},{193,65... | collective-permute-start | bytes 221192 | tf_op jit(solution)/shard_map/ppermute | solution.py:532
  123.3 1.2 collective-permute-start.12
  125.3 1.1 shard_map.107.q0
  126.4 1.6 %collective-permute-done.11.q1 = bf16[144,256]{1,0:T(8,128)(2,1)S(1)} collective-permute-done((bf16[144,256]{1,0:T(8,128)(2,1)S(1)}, bf16[144,256]{1,0:T(8,128)(2,1)S(1)}, u32[]{:S(2)}, u32[]{:S(2)}) %collective-permute-start.11) | collective-permute-done | bytes 73760 | tf_op jit(solution)/shard_map/ppermute | solution.py:532
  128.0 2.0 %collective-permute-done.13.q3 = bf16[144,256]{1,0:T(8,128)(2,1)S(1)} collective-permute-done((bf16[144,256]{1,0:T(8,128)(2,1)S(1)}, bf16[144,256]{1,0:T(8,128)(2,1)S(1)}, u32[]{:S(2)}, u32[]{:S(2)}) %collective-permute-start.13) | collective-permute-done | bytes 73760 | tf_op jit(solution)/shard_map/ppermute | solution.py:532
  130.0 1.4 %shard_map.108 = (bf16[256,128]{1,0:T(8,128)(2,1)}, f32[3,256]{1,0:T(4,128)}) custom-call(s32[3]{0:T(128)S(1)} %pad_add_fusion.place, bf16[144,256]{1,0:T(8,128)(2,1)S(1)} %shard_map.107.q0, bf16[144,256]{1,0:T(8,128)(2,1)S(1)} %collective-permute-done.11.q1, bf16[144,256]{1,0:T(8,128)(2,1)S(1)} %collective-permute-done.12.q2, ...), custom_call_target="tpu_custom_call" | custom-call | flops 2000000000 | bytes 2000000 | tf_op jit(solution)/shard_map/pallas_call | solution.py:517
  (43 shorter events, 9.6 us)
Async XLA Ops:
  0.7 4.8 %copy-start.7 = (s32[3,512]{1,0:T(4,128)S(1)}, s32[3,512]{1,0:T(4,128)}, u32[]{:S(2)}) copy-start(s32[3,512]{1,0:T(4,128)} %param.11) | copy-start | bytes 18436
  5.4 1.7 %collective-permute-start = (bf16[32,40,128]{2,1,0:T(8,128)(2,1)S(1)}, bf16[32,40,128]{2,1,0:T(8,128)(2,1)S(1)}, u32[]{:S(2)}, u32[]{:S(2)}) collective-permute-start(bf16[32,40,128]{2,1,0:T(8,128)(2,1)S(1)} %get-tuple-element.36), channel_id=1, source_target_pairs={{0,1},{1,0},{2,3},{3,2},{4,5},{5,4},{6,7},{7,6},{8,9},{9,8},{10,11... | collective-permute-start | bytes 983048 | tf_op jit(solution)/shard_map/ppermute | solution.py:540
  5.5 0.7 collective-permute-start.1
  54.0 1.6 %collective-permute-start.2 = (bf16[32,40,128]{2,1,0:T(8,128)(2,1)S(1)}, bf16[32,40,128]{2,1,0:T(8,128)(2,1)S(1)}, u32[]{:S(2)}, u32[]{:S(2)}) collective-permute-start(bf16[32,40,128]{2,1,0:T(8,128)(2,1)S(1)} %all_to_all.21.mine_ref), channel_id=1, source_target_pairs={{0,1},{1,0},{2,3},{3,2},{4,5},{5,4},{6,7},{7,6},{8,9},{9,8},{10,11... | collective-permute-start | bytes 983048 | tf_op jit(solution)/shard_map/ppermute | solution.py:540
  56.7 4.9 %copy-start.1 = (bf16[2048,128]{1,0:T(8,128)(2,1)S(1)}, bf16[2048,128]{1,0:T(8,128)(2,1)}, u32[]{:S(2)}) copy-start(bf16[2048,128]{1,0:T(8,128)(2,1)} %features_ref.1) | copy-start | bytes 1572868
  56.7 4.9 %copy-start.2 = (bf16[2048,128]{1,0:T(8,128)(2,1)S(1)}, bf16[2048,128]{1,0:T(8,128)(2,1)}, u32[]{:S(2)}) copy-start(bf16[2048,128]{1,0:T(8,128)(2,1)} %upstream_ref.1) | copy-start | bytes 1572868
  56.7 4.9 %copy-start.3 = (bf16[2,128,128]{2,1,0:T(8,128)(2,1)S(1)}, bf16[2,128,128]{2,1,0:T(8,128)(2,1)}, u32[]{:S(2)}) copy-start(bf16[2,128,128]{2,1,0:T(8,128)(2,1)} %inward_ref.1) | copy-start | bytes 196612
  56.8 4.9 %copy-start.4 = (s32[2048]{0:T(1024)S(1)}, s32[2048]{0:T(1024)}, u32[]{:S(2)}) copy-start(s32[2048]{0:T(1024)} %param.10) | copy-start | bytes 24580
  56.8 4.9 %copy-start.5 = (f32[2,6,128]{2,0,1:T(2,128)S(1)}, f32[2,6,128]{2,0,1:T(2,128)}, u32[]{:S(2)}) copy-start(f32[2,6,128]{2,0,1:T(2,128)} %param.14) | copy-start | bytes 18436
  56.8 10.4 %copy-start.6 = (bf16[2,128,128]{2,1,0:T(8,128)(2,1)S(1)}, bf16[2,128,128]{2,1,0:T(8,128)(2,1)}, u32[]{:S(2)}) copy-start(bf16[2,128,128]{2,1,0:T(8,128)(2,1)} %outward_ref.1) | copy-start | bytes 196612
  56.8 7.9 %collective-permute-start.3 = (bf16[256,256]{1,0:T(8,128)(2,1)S(1)}, bf16[256,256]{1,0:T(8,128)(2,1)S(1)}, u32[]{:S(2)}, u32[]{:S(2)}) collective-permute-start(bf16[256,256]{1,0:T(8,128)(2,1)S(1)} %get-tuple-element.43), channel_id=1, source_target_pairs={{0,128},{64,192},{128,0},{192,64},{1,129},{65,193},{129,1},{193,65... | collective-permute-start | bytes 393224 | tf_op jit(solution)/shard_map/ppermute | solution.py:532
  58.3 6.6 %collective-permute-start.4 = (bf16[256,256]{1,0:T(8,128)(2,1)S(1)}, bf16[256,256]{1,0:T(8,128)(2,1)S(1)}, u32[]{:S(2)}, u32[]{:S(2)}) collective-permute-start(bf16[256,256]{1,0:T(8,128)(2,1)S(1)} %get-tuple-element.44), channel_id=1, source_target_pairs={{0,64},{64,128},{128,192},{192,0},{1,65},{65,129},{129,193},{193,1... | collective-permute-start | bytes 393224 | tf_op jit(solution)/shard_map/ppermute | solution.py:532
  60.4 6.8 %collective-permute-start.5 = (bf16[256,256]{1,0:T(8,128)(2,1)S(1)}, bf16[256,256]{1,0:T(8,128)(2,1)S(1)}, u32[]{:S(2)}, u32[]{:S(2)}) collective-permute-start(bf16[256,256]{1,0:T(8,128)(2,1)S(1)} %get-tuple-element.45), channel_id=1, source_target_pairs={{0,192},{64,0},{128,64},{192,128},{1,193},{65,1},{129,65},{193,129... | collective-permute-start | bytes 393224 | tf_op jit(solution)/shard_map/ppermute | solution.py:532
  68.2 7.9 %collective-permute-start.6 = (bf16[256,256]{1,0:T(8,128)(2,1)S(1)}, bf16[256,256]{1,0:T(8,128)(2,1)S(1)}, u32[]{:S(2)}, u32[]{:S(2)}) collective-permute-start(bf16[256,256]{1,0:T(8,128)(2,1)S(1)} %get-tuple-element.51.v0), channel_id=1, source_target_pairs={{0,128},{64,192},{128,0},{192,64},{1,129},{65,193},{129,1},{193,65... | collective-permute-start | bytes 393224 | tf_op jit(solution)/shard_map/ppermute | solution.py:532
  69.6 6.5 %collective-permute-start.7 = (bf16[256,256]{1,0:T(8,128)(2,1)S(1)}, bf16[256,256]{1,0:T(8,128)(2,1)S(1)}, u32[]{:S(2)}, u32[]{:S(2)}) collective-permute-start(bf16[256,256]{1,0:T(8,128)(2,1)S(1)} %get-tuple-element.51.v0), channel_id=1, source_target_pairs={{0,64},{64,128},{128,192},{192,0},{1,65},{65,129},{129,193},{193,1... | collective-permute-start | bytes 393224 | tf_op jit(solution)/shard_map/ppermute | solution.py:532
  70.8 7.0 %collective-permute-start.8 = (bf16[256,256]{1,0:T(8,128)(2,1)S(1)}, bf16[256,256]{1,0:T(8,128)(2,1)S(1)}, u32[]{:S(2)}, u32[]{:S(2)}) collective-permute-start(bf16[256,256]{1,0:T(8,128)(2,1)S(1)} %get-tuple-element.51.v0), channel_id=1, source_target_pairs={{0,192},{64,0},{128,64},{192,128},{1,193},{65,1},{129,65},{193,129... | collective-permute-start | bytes 393224 | tf_op jit(solution)/shard_map/ppermute | solution.py:532
  78.8 20.8 %copy-start = (bf16[256,1024]{1,0:T(8,128)(2,1)}, bf16[256,1024]{1,0:T(8,128)(2,1)S(1)}, u32[]{:S(2)}) copy-start(bf16[256,1024]{1,0:T(8,128)(2,1)S(1)} %get-tuple-element.52.values_ref.second_hbm) | copy-start | bytes 1572868
  78.8 1.7 %collective-permute-start.9 = (bf16[32,40,128]{2,1,0:T(8,128)(2,1)S(1)}, bf16[32,40,128]{2,1,0:T(8,128)(2,1)S(1)}, u32[]{:S(2)}, u32[]{:S(2)}) collective-permute-start(bf16[32,40,128]{2,1,0:T(8,128)(2,1)S(1)} %get-tuple-element.53), channel_id=1, source_target_pairs={{0,1},{1,0},{2,3},{3,2},{4,5},{5,4},{6,7},{7,6},{8,9},{9,8},{10,11... | collective-permute-start | bytes 983048 | tf_op jit(solution)/shard_map/ppermute | solution.py:540
  117.5 2.3 %collective-permute-start.10 = (bf16[32,40,128]{2,1,0:T(8,128)(2,1)S(1)}, bf16[32,40,128]{2,1,0:T(8,128)(2,1)S(1)}, u32[]{:S(2)}, u32[]{:S(2)}) collective-permute-start(bf16[32,40,128]{2,1,0:T(8,128)(2,1)S(1)} %all_to_all.23.mine_ref), channel_id=1, source_target_pairs={{0,1},{1,0},{2,3},{3,2},{4,5},{5,4},{6,7},{7,6},{8,9},{9,8},{10,11... | collective-permute-start | bytes 983048 | tf_op jit(solution)/shard_map/ppermute | solution.py:540
  121.6 6.4 %collective-permute-start.11 = (bf16[144,256]{1,0:T(8,128)(2,1)S(1)}, bf16[144,256]{1,0:T(8,128)(2,1)S(1)}, u32[]{:S(2)}, u32[]{:S(2)}) collective-permute-start(bf16[144,256]{1,0:T(8,128)(2,1)S(1)} %get-tuple-element.61), channel_id=1, source_target_pairs={{0,128},{64,192},{128,0},{192,64},{1,129},{65,193},{129,1},{193,65... | collective-permute-start | bytes 221192 | tf_op jit(solution)/shard_map/ppermute | solution.py:532
  123.3 4.7 %collective-permute-start.12 = (bf16[144,256]{1,0:T(8,128)(2,1)S(1)}, bf16[144,256]{1,0:T(8,128)(2,1)S(1)}, u32[]{:S(2)}, u32[]{:S(2)}) collective-permute-start(bf16[144,256]{1,0:T(8,128)(2,1)S(1)} %get-tuple-element.62), channel_id=1, source_target_pairs={{0,64},{64,128},{128,192},{192,0},{1,65},{65,129},{129,193},{193,1... | collective-permute-start | bytes 221192 | tf_op jit(solution)/shard_map/ppermute | solution.py:532
  124.5 5.6 %collective-permute-start.13 = (bf16[144,256]{1,0:T(8,128)(2,1)S(1)}, bf16[144,256]{1,0:T(8,128)(2,1)S(1)}, u32[]{:S(2)}, u32[]{:S(2)}) collective-permute-start(bf16[144,256]{1,0:T(8,128)(2,1)S(1)} %get-tuple-element.63), channel_id=1, source_target_pairs={{0,192},{64,0},{128,64},{192,128},{1,193},{65,1},{129,65},{193,129... | collective-permute-start | bytes 221192 | tf_op jit(solution)/shard_map/ppermute | solution.py:532
